TPU v7x, 32 devices: a whole 2x2x4 slice. The times are simulated.
32 devices in a mesh: dp: 16 (over z, x, core), mesh: 2 (over y).
Axes of the slice: x: 2, y: 2, z: 4, core: 2. Of those that a mesh axis runs over, the one named last changes fastest.
Arguments:
- node_feats: bfloat16 [16, 128, 512], P('dp', 'mesh'), may hold values from -6 to 6
- edge_feats: bfloat16 [16, 128, 8, 512], P('dp', 'mesh'), may hold values from -6 to 6
- node_cot: bfloat16 [16, 128, 512], P('dp', 'mesh'), may hold values from -6 to 6
- edge_cot: bfloat16 [16, 128, 8, 512], P('dp', 'mesh'), may hold values from -6 to 6
- w_edge_in: bfloat16 [2, 1536, 512], replicated, may hold values from -0.15625 to 0.15625
- w_edge_out: bfloat16 [2, 512, 512], replicated, may hold values from -0.25 to 0.25
- w_node_in: bfloat16 [2, 1024, 512], replicated, may hold values from -0.1875 to 0.1875
- w_node_out: bfloat16 [2, 512, 512], replicated, may hold values from -0.25 to 0.25
- neighbours: int32 [128, 8], P('mesh'), may hold values from 0 to 95
- send_rows: int32 [2, 32], P('mesh'), may hold values from 0 to 63, as said below
- edge_counts: int32 [128], P('mesh'), may hold values from 1 to 8
- ocean_mask: int32 [128], P('mesh'), may hold values 0 or 1
Outputs:
- grad_nodes: float32 [16, 128, 512], P('dp', 'mesh')
- grad_edges: bfloat16 [16, 128, 8, 512], P('dp', 'mesh')
- grad_edge_in: float32 [2, 1536, 512], P(None, 'dp')
- grad_edge_out: float32 [2, 512, 512], P(None, 'dp')
- grad_node_in: float32 [2, 1024, 512], P(None, 'dp')
- grad_node_out: float32 [2, 512, 512], P(None, 'dp')
Inputs may be any that keep to these rules, and one draw needn't show every extreme that they name: `send_rows`: within each partition's row the (32) entries are distinct local rows.
All inputs are finite; a program needn't handle non-finite values. No bound on the sum of `ocean_mask` on one device may be relied on, other than what follows from the above.
Results may differ from a plain program's by a relative error of at most 0.03.
Values may be sent and summed in bfloat16 or wider, within the bound.
No kernel may reach another device: no remote copies, remote signals or barrier semaphores. Data moves between devices by JAX's collectives and lax.ppermute only.
A program may use at most 128 MiB of HBM per device.

v0:
```python
import jax
import jax.numpy as jnp
from jax import lax
from jax.sharding import PartitionSpec as P


def with_halo(shard, sides, width):
    for axis, dim in sides:
        devices, length = (lax.axis_size(axis), shard.shape[dim])
        up = [(i, (i + 1) % devices) for i in range(devices)]
        down = [(j, i) for i, j in up]
        last = lax.slice_in_dim(shard, length - width, length, axis=dim)
        initial = lax.slice_in_dim(shard, 0, width, axis=dim)
        before = lax.ppermute(last, axis, up)
        after = lax.ppermute(initial, axis, down)
        shard = jnp.concatenate([before, shard, after], axis=dim)
    return shard


def normalize(values):
    center = jnp.mean(values, axis=-1, keepdims=True)
    shifted = values - center
    inverse = lax.rsqrt(jnp.mean(shifted * shifted, axis=-1, keepdims=True) + 1e-05)
    return shifted * inverse


def normalize_back(values, upstream):
    center = jnp.mean(values, axis=-1, keepdims=True)
    shifted = values - center
    inverse = lax.rsqrt(jnp.mean(shifted * shifted, axis=-1, keepdims=True) + 1e-05)
    normed = shifted * inverse
    return inverse * (
        upstream
        - jnp.mean(upstream, axis=-1, keepdims=True)
        - normed * jnp.mean(upstream * normed, axis=-1, keepdims=True)
    )


def silu_slope(values):
    sigmoid_val = jax.nn.sigmoid(values)
    return sigmoid_val * (1.0 + values * (1.0 - sigmoid_val))


def forward(nodes, edges, sources, active_slots, wet_ocean_rows, weights):
    edge_in, edge_out, node_in, node_out = weights
    count, slot_count, features = edges.shape
    edge_input = jnp.concatenate(
        [edges, sources, jnp.broadcast_to(nodes[:, None, :], edges.shape)], axis=-1
    ).reshape(count * slot_count, 3 * features)
    pre_edge = jnp.dot(edge_input, edge_in, preferred_element_type=jnp.float32)
    act_edge = jax.nn.silu(pre_edge).astype(jnp.bfloat16)
    pre_edge_out = jnp.dot(act_edge, edge_out, preferred_element_type=jnp.float32)
    update = normalize(pre_edge_out).reshape(count, slot_count, features)
    new_edges = (edges.astype(jnp.float32) + active_slots[:, :, None] * update).astype(jnp.bfloat16)
    message = jnp.sum(active_slots[:, :, None] * new_edges.astype(jnp.float32), axis=1).astype(
        jnp.bfloat16
    )
    node_input = jnp.concatenate([nodes, message], axis=-1)
    pre_node = jnp.dot(node_input, node_in, preferred_element_type=jnp.float32)
    act_node = jax.nn.silu(pre_node).astype(jnp.bfloat16)
    pre_node_out = jnp.dot(act_node, node_out, preferred_element_type=jnp.float32)
    new_nodes = (
        nodes.astype(jnp.float32) + wet_ocean_rows[:, None] * normalize(pre_node_out)
    ).astype(jnp.bfloat16)
    return (
        new_nodes,
        new_edges,
        (
            edge_input,
            pre_edge,
            act_edge,
            pre_edge_out,
            node_input,
            pre_node,
            act_node,
            pre_node_out,
        ),
    )


def reverse_sweep(saved_activation, grad_nodes, grad_edges, active_slots, wet_ocean_rows, weights):
    edge_in, edge_out, node_in, node_out = weights
    edge_input, pre_edge, act_edge, pre_edge_out, node_input, pre_node, act_node, pre_node_out = (
        saved_activation
    )
    count, slot_count, features = grad_edges.shape
    grad_out = normalize_back(pre_node_out, wet_ocean_rows[:, None] * grad_nodes).astype(
        jnp.bfloat16
    )
    grad_node_out = jnp.dot(act_node.T, grad_out, preferred_element_type=jnp.float32)
    grad_act = jnp.dot(grad_out, node_out.T, preferred_element_type=jnp.float32)
    grad_pre = (grad_act * silu_slope(pre_node)).astype(jnp.bfloat16)
    grad_node_in = jnp.dot(node_input.T, grad_pre, preferred_element_type=jnp.float32)
    grad_input = jnp.dot(grad_pre, node_in.T, preferred_element_type=jnp.float32)
    grad_nodes = grad_nodes + grad_input[:, :features]
    grad_edges = grad_edges + active_slots[:, :, None] * grad_input[:, None, features:]
    upstream = (active_slots[:, :, None] * grad_edges).reshape(count * slot_count, features)
    grad_edge_pre_out = normalize_back(pre_edge_out, upstream).astype(jnp.bfloat16)
    grad_edge_out = jnp.dot(act_edge.T, grad_edge_pre_out, preferred_element_type=jnp.float32)
    grad_edge_act = jnp.dot(grad_edge_pre_out, edge_out.T, preferred_element_type=jnp.float32)
    grad_edge_pre = (grad_edge_act * silu_slope(pre_edge)).astype(jnp.bfloat16)
    grad_edge_in = jnp.dot(edge_input.T, grad_edge_pre, preferred_element_type=jnp.float32)
    grad_edge_input = jnp.dot(grad_edge_pre, edge_in.T, preferred_element_type=jnp.float32)
    grad_edge_input = grad_edge_input.reshape(count, slot_count, 3 * features)
    grad_edges = grad_edges + grad_edge_input[:, :, :features]
    source_gradient = grad_edge_input[:, :, features : 2 * features]
    grad_nodes = grad_nodes + jnp.sum(grad_edge_input[:, :, 2 * features :], axis=1)
    return (
        grad_nodes,
        grad_edges,
        source_gradient,
        (grad_edge_in, grad_edge_out, grad_node_in, grad_node_out),
    )


def reduce_grads(layer_gradients, factor, features):
    pieces = (
        lax.psum_scatter(
            layer_gradients[0].reshape(-1), ("dp", "mesh"), scatter_dimension=0, tiled=True
        ),
        lax.psum_scatter(
            layer_gradients[1].reshape(-1), ("dp", "mesh"), scatter_dimension=0, tiled=True
        ),
        lax.psum_scatter(
            layer_gradients[2].reshape(-1), ("dp", "mesh"), scatter_dimension=0, tiled=True
        ),
        lax.psum_scatter(
            layer_gradients[3].reshape(-1), ("dp", "mesh"), scatter_dimension=0, tiled=True
        ),
    )
    joined = (
        lax.all_gather(pieces[0], "mesh", axis=0, tiled=True),
        lax.all_gather(pieces[1], "mesh", axis=0, tiled=True),
        lax.all_gather(pieces[2], "mesh", axis=0, tiled=True),
        lax.all_gather(pieces[3], "mesh", axis=0, tiled=True),
    )
    totals = tuple((piece.reshape(-1, features) for piece in joined))
    return tuple((total * factor for total in totals))


def body(
    node_feats,
    edge_feats,
    node_cot,
    edge_cot,
    w_edge_in,
    w_edge_out,
    w_node_in,
    w_node_out,
    neighbours,
    send_rows,
    edge_counts,
    ocean_mask,
):
    samples, local_nodes, features = node_feats.shape
    slot_count = neighbours.shape[1]
    halo_rows = send_rows.shape[1] // 2
    layer_count = w_edge_in.shape[0]
    send_list = send_rows[0]
    flat_sources = neighbours.reshape(-1)
    live_one = (jnp.arange(slot_count, dtype=jnp.int32)[None, :] < edge_counts[:, None]).astype(
        jnp.float32
    )
    active_slots = jnp.tile(live_one, (samples, 1))
    wet_ocean_rows = jnp.tile(ocean_mask.astype(jnp.float32), (samples,))
    total_rows = samples * lax.axis_size("dp") * local_nodes * lax.axis_size("mesh")
    factor = 1.0 / total_rows**0.5
    weight_per_layer = [
        (
            w_edge_in[layer_index],
            w_edge_out[layer_index],
            w_node_in[layer_index],
            w_node_out[layer_index],
        )
        for layer_index in range(layer_count)
    ]
    nodes = node_feats.reshape(samples * local_nodes, features)
    edges = edge_feats.reshape(samples * local_nodes, slot_count, features)
    saved_activations = []
    for layer_index in range(layer_count):
        field = nodes.reshape(samples, local_nodes, features)
        packed = field[:, send_list, :]
        beside_all = with_halo(packed, (("mesh", 1),), halo_rows)
        extend_row_table = jnp.concatenate(
            [field, beside_all[:, :halo_rows], beside_all[:, 3 * halo_rows :]], axis=1
        )
        sources = extend_row_table[:, flat_sources, :].reshape(
            samples * local_nodes, slot_count, features
        )
        nodes, edges, saved_activation = forward(
            nodes, edges, sources, active_slots, wet_ocean_rows, weight_per_layer[layer_index]
        )
        saved_activations.append(saved_activation)
    node_gradient = node_cot.reshape(samples * local_nodes, features).astype(jnp.float32)
    edge_gradient = edge_cot.reshape(samples * local_nodes, slot_count, features).astype(
        jnp.float32
    )
    reduced = [None] * layer_count
    for layer_index in reversed(range(layer_count)):
        node_gradient, edge_gradient, source_gradient, layer_gradients = reverse_sweep(
            saved_activations[layer_index],
            node_gradient,
            edge_gradient,
            active_slots,
            wet_ocean_rows,
            weight_per_layer[layer_index],
        )
        row_table = jnp.zeros((samples, local_nodes + 2 * halo_rows, features), jnp.float32)
        row_table = row_table.at[:, flat_sources].add(
            source_gradient.reshape(samples, local_nodes * slot_count, features)
        )
        outgoing = row_table[:, local_nodes:]
        returned = with_halo(outgoing.astype(jnp.bfloat16), (("mesh", 1),), halo_rows).astype(
            outgoing.dtype
        )
        arriving = jnp.concatenate([returned[:, :halo_rows], returned[:, 3 * halo_rows :]], axis=1)
        owned = row_table[:, :local_nodes].at[:, send_list].add(arriving)
        node_gradient = node_gradient + owned.reshape(samples * local_nodes, features)
        reduced[layer_index] = reduce_grads(layer_gradients, factor, features)
    stacked = [
        jnp.stack([reduced[layer_index][kind] for layer_index in range(layer_count)])
        for kind in range(4)
    ]
    return (
        node_gradient.reshape(samples, local_nodes, features),
        edge_gradient.astype(jnp.bfloat16).reshape(samples, local_nodes, slot_count, features),
        stacked[0],
        stacked[1],
        stacked[2],
        stacked[3],
    )


def solution(mesh):
    placed = (
        P("dp", "mesh", None),
        P("dp", "mesh", None, None),
        P("dp", "mesh", None),
        P("dp", "mesh", None, None),
        P(),
        P(),
        P(),
        P(),
        P("mesh", None),
        P("mesh", None),
        P("mesh"),
        P("mesh"),
    )
    return jax.shard_map(
        body,
        mesh=mesh,
        in_specs=placed,
        out_specs=(
            P("dp", "mesh", None),
            P("dp", "mesh", None, None),
            P(None, "dp", None),
            P(None, "dp", None),
            P(None, "dp", None),
            P(None, "dp", None),
        ),
        check_vma=False,
    )
```

profile of v0, /device:TPU:0, one launch (start us, length us, event | category | flops | bytes accessed | tf_op | source)
XLA Modules:
  0.0 410.6 jit_solution(1458921759849190390)
XLA Ops:
  9.6 3.0 collective-permute-start.1
  17.7 2.6 gather_fusion.1
  20.3 2.4 fusion.6
  33.4 2.6 gather_fusion.3
  36.0 2.8 fusion.4
  47.3 2.2 fusion.12
  51.0 2.7 convolution_bitcast_fusion
  56.6 4.5 %scatter_custom_fusion = f32[96,512]{1,0:T(8,128)S(1)} fusion(s32[512]{0:T(512)} %bitcast.232, f32[64,8,1536]{2,1,0:T(8,128)} %copy-done, f32[]{:T(128)} %constant.41.clone.1), kind=kCustom, calls=%fused_computation.58 | custom fusion | flops 262144 | bytes 1245696 | tf_op jit(solution)/shard_map/scatter-add | solution.py:209
  65.3 4.4 %copy.21 = f32[192,4,8,128]{3,1,2,0:T(4,128)} copy(f32[192,4,8,128]{3,2,1,0:T(8,128)} %convolution_bitcast_fusion) | data formatting | bytes 6291456
  74.2 2.4 scatter_custom_fusion.1
  83.5 2.1 fusion.13
  88.8 2.5 copy.20
  95.7 4.1 fusion
  99.8 4.4 %scatter_custom_fusion.2 = f32[96,512]{1,0:T(8,128)S(1)} fusion(s32[512]{0:T(512)} %bitcast.233, f32[64,8,1536]{2,1,0:T(8,128)} %fusion, f32[]{:T(128)} %constant.41.clone.1), kind=kCustom, calls=%fused_computation.55 | custom fusion | flops 262144 | bytes 1245696 | tf_op jit(solution)/shard_map/scatter-add | solution.py:209
  106.3 2.6 fusion.51
  110.7 244.5 %all-reduce.11.cloned.1.call-done = (f32[786432]{0:T(1024)}, f32[786432]{0:T(1024)}, f32[262144]{0:T(1024)}, f32[262144]{0:T(1024)}, f32[524288]{0:T(1024)}, /*i...) async-done(((f32[786432]{0:T(1024)}, f32[786432]{0:T(1024)}, f32[262144]{0:T(1024)}, f32[262144]{0:T(1024)}, f32[524288]{0:T(1024)}, /*index=5*/f32[524288]{0:T(1024)}, ...) | async-done | bytes 14680080
  356.1 5.3 %all_gather.25 = f32[49152]{0:T(1024)S(1)} all-gather(f32[24576]{0:T(1024)S(1)} %dynamic-slice.1), channel_id=1, replica_groups=mesh['dp'=16,'mesh'=2] {'mesh'}, dimensions={0}, use_global_device_ids=true | all-gather | bytes 294912 | tf_op jit(solution)/shard_map/all_gather | solution.py:132
  362.4 5.3 %all_gather.24 = f32[49152]{0:T(1024)S(1)} all-gather(f32[24576]{0:T(1024)S(1)} %dynamic-slice), channel_id=1, replica_groups=mesh['dp'=16,'mesh'=2] {'mesh'}, dimensions={0}, use_global_device_ids=true | all-gather | bytes 294912 | tf_op jit(solution)/shard_map/all_gather | solution.py:132
  368.5 4.7 %all_gather.27 = f32[16384]{0:T(1024)S(1)} all-gather(f32[8192]{0:T(1024)S(1)} %dynamic-slice.3), channel_id=1, replica_groups=mesh['dp'=16,'mesh'=2] {'mesh'}, dimensions={0}, use_global_device_ids=true | all-gather | bytes 98304 | tf_op jit(solution)/shard_map/all_gather | solution.py:133
  373.9 4.6 %all_gather.26 = f32[16384]{0:T(1024)S(1)} all-gather(f32[8192]{0:T(1024)S(1)} %dynamic-slice.2), channel_id=1, replica_groups=mesh['dp'=16,'mesh'=2] {'mesh'}, dimensions={0}, use_global_device_ids=true | all-gather | bytes 98304 | tf_op jit(solution)/shard_map/all_gather | solution.py:133
  379.4 4.9 %all_gather.29 = f32[32768]{0:T(1024)S(1)} all-gather(f32[16384]{0:T(1024)S(1)} %dynamic-slice.5), channel_id=1, replica_groups=mesh['dp'=16,'mesh'=2] {'mesh'}, dimensions={0}, use_global_device_ids=true | all-gather | bytes 196608 | tf_op jit(solution)/shard_map/all_gather | solution.py:134
  385.2 4.9 %all_gather.28 = f32[32768]{0:T(1024)S(1)} all-gather(f32[16384]{0:T(1024)S(1)} %dynamic-slice.4), channel_id=1, replica_groups=mesh['dp'=16,'mesh'=2] {'mesh'}, dimensions={0}, use_global_device_ids=true | all-gather | bytes 196608 | tf_op jit(solution)/shard_map/all_gather | solution.py:134
  390.9 4.6 %all_gather.31 = f32[16384]{0:T(1024)S(1)} all-gather(f32[8192]{0:T(1024)S(1)} %dynamic-slice.7), channel_id=1, replica_groups=mesh['dp'=16,'mesh'=2] {'mesh'}, dimensions={0}, use_global_device_ids=true | all-gather | bytes 98304 | tf_op jit(solution)/shard_map/all_gather | solution.py:135
  396.3 4.6 %all_gather.30 = f32[16384]{0:T(1024)S(1)} all-gather(f32[8192]{0:T(1024)S(1)} %dynamic-slice.6), channel_id=1, replica_groups=mesh['dp'=16,'mesh'=2] {'mesh'}, dimensions={0}, use_global_device_ids=true | all-gather | bytes 98304 | tf_op jit(solution)/shard_map/all_gather | solution.py:135
  (239 shorter events, 66.9 us)
Async XLA Ops:
  7.2 13.1 %copy-start.3 = (bf16[2,1536,512]{2,1,0:T(8,128)(2,1)S(1)}, bf16[2,1536,512]{2,1,0:T(8,128)(2,1)}, u32[]{:S(2)}) copy-start(bf16[2,1536,512]{2,1,0:T(8,128)(2,1)} %param.16) | copy-start | bytes 9437188
  7.2 348.0 %all-reduce.11.cloned.1.call-start = ((), (), s32[]{:S(2)}) async-start(), calls=%async_computation | async-start | bytes 29360128
  8.0 7.3 %copy-start.43 = (s32[32]{0:T(128)}, s32[32]{0:T(128)S(1)}, u32[]{:S(2)}) copy-start(s32[32]{0:T(128)S(1)} %fusion.97) | copy-start | bytes 388
  9.6 7.2 %collective-permute-start.1 = (bf16[1,16,512]{2,1,0:T(8,128)(2,1)S(1)}, bf16[1,16,512]{2,1,0:T(8,128)(2,1)S(1)}, u32[]{:S(2)}, u32[]{:S(2)}) collective-permute-start(bf16[1,16,512]{2,1,0:T(8,128)(2,1)S(1)} %get-tuple-element.36), channel_id=1, source_target_pairs={{1,0},{0,1},{3,2},{2,3},{5,4},{4,5},{7,6},{6,7},{9,8},{8,9},{11,10... | collective-permute-start | bytes 49160 | tf_op jit(solution)/shard_map/ppermute | solution.py:15
  12.7 4.2 %collective-permute-start = (bf16[1,16,512]{2,1,0:T(8,128)(2,1)S(1)}, bf16[1,16,512]{2,1,0:T(8,128)(2,1)S(1)}, u32[]{:S(2)}, u32[]{:S(2)}) collective-permute-start(bf16[1,16,512]{2,1,0:T(8,128)(2,1)S(1)} %get-tuple-element.35), channel_id=1, source_target_pairs={{0,1},{1,0},{2,3},{3,2},{4,5},{5,4},{6,7},{7,6},{8,9},{9,8},{10,11... | collective-permute-start | bytes 49160 | tf_op jit(solution)/shard_map/ppermute | solution.py:14
  16.7 25.2 %copy-start.28 = (f32[64]{0:T(128)}, f32[64]{0:T(128)S(1)}, u32[]{:S(2)}) copy-start(f32[64]{0:T(128)S(1)} %convert_element_type.140) | copy-start | bytes 772
  20.3 3.4 copy-start.46
  25.3 4.3 %copy-start.19 = (bf16[64,512]{1,0:T(8,128)(2,1)}, bf16[64,512]{1,0:T(8,128)(2,1)S(1)}, u32[]{:S(2)}) copy-start(bf16[64,512]{1,0:T(8,128)(2,1)S(1)} %get-tuple-element.21) | copy-start | bytes 196612
  26.5 9.5 %copy-start.30 = (f32[64]{0:T(128)}, f32[64]{0:T(128)S(1)}, u32[]{:S(2)}) copy-start(f32[64]{0:T(128)S(1)} %broadcast_multiply_fusion.19) | copy-start | bytes 772
  26.9 9.2 %copy-start.35 = (f32[64]{0:T(128)}, f32[64]{0:T(128)S(1)}, u32[]{:S(2)}) copy-start(f32[64]{0:T(128)S(1)} %add_rsqrt_fusion.3) | copy-start | bytes 772
  27.6 4.0 collective-permute-start.3
  29.6 3.7 collective-permute-start.2
  30.0 6.0 %copy-start.13 = (bf16[512,512]{1,0:T(8,128)(2,1)}, bf16[512,512]{1,0:T(8,128)(2,1)S(1)}, u32[]{:S(2)}) copy-start(bf16[512,512]{1,0:T(8,128)(2,1)S(1)} %add_convert_fusion) | copy-start | bytes 1572868
  39.8 3.5 copy-start.27
  51.0 4.7 %copy-start = (f32[64,8,1536]{2,1,0:T(8,128)}, f32[64,8,1536]{2,1,0:T(8,128)S(1)}, u32[]{:S(2)}) copy-start(f32[64,8,1536]{2,1,0:T(8,128)S(1)} %fusion.2) | copy-start | bytes 9437188
  61.2 8.5 %copy-start.18 = (bf16[1,96,512]{2,1,0:T(8,128)(2,1)}, bf16[1,96,512]{2,1,0:T(8,128)(2,1)S(1)}, u32[]{:S(2)}) copy-start(bf16[1,96,512]{2,1,0:T(8,128)(2,1)S(1)} %bitcast_convert_fusion.1) | copy-start | bytes 294916
  61.9 12.3 %collective-permute-start.5 = (bf16[1,16,512]{2,1,0:T(8,128)(2,1)S(1)}, bf16[1,16,512]{2,1,0:T(8,128)(2,1)S(1)}, u32[]{:S(2)}, u32[]{:S(2)}) collective-permute-start(bf16[1,16,512]{2,1,0:T(8,128)(2,1)S(1)} %get-tuple-element.28), channel_id=1, source_target_pairs={{1,0},{0,1},{3,2},{2,3},{5,4},{4,5},{7,6},{6,7},{9,8},{8,9},{11,10... | collective-permute-start | bytes 49160 | tf_op jit(solution)/shard_map/ppermute | solution.py:15
  62.1 12.1 %collective-permute-start.4 = (bf16[1,16,512]{2,1,0:T(8,128)(2,1)S(1)}, bf16[1,16,512]{2,1,0:T(8,128)(2,1)S(1)}, u32[]{:S(2)}, u32[]{:S(2)}) collective-permute-start(bf16[1,16,512]{2,1,0:T(8,128)(2,1)S(1)} %get-tuple-element.27), channel_id=1, source_target_pairs={{0,1},{1,0},{2,3},{3,2},{4,5},{5,4},{6,7},{7,6},{8,9},{9,8},{10,11... | collective-permute-start | bytes 49160 | tf_op jit(solution)/shard_map/ppermute | solution.py:14
  65.3 4.4 %copy-start.9 = (f32[64,4,8,128]{3,2,1,0:T(8,128)S(1)}, f32[64,4,8,128]{3,2,1,0:T(8,128)}, u32[]{:S(2)}) copy-start(f32[64,4,8,128]{3,2,1,0:T(8,128)} %convolution_bitcast_fusion.6) | copy-start | bytes 3145732
  71.0 5.6 %copy-start.11 = (bf16[1,64,512]{2,1,0:T(8,128)(2,1)S(1)}, bf16[1,64,512]{2,1,0:T(8,128)(2,1)}, u32[]{:S(2)}) copy-start(bf16[1,64,512]{2,1,0:T(8,128)(2,1)} %param.14) | copy-start | bytes 196612
  71.0 5.6 %copy-start.31 = (f32[64]{0:T(128)S(1)}, f32[64]{0:T(128)}, u32[]{:S(2)}) copy-start(f32[64]{0:T(128)} %copy-done.30) | copy-start | bytes 772
  71.0 5.6 %copy-start.36 = (f32[64]{0:T(128)S(1)}, f32[64]{0:T(128)}, u32[]{:S(2)}) copy-start(f32[64]{0:T(128)} %copy-done.35) | copy-start | bytes 772
  104.2 4.8 %collective-permute-start.7 = (bf16[1,16,512]{2,1,0:T(8,128)(2,1)S(1)}, bf16[1,16,512]{2,1,0:T(8,128)(2,1)S(1)}, u32[]{:S(2)}, u32[]{:S(2)}) collective-permute-start(bf16[1,16,512]{2,1,0:T(8,128)(2,1)S(1)} %get-tuple-element.26), channel_id=1, source_target_pairs={{1,0},{0,1},{3,2},{2,3},{5,4},{4,5},{7,6},{6,7},{9,8},{8,9},{11,10... | collective-permute-start | bytes 49160 | tf_op jit(solution)/shard_map/ppermute | solution.py:15
  104.4 4.5 %collective-permute-start.6 = (bf16[1,16,512]{2,1,0:T(8,128)(2,1)S(1)}, bf16[1,16,512]{2,1,0:T(8,128)(2,1)S(1)}, u32[]{:S(2)}, u32[]{:S(2)}) collective-permute-start(bf16[1,16,512]{2,1,0:T(8,128)(2,1)S(1)} %get-tuple-element.25), channel_id=1, source_target_pairs={{0,1},{1,0},{2,3},{3,2},{4,5},{5,4},{6,7},{7,6},{8,9},{9,8},{10,11... | collective-permute-start | bytes 49160 | tf_op jit(solution)/shard_map/ppermute | solution.py:14
  (38 other events, 59.4 us)
Sparse Core Ops, SparseCore 0:
  95.8 259.3 all-reduce.10
where the time goes:
time: 412 us; the launch traced here: 411 us
  waiting for transfers between devices  247 us (60%)
  local copies, waits for them, and re-layouts  39.7 us (10%)
  blocking collectives  38.8 us (9%)
  other arithmetic  31.9 us (8%)
  matrix products  28.8 us (7%)
  between operations  15 us (4%)
  starting transfers between devices  9.37 us (2%)
    unnamed x2, waiting for transfers between devices  245 us
    unnamed x121, local copies, waits for them, and re-layouts  27.6 us
    all_gather x2, blocking collectives, reduce_grads(): lax.all_gather(pieces[0], 'mesh', axis=0, tiled=True)  10.6 us
    all_gather x2, blocking collectives, reduce_grads(): lax.all_gather(pieces[2], 'mesh', axis=0, tiled=True)  9.86 us
    all_gather x2, blocking collectives, reduce_grads(): lax.all_gather(pieces[1], 'mesh', axis=0, tiled=True)  9.23 us
    all_gather x2, blocking collectives, reduce_grads(): lax.all_gather(pieces[3], 'mesh', axis=0, tiled=True)  9.16 us
    scatter-add x2, other arithmetic, body(): row_table.at[:, flat_sources]  8.91 us
  transfers between devices with their start and end apart: 9, of which 3 were waited for; matrix products, arithmetic and copies ran while one was open for 7% of the time, Pallas kernels for 0%

commit v1 on v0

v1 whole, which is shorter than its diff:
```python
import functools

import jax
import jax.numpy as jnp
from jax import lax
from jax.experimental import pallas as pl
from jax.experimental.pallas import tpu as pltpu
from jax.sharding import PartitionSpec as P

F32 = jnp.float32
BF16 = jnp.bfloat16
VMEM = pltpu.VMEM
EPS = 1e-05


def params():
    return pltpu.CompilerParams(vmem_limit_bytes=48 * 1024 * 1024)


def whole(shape):
    return pl.BlockSpec(shape, lambda i: (0,) * len(shape))


def layer_of(array, layer):
    return pl.BlockSpec((1,) + array.shape[1:], lambda i: (layer, 0, 0))


def call(kernel, operands, specs, outs, scratch=(), flops=0):
    shapes = tuple(jax.ShapeDtypeStruct(shape, dtype) for shape, dtype in outs)
    moved = sum(a.size * a.dtype.itemsize for a in operands)
    moved += sum(s.size * s.dtype.itemsize for s in shapes)
    return pl.pallas_call(
        kernel,
        grid=(1,),
        in_specs=[whole(a.shape) if s is None else s for a, s in zip(operands, specs)],
        out_specs=tuple(whole(s.shape) for s in shapes),
        out_shape=shapes,
        scratch_shapes=list(scratch),
        compiler_params=params(),
        cost_estimate=pl.CostEstimate(flops=flops, bytes_accessed=moved, transcendentals=0),
    )(*operands)


def dot(a, b):
    return jnp.dot(a, b, preferred_element_type=F32)


def dot_nt(a, b):
    return lax.dot_general(a, b, (((1,), (1,)), ((), ())), preferred_element_type=F32)


def dot_tn(a, b):
    return lax.dot_general(a, b, (((0,), (0,)), ((), ())), preferred_element_type=F32)


def silu_and_slope(values):
    sigmoid = 0.5 * jnp.tanh(0.5 * values) + 0.5
    act = values * sigmoid
    return act, sigmoid + act * (1.0 - sigmoid)


def norm_parts(values):
    center = jnp.mean(values, axis=-1, keepdims=True)
    shifted = values - center
    inverse = lax.rsqrt(jnp.mean(shifted * shifted, axis=-1, keepdims=True) + EPS)
    return shifted * inverse, inverse


def norm_back(normed, inverse, upstream):
    return inverse * (
        upstream
        - jnp.mean(upstream, axis=-1, keepdims=True)
        - normed * jnp.mean(upstream * normed, axis=-1, keepdims=True)
    )


def halves(values):
    high = values.astype(BF16)
    low = (values - high.astype(F32)).astype(BF16)
    return jnp.concatenate([high, low], axis=0)


def node_of_edge(rows, nodes, slots):
    edge = lax.broadcasted_iota(jnp.int32, (rows, nodes), 0)
    node = lax.broadcasted_iota(jnp.int32, (rows, nodes), 1)
    return (edge // slots) == node


def pack_kernel(send_ref, h_ref, packed_ref):
    nodes, sent = h_ref.shape[0], send_ref.shape[1]
    row = lax.broadcasted_iota(jnp.int32, (nodes, sent), 0)
    pick = (row == send_ref[...]).astype(F32).astype(BF16)
    packed_ref[...] = dot_tn(pick, h_ref[...]).astype(BF16)


def prepare_kernel(slots, table, nb_ref, count_ref, spread_ref, mask_ref, live_ref):
    nodes = nb_ref.shape[0]
    rows = nodes * slots
    owner = node_of_edge(rows, nodes, slots).astype(F32)
    owner16 = owner.astype(BF16)
    listed = dot(owner16, nb_ref[...].astype(F32).astype(BF16))
    counts = dot(owner16, count_ref[...].astype(F32).astype(BF16))
    slot_here = lax.broadcasted_iota(jnp.int32, (rows, slots), 0) % slots
    slot_at = lax.broadcasted_iota(jnp.int32, (rows, slots), 1)
    source = jnp.sum(jnp.where(slot_here == slot_at, listed, 0.0), axis=1, keepdims=True)
    live = jnp.where(slot_here[:, :1].astype(F32) < counts, 1.0, 0.0)
    at = lax.broadcasted_iota(jnp.int32, (rows, table), 1).astype(F32)
    spread_ref[:, :table] = jnp.where(at == source, 1.0, 0.0).astype(BF16)
    spread_ref[:, table:] = owner16
    mask_ref[...] = (owner * live).astype(BF16)
    live_ref[...] = live


def forward_edges(chunk, e_ref, h, table, spread_ref, live_ref, wi_ref, wo_ref, put):
    rows, width = e_ref.shape
    known = table.shape[0]
    for start in range(0, rows, chunk):
        at = pl.ds(start, chunk)
        spread = spread_ref[at, :]
        src = dot(spread[:, :known], table).astype(BF16)
        own = dot(spread[:, known:], h).astype(BF16)
        e = e_ref[at, :]
        pre = dot(e, wi_ref[0, :width, :])
        pre += dot(src, wi_ref[0, width : 2 * width, :])
        pre += dot(own, wi_ref[0, 2 * width :, :])
        act, slope = silu_and_slope(pre)
        act = act.astype(BF16)
        normed, inverse = norm_parts(dot(act, wo_ref[0]))
        new_e = (e.astype(F32) + live_ref[at, :] * normed).astype(BF16)
        put(at, act, slope, normed, inverse, new_e)


def forward_nodes(h, message, wi_ref, wo_ref):
    width = h.shape[1]
    pre = dot(h, wi_ref[0, :width, :]) + dot(message, wi_ref[0, width:, :])
    act, slope = silu_and_slope(pre)
    act = act.astype(BF16)
    normed, inverse = norm_parts(dot(act, wo_ref[0]))
    return act, slope, normed, inverse


def first_forward_kernel(
    chunk, e_ref, h_ref, halo_ref, spread_ref, mask_ref, live_ref, ocean_ref, send_ref,
    wei_ref, weo_ref, wni_ref, wno_ref,
    act_ref, slope_ref, normed_ref, inverse_ref, new_e_ref,
    new_h_ref, message_ref, act_n_ref, slope_n_ref, normed_n_ref, inverse_n_ref, packed_ref,
):
    h = h_ref[...]
    table = jnp.concatenate([h, halo_ref[...]], axis=0)

    def put(at, act, slope, normed, inverse, new_e):
        act_ref[at, :] = act
        slope_ref[at, :] = slope.astype(BF16)
        normed_ref[at, :] = normed.astype(BF16)
        inverse_ref[at, :] = inverse
        new_e_ref[at, :] = new_e

    forward_edges(chunk, e_ref, h, table, spread_ref, live_ref, wei_ref, weo_ref, put)
    message = dot_tn(mask_ref[...], new_e_ref[...]).astype(BF16)
    act, slope, normed, inverse = forward_nodes(h, message, wni_ref, wno_ref)
    new_h = (h.astype(F32) + ocean_ref[...].astype(F32) * normed).astype(BF16)
    new_h_ref[...] = new_h
    message_ref[...] = message
    act_n_ref[...] = act
    slope_n_ref[...] = slope.astype(BF16)
    normed_n_ref[...] = normed.astype(BF16)
    inverse_n_ref[...] = inverse
    pack_kernel(send_ref, new_h_ref, packed_ref)


def backward_nodes(gh, h, message, act, slope, normed, inverse, ocean_ref, wi_ref, wo_ref):
    up = ocean_ref[...].astype(F32) * gh
    gout = norm_back(normed, inverse, up).astype(BF16)
    grad_out = dot_tn(act, gout)
    gpre = (dot_nt(gout, wo_ref[0]) * slope).astype(BF16)
    grad_in = dot_tn(jnp.concatenate([h, message], axis=1), gpre)
    ginput = dot_nt(gpre, wi_ref[0])
    width = h.shape[1]
    return gh + ginput[:, :width], ginput[:, width:], grad_in, grad_out


def place(blocks, me, sources, keep_ref, send_ref):
    for slot, bits in enumerate(blocks):
        for bit, ref in ((0, keep_ref), (1, send_ref)):
            device = jnp.bitwise_xor(me, bits + bit)
            row = 0
            for source in sources:
                size = source.shape[0] // (2 * len(blocks))
                start = pl.multiple_of(device * size, 16)
                ref[slot, row : row + size, :] = source[pl.ds(start, size), :].astype(BF16)
                row += size


def middle_kernel(
    chunk, blocks, me_ref, e_ref, h_ref, halo_ref, spread_ref, mask_ref, live_ref, ocean_ref,
    gh_ref, wei_ref, weo_ref, wni_ref, wno_ref,
    act_ref, slope_ref, normed_ref, inverse_ref,
    gh_out_ref, gmsg_ref, keep_ref, sent_ref,
    new_e_ref, grad_in_ref, grad_out_ref,
):
    h = h_ref[...]
    table = jnp.concatenate([h, halo_ref[...]], axis=0)

    def put(at, act, slope, normed, inverse, new_e):
        act_ref[at, :] = act
        slope_ref[at, :] = slope.astype(BF16)
        normed_ref[at, :] = normed.astype(BF16)
        inverse_ref[at, :] = inverse
        new_e_ref[at, :] = new_e

    forward_edges(chunk, e_ref, h, table, spread_ref, live_ref, wei_ref, weo_ref, put)
    message = dot_tn(mask_ref[...], new_e_ref[...]).astype(BF16)
    act, slope, normed, inverse = forward_nodes(h, message, wni_ref, wno_ref)
    gh, gmsg, grad_in, grad_out = backward_nodes(
        gh_ref[...].astype(F32), h, message, act, slope, normed, inverse, ocean_ref, wni_ref, wno_ref
    )
    gh_out_ref[...] = gh
    gmsg_ref[...] = gmsg
    grad_in_ref[...] = grad_in
    grad_out_ref[...] = grad_out
    place(blocks, me_ref[0], (grad_in_ref, grad_out_ref), keep_ref, sent_ref)


def return_halo(gh_ref, own_ref, back_ref, send_ref, wei_ref):
    nodes, width = gh_ref.shape
    row = lax.broadcasted_iota(jnp.int32, (nodes, send_ref.shape[1]), 0)
    pick = (row == send_ref[...]).astype(F32).astype(BF16)
    total = own_ref[...] + dot(pick, back_ref[...])
    both = dot_nt(halves(total), wei_ref[0, width : 2 * width, :])
    return gh_ref[...] + both[:nodes] + both[nodes:]


def nodes_back_kernel(
    blocks, me_ref, gh_ref, own_ref, back_ref, send_ref, h_ref, message_ref, act_ref, slope_ref,
    normed_ref, inverse_ref, ocean_ref, wei_ref, wni_ref, wno_ref,
    gh_out_ref, gmsg_ref, keep_ref, sent_ref, grad_in_ref, grad_out_ref,
):
    gh = return_halo(gh_ref, own_ref, back_ref, send_ref, wei_ref)
    gh, gmsg, grad_in, grad_out = backward_nodes(
        gh, h_ref[...], message_ref[...], act_ref[...], slope_ref[...].astype(F32),
        normed_ref[...].astype(F32), inverse_ref[...], ocean_ref, wni_ref, wno_ref,
    )
    gh_out_ref[...] = gh
    gmsg_ref[...] = gmsg
    grad_in_ref[...] = grad_in
    grad_out_ref[...] = grad_out
    place(blocks, me_ref[0], (grad_in_ref, grad_out_ref), keep_ref, sent_ref)


def edges_back_kernel(
    chunk, blocks, me_ref, gh_ref, gmsg_ref, ge_ref, e_ref, h_ref, halo_ref, spread_ref, live_ref,
    act_ref, slope_ref, normed_ref, inverse_ref, wei_ref, weo_ref,
    gh_out_ref, own_ref, halo_out_ref, ge_out_ref, keep_ref, sent_ref,
    gedge_ref, gpe_ref, grad_in_ref, grad_out_ref,
):
    rows, width = e_ref.shape
    nodes = h_ref.shape[0]
    known = nodes + halo_ref.shape[0]
    gmsg = halves(gmsg_ref[...])
    for start in range(0, rows, chunk):
        at = pl.ds(start, chunk)
        live = live_ref[at, :]
        owner = spread_ref[at, known:]
        sent = dot(jnp.concatenate([owner, owner], axis=1), gmsg)
        ge = ge_ref[at, :].astype(F32) + live * sent
        gedge = norm_back(normed_ref[at, :].astype(F32), inverse_ref[at, :], live * ge)
        gedge = gedge.astype(BF16)
        gpe = (dot_nt(gedge, weo_ref[0]) * slope_ref[at, :].astype(F32)).astype(BF16)
        gedge_ref[at, :] = gedge
        gpe_ref[at, :] = gpe
        ge = ge + dot_nt(gpe, wei_ref[0, :width, :])
        ge_out_ref[at, :] = ge.astype(ge_out_ref.dtype)
    gpe = gpe_ref[...]
    gathered = dot_tn(spread_ref[...], gpe)
    source, own = gathered[:known], gathered[known:]
    own_ref[...] = source[:nodes]
    halo_out_ref[...] = source[nodes:].astype(BF16)
    both = dot_nt(halves(own), wei_ref[0, 2 * width :, :])
    gh_out_ref[...] = gh_ref[...] + both[:nodes] + both[nodes:]
    h = h_ref[...]
    table = jnp.concatenate([h, halo_ref[...]], axis=0)
    grad_in_ref[:width, :] = dot_tn(e_ref[...], gpe)
    grad_in_ref[width : 2 * width, :] = dot_tn(table, source.astype(BF16))
    grad_in_ref[2 * width :, :] = dot_tn(h, own.astype(BF16))
    grad_out_ref[...] = dot_tn(act_ref[...], gedge_ref[...])
    place(blocks, me_ref[0], (grad_in_ref, grad_out_ref), keep_ref, sent_ref)


def last_kernel(gh_ref, own_ref, back_ref, send_ref, wei_ref, out_ref):
    out_ref[...] = return_halo(gh_ref, own_ref, back_ref, send_ref, wei_ref)


def trade(rows):
    count = lax.axis_size("mesh")
    half = rows.shape[0] // 2
    if count == 2:
        other = lax.ppermute(rows, "mesh", [(0, 1), (1, 0)])
        return jnp.concatenate([other[half:], other[:half]], axis=0)
    up = [(i, (i + 1) % count) for i in range(count)]
    down = [(j, i) for i, j in up]
    return jnp.concatenate(
        [lax.ppermute(rows[half:], "mesh", up), lax.ppermute(rows[:half], "mesh", down)], axis=0
    )


def flip(values, axis, bit):
    return lax.ppermute(values, axis, [(i, i ^ bit) for i in range(lax.axis_size(axis))])


def bits_of(axis):
    size = lax.axis_size(axis)
    return [1 << i for i in range(size.bit_length() - 1)]


def slot_order(route):
    order = [0]
    for bit in reversed(route):
        order = order + [slot + bit for slot in order]
    return order


def scatter_sum(keep, sent, route):
    held = [keep, flip(sent, "dp", 1)]

    def total(start, stop):
        return sum(part[start:stop].astype(F32) for part in held)

    slots = keep.shape[0]
    for bit in route:
        slots //= 2
        held.append(flip(total(slots, 2 * slots).astype(BF16), "dp", bit))
    value = total(0, 1)[0]
    for bit in bits_of("mesh"):
        mine = value.astype(BF16)
        value = mine.astype(F32) + flip(mine, "mesh", bit).astype(F32)
    return value


def body(
    node_feats,
    edge_feats,
    node_cot,
    edge_cot,
    w_edge_in,
    w_edge_out,
    w_node_in,
    w_node_out,
    neighbours,
    send_rows,
    edge_counts,
    ocean_mask,
):
    samples, nodes, width = node_feats.shape
    slots = neighbours.shape[1]
    rows = nodes * slots
    sent = send_rows.shape[1]
    known = nodes + sent
    chunk = rows // 2
    shards = lax.axis_size("dp")
    route = bits_of("dp")[1:]
    blocks = slot_order(route)
    total_rows = samples * shards * nodes * lax.axis_size("mesh")
    factor = 1.0 / total_rows**0.5
    me = lax.axis_index("dp").astype(jnp.int32).reshape(1)
    scalar = pl.BlockSpec(memory_space=pltpu.SMEM)

    h0 = node_feats.reshape(nodes, width)
    e0 = edge_feats.reshape(rows, width)
    gh = node_cot.reshape(nodes, width)
    ge = edge_cot.reshape(rows, width)
    ocean = ocean_mask.reshape(nodes, 1)
    small, large = (nodes, width), (rows, width)

    (packed0,) = call(pack_kernel, (send_rows, h0), (None,) * 2, [((sent, width), BF16)])
    halo0 = trade(packed0)
    spread, mask, live = call(
        functools.partial(prepare_kernel, slots, known),
        (neighbours, edge_counts.reshape(nodes, 1)),
        (None,) * 2,
        [((rows, known + nodes), BF16), ((rows, nodes), BF16), ((rows, 1), F32)],
    )

    weights = (w_edge_in, w_edge_out, w_node_in, w_node_out)
    specs = [tuple(layer_of(w, layer) for w in weights) for layer in range(2)]
    square = rows * width * width
    (
        act0, slope0, normed0, inverse0, e1,
        h1, message0, act_n0, slope_n0, normed_n0, inverse_n0, packed1,
    ) = call(
        functools.partial(first_forward_kernel, chunk),
        (e0, h0, halo0, spread, mask, live, ocean, send_rows) + weights,
        (None,) * 8 + specs[0],
        [(large, BF16)] * 3 + [((rows, 1), F32), (large, BF16)]
        + [(small, BF16)] * 5 + [((nodes, 1), F32), ((sent, width), BF16)],
        flops=8 * square,
    )
    halo1 = trade(packed1)

    def split(kinds):
        size = sum(w.shape[1] // shards for w in kinds)
        return [((len(blocks), size, width), BF16)] * 2

    node_kinds, edge_kinds = (w_node_in, w_node_out), (w_edge_in, w_edge_out)
    node_scratch = [VMEM(w.shape[1:], F32) for w in node_kinds]
    edge_scratch = [VMEM(large, BF16)] * 2 + [VMEM(w.shape[1:], F32) for w in edge_kinds]

    act1, slope1, normed1, inverse1, gh, gmsg, keep_n1, sent_n1 = call(
        functools.partial(middle_kernel, chunk, blocks),
        (me, e1, h1, halo1, spread, mask, live, ocean, gh) + weights,
        (scalar,) + (None,) * 8 + specs[1],
        [(large, BF16)] * 3 + [((rows, 1), F32)] + [(small, F32)] * 2 + split(node_kinds),
        scratch=[VMEM(large, BF16)] + node_scratch,
        flops=10 * square,
    )
    sum_n1 = scatter_sum(keep_n1, sent_n1, route)

    def edges_back(layer, gh, gmsg, ge, e, h, halo, act, slope, normed, inverse, ge_type):
        return call(
            functools.partial(edges_back_kernel, chunk, blocks),
            (me, gh, gmsg, ge, e, h, halo, spread, live, act, slope, normed, inverse) + weights[:2],
            (scalar,) + (None,) * 12 + specs[layer][:2],
            [(small, F32)] * 2 + [((sent, width), BF16), (large, ge_type)] + split(edge_kinds),
            scratch=edge_scratch,
            flops=12 * square,
        )

    gh, own, halo_out, ge, keep_e1, sent_e1 = edges_back(
        1, gh, gmsg, ge, e1, h1, halo1, act1, slope1, normed1, inverse1, F32
    )
    back = trade(halo_out)
    sum_e1 = scatter_sum(keep_e1, sent_e1, route)

    gh, gmsg, keep_n0, sent_n0 = call(
        functools.partial(nodes_back_kernel, blocks),
        (me, gh, own, back, send_rows, h0, message0, act_n0, slope_n0, normed_n0, inverse_n0, ocean)
        + (w_edge_in, w_node_in, w_node_out),
        (scalar,) + (None,) * 11 + (specs[1][0],) + specs[0][2:],
        [(small, F32)] * 2 + split(node_kinds),
        scratch=node_scratch,
        flops=3 * square,
    )
    sum_n0 = scatter_sum(keep_n0, sent_n0, route)
    gh, own, halo_out, ge, keep_e0, sent_e0 = edges_back(
        0, gh, gmsg, ge, e0, h0, halo0, act0, slope0, normed0, inverse0, BF16
    )
    back = trade(halo_out)
    sum_e0 = scatter_sum(keep_e0, sent_e0, route)
    (gh,) = call(
        last_kernel,
        (gh, own, back, send_rows, w_edge_in),
        (None,) * 4 + (specs[0][0],),
        [(small, F32)],
        flops=square // 4,
    )

    def joined(first, last, start, stop):
        return jnp.stack([first[start:stop], last[start:stop]]) * factor

    cut_e, cut_n = w_edge_in.shape[1] // shards, w_node_in.shape[1] // shards
    return (
        gh.reshape(samples, nodes, width),
        ge.reshape(samples, nodes, slots, width),
        joined(sum_e0, sum_e1, 0, cut_e),
        joined(sum_e0, sum_e1, cut_e, None),
        joined(sum_n0, sum_n1, 0, cut_n),
        joined(sum_n0, sum_n1, cut_n, None),
    )


def solution(mesh):
    placed = (
        P("dp", "mesh", None),
        P("dp", "mesh", None, None),
        P("dp", "mesh", None),
        P("dp", "mesh", None, None),
        P(),
        P(),
        P(),
        P(),
        P("mesh", None),
        P("mesh", None),
        P("mesh"),
        P("mesh"),
    )
    return jax.shard_map(
        body,
        mesh=mesh,
        in_specs=placed,
        out_specs=(
            P("dp", "mesh", None),
            P("dp", "mesh", None, None),
            P(None, "dp", None),
            P(None, "dp", None),
            P(None, "dp", None),
            P(None, "dp", None),
        ),
        check_vma=False,
    )
```

time: 412 us -> 125 us (0.30)
  waiting for transfers between devices: 247 us -> 41.3 us
  blocking collectives: 38.8 us -> 0 us
  matrix products: 28.8 us -> 0 us
  Pallas kernels: 0 us -> 28 us
  local copies, waits for them, and re-layouts: 39.7 us -> 14.6 us
  other arithmetic: 31.9 us -> 8.07 us
  starting transfers between devices: 9.37 us -> 31.3 us
  between operations: 15 us -> 1.08 us
    unnamed x2 -> x0, waiting for transfers between devices: 245 us -> none
    ppermute x8 -> x24, waiting for transfers between devices: 2.41 us -> 41.3 us  [the longest x20 32.9 us: flip(): lax.ppermute(values, axis, [(i, i ^ bit) for i in range(lax.axis_size(axi...]
    all_gather x8 -> x0, blocking collectives: 38.8 us -> none  [the longest x2 10.6 us: reduce_grads(): lax.all_gather(pieces[0], 'mesh', axis=0, tiled=True)]
    dot_general x24 -> x0, matrix products: 28.8 us -> none  [the longest x2 5.2 us: forward(): pre_edge = jnp.dot(edge_input, edge_in, preferred_element_type=jnp.float32)]
    pallas_call x0 -> x8, Pallas kernels: none -> 28 us  [call(): pl.pallas_call(kernel, grid=(1,), in_specs=[whole(a.shape) if s is None e...]
    ppermute x8 -> x24, starting transfers between devices: 9.33 us -> 31.3 us  [the longest x20 25.5 us: flip(): lax.ppermute(values, axis, [(i, i ^ bit) for i in range(lax.axis_size(axi...]
    unnamed x121 -> x59, local copies, waits for them, and re-layouts: 27.6 us -> 12.3 us
    scatter-add x4 -> x0, other arithmetic: 12.3 us -> none  [the longest x2 8.91 us: body(): row_table.at[:, flat_sources]]
  transfers between devices with their start and end apart: 9 -> 24, of which waited for: 3 -> 15; matrix products, arithmetic and copies ran while one was open for 7% -> 7% of each run, Pallas kernels for 0% -> 9%
where the time goes in v1:
time: 125 us; the launch traced here: 124 us
  waiting for transfers between devices  41.3 us (33%)
  starting transfers between devices  31.3 us (25%)
  Pallas kernels  28 us (22%)
  local copies, waits for them, and re-layouts  14.6 us (12%)
  other arithmetic  8.07 us (6%)
    ppermute x20, waiting for transfers between devices, flip(): lax.ppermute(values, axis, [(i, i ^ bit) for i in range(lax.axis_size(axi...  32.9 us
    pallas_call x8, Pallas kernels, call(): pl.pallas_call(kernel, grid=(1,), in_specs=[whole(a.shape) if s is None e...  28 us
    ppermute x20, starting transfers between devices, flip(): lax.ppermute(values, axis, [(i, i ^ bit) for i in range(lax.axis_size(axi...  25.5 us
    unnamed x59, local copies, waits for them, and re-layouts  12.3 us
    ppermute x4, waiting for transfers between devices, trade(): other = lax.ppermute(rows, 'mesh', [(0, 1), (1, 0)])  8.46 us
    ppermute x4, starting transfers between devices, trade(): other = lax.ppermute(rows, 'mesh', [(0, 1), (1, 0)])  5.87 us
    convert_element_type x12, other arithmetic, scatter_sum(): held.append(flip(total(slots, 2 * slots).astype(BF16), 'dp', bit))  3.9 us
    mul x4, other arithmetic, joined(): return jnp.stack([first[start:stop], last[start:stop]]) * factor  2.85 us
  transfers between devices with their start and end apart: 24, of which 15 were waited for; matrix products, arithmetic and copies ran while one was open for 7% of the time, Pallas kernels for 9%

profile of v1, /device:TPU:0, one launch (start us, length us, event | category | flops | bytes accessed | tf_op | source)
XLA Modules:
  0.0 124.5 jit_solution(3138088791238781867)
XLA Ops:
  2.3 3.0 %collective-permute-start = (bf16[32,512]{1,0:T(8,128)(2,1)S(1)}, bf16[32,512]{1,0:T(8,128)(2,1)S(1)}, u32[]{:S(2)}, u32[]{:S(2)}) collective-permute-start(bf16[32,512]{1,0:T(8,128)(2,1)S(1)} %shard_map.163), channel_id=1, source_target_pairs={{0,1},{1,0},{2,3},{3,2},{4,5},{5,4},{6,7},{7,6},{8,9},{9,8},{10,11... | collective-permute-start | bytes 98312 | tf_op jit(solution)/shard_map/ppermute | solution.py:297
  13.2 5.4 %shard_map.165 = (bf16[512,512]{1,0:T(8,128)(2,1)S(1)}, bf16[512,512]{1,0:T(8,128)(2,1)S(1)}, bf16[512,512]{1,0:T(8,128)(2,1)S(1)}, f32[512,1]{1,0:T(8,128)S(1)}...) custom-call(bf16[512,512]{1,0:T(8,128)(2,1)S(1)} %bitcast.33, ...), custom_call_target="tpu_custom_call" | custom-call | flops 1073741824 | bytes 10654336 | tf_op jit(solution)/shard_map/pallas_call | solution.py:32
  23.6 3.3 %collective-permute-done.1 = bf16[32,512]{1,0:T(8,128)(2,1)} collective-permute-done((bf16[32,512]{1,0:T(8,128)(2,1)}, bf16[32,512]{1,0:T(8,128)(2,1)}, u32[]{:S(2)}, u32[]{:S(2)}) %collective-permute-start.1) | collective-permute-done | bytes 32800 | tf_op jit(solution)/shard_map/ppermute | solution.py:297
  27.6 5.9 %shard_map.166 = (bf16[512,512]{1,0:T(8,128)(2,1)S(1)}, bf16[512,512]{1,0:T(8,128)(2,1)S(1)}, bf16[512,512]{1,0:T(8,128)(2,1)S(1)}, f32[512,1]{1,0:T(8,128)S(1)}...) custom-call(s32[1]{0:T(128)} %bitcast.me_ref, ...), custom_call_target="tpu_custom_call" | custom-call | flops 1342177280 | bytes 11669764 | tf_op jit(solution)/shard_map/pallas_call | solution.py:32
  33.6 5.9 %shard_map.167 = (f32[64,512]{1,0:T(8,128)S(1)}, f32[64,512]{1,0:T(8,128)S(1)}, bf16[32,512]{1,0:T(8,128)(2,1)S(1)}, f32[512,512]{1,0:T(8,128)S(1)}, bf16[8,128,...) custom-call(s32[1]{0:T(128)} %bitcast.me_ref, f32[64,512]{1,0:T(8,128)S(1)} %get-tuple-element.51.gh_ref, ...), custom_call_target="tpu_custom_call" | custom-call | flops 1610612736 | bytes 10784772 | tf_op jit(solution)/shard_map/pallas_call | solution.py:32
  42.0 2.4 %collective-permute-done.2 = bf16[32,512]{1,0:T(8,128)(2,1)S(1)} collective-permute-done((bf16[32,512]{1,0:T(8,128)(2,1)S(1)}, bf16[32,512]{1,0:T(8,128)(2,1)S(1)}, u32[]{:S(2)}, u32[]{:S(2)}) %collective-permute-start.2) | collective-permute-done | bytes 32800 | tf_op jit(solution)/shard_map/ppermute | solution.py:297
  44.5 3.1 %shard_map.168 = (f32[64,512]{1,0:T(8,128)S(1)}, f32[64,512]{1,0:T(8,128)S(1)}, bf16[8,96,512]{2,1,0:T(8,128)(2,1)S(1)}, bf16[8,96,512]{2,1,0:T(8,128)(2,1)S(1)}) custom-call(s32[1]{0:T(128)} %bitcast.me_ref, f32[64,512]{1,0:T(8,128)S(1)} %get-tuple-element.57.gh_ref, f32[64,512]{1,0:T(8,128)S(1)} %get-tuple-element.58.own_ref, ...), custom_call_target="tpu_custom_call" | custom-call | flops 402653184 | bytes 8749700 | tf_op jit(solution)/shard_map/pallas_call | solution.py:32
  47.8 5.7 %shard_map.169 = (f32[64,512]{1,0:T(8,128)S(1)}, f32[64,512]{1,0:T(8,128)S(1)}, bf16[32,512]{1,0:T(8,128)(2,1)S(1)}, bf16[512,512]{1,0:T(8,128)(2,1)}, bf16[8,12...) custom-call(s32[1]{0:T(128)} %bitcast.me_ref, f32[64,512]{1,0:T(8,128)S(1)} %get-tuple-element.65.gh_ref, ...), custom_call_target="tpu_custom_call" | custom-call | flops 1610612736 | bytes 10784772 | tf_op jit(solution)/shard_map/pallas_call | solution.py:32
  54.7 2.8 %collective-permute-done.3 = bf16[32,512]{1,0:T(8,128)(2,1)S(1)} collective-permute-done((bf16[32,512]{1,0:T(8,128)(2,1)S(1)}, bf16[32,512]{1,0:T(8,128)(2,1)S(1)}, u32[]{:S(2)}, u32[]{:S(2)}) %collective-permute-start.3) | collective-permute-done | bytes 32800 | tf_op jit(solution)/shard_map/ppermute | solution.py:297
  64.4 7.4 %collective-permute-done.20 = bf16[4,96,512]{2,1,0:T(8,128)(2,1)S(1)} collective-permute-done((bf16[4,96,512]{2,1,0:T(8,128)(2,1)S(1)}, bf16[4,96,512]{2,1,0:T(8,128)(2,1)S(1)}, u32[]{:S(2)}, u32[]{:S(2)}) %collective-permute-start.20) | collective-permute-done | bytes 393248 | tf_op jit(solution)/shard_map/ppermute | solution.py:307
  74.5 5.8 %collective-permute-done.15 = bf16[4,96,512]{2,1,0:T(8,128)(2,1)S(1)} collective-permute-done((bf16[4,96,512]{2,1,0:T(8,128)(2,1)S(1)}, bf16[4,96,512]{2,1,0:T(8,128)(2,1)S(1)}, u32[]{:S(2)}, u32[]{:S(2)}) %collective-permute-start.15) | collective-permute-done | bytes 393248 | tf_op jit(solution)/shard_map/ppermute | solution.py:307
  80.3 1.7 %collective-permute-start.16 = (bf16[2,96,512]{2,1,0:T(8,128)(2,1)S(1)}, bf16[2,96,512]{2,1,0:T(8,128)(2,1)S(1)}, u32[]{:S(2)}, u32[]{:S(2)}) collective-permute-start(bf16[2,96,512]{2,1,0:T(8,128)(2,1)S(1)} %add_convert_fusion.7), channel_id=1, source_target_pairs={{0,8},{2,10},{4,12},{6,14},{8,0},{10,2},{12,4},{14,6},{16,24},{18,... | collective-permute-start | bytes 589832 | tf_op jit(solution)/shard_map/ppermute | solution.py:307
  82.9 2.6 %collective-permute-start.22 = (bf16[1,96,512]{2,1,0:T(8,128)(2,1)S(1)}, bf16[1,96,512]{2,1,0:T(8,128)(2,1)S(1)}, u32[]{:S(2)}, u32[]{:S(2)}) collective-permute-start(bf16[1,96,512]{2,1,0:T(8,128)(2,1)S(1)} %add_convert_fusion.13), channel_id=1, source_target_pairs={{0,16},{2,18},{4,20},{6,22},{8,24},{10,26},{12,28},{14,30},{16,0},... | collective-permute-start | bytes 294920 | tf_op jit(solution)/shard_map/ppermute | solution.py:307
  87.2 2.6 %collective-permute-start.17 = (bf16[1,96,512]{2,1,0:T(8,128)(2,1)S(1)}, bf16[1,96,512]{2,1,0:T(8,128)(2,1)S(1)}, u32[]{:S(2)}, u32[]{:S(2)}) collective-permute-start(bf16[1,96,512]{2,1,0:T(8,128)(2,1)S(1)} %add_convert_fusion.15), channel_id=1, source_target_pairs={{0,16},{2,18},{4,20},{6,22},{8,24},{10,26},{12,28},{14,30},{16,0},... | collective-permute-start | bytes 294920 | tf_op jit(solution)/shard_map/ppermute | solution.py:307
  91.8 2.1 %collective-permute-done.17 = bf16[1,96,512]{2,1,0:T(8,128)(2,1)S(1)} collective-permute-done((bf16[1,96,512]{2,1,0:T(8,128)(2,1)S(1)}, bf16[1,96,512]{2,1,0:T(8,128)(2,1)S(1)}, u32[]{:S(2)}, u32[]{:S(2)}) %collective-permute-start.17) | collective-permute-done | bytes 98336 | tf_op jit(solution)/shard_map/ppermute | solution.py:307
  96.8 1.9 %collective-permute-done.18 = bf16[96,512]{1,0:T(8,128)(2,1)S(1)} collective-permute-done((bf16[96,512]{1,0:T(8,128)(2,1)S(1)}, bf16[96,512]{1,0:T(8,128)(2,1)S(1)}, u32[]{:S(2)}, u32[]{:S(2)}) %collective-permute-start.18) | collective-permute-done | bytes 98336 | tf_op jit(solution)/shard_map/ppermute | solution.py:307
  98.7 2.3 %collective-permute-done.5 = bf16[4,128,512]{2,1,0:T(8,128)(2,1)S(1)} collective-permute-done((bf16[4,128,512]{2,1,0:T(8,128)(2,1)S(1)}, bf16[4,128,512]{2,1,0:T(8,128)(2,1)S(1)}, u32[]{:S(2)}, u32[]{:S(2)}) %collective-permute-start.5) | collective-permute-done | bytes 524320 | tf_op jit(solution)/shard_map/ppermute | solution.py:307
  104.3 2.6 %collective-permute-start.12 = (bf16[1,128,512]{2,1,0:T(8,128)(2,1)S(1)}, bf16[1,128,512]{2,1,0:T(8,128)(2,1)S(1)}, u32[]{:S(2)}, u32[]{:S(2)}) collective-permute-start(bf16[1,128,512]{2,1,0:T(8,128)(2,1)S(1)} %add_convert_fusion.9), channel_id=1, source_target_pairs={{0,16},{2,18},{4,20},{6,22},{8,24},{10,26},{12,28},{14,30},{16,0},... | collective-permute-start | bytes 393224 | tf_op jit(solution)/shard_map/ppermute | solution.py:307
  106.9 2.7 %collective-permute-done.6 = bf16[2,128,512]{2,1,0:T(8,128)(2,1)S(1)} collective-permute-done((bf16[2,128,512]{2,1,0:T(8,128)(2,1)S(1)}, bf16[2,128,512]{2,1,0:T(8,128)(2,1)S(1)}, u32[]{:S(2)}, u32[]{:S(2)}) %collective-permute-start.6) | collective-permute-done | bytes 262176 | tf_op jit(solution)/shard_map/ppermute | solution.py:307
  109.7 2.3 %collective-permute-start.7 = (bf16[1,128,512]{2,1,0:T(8,128)(2,1)S(1)}, bf16[1,128,512]{2,1,0:T(8,128)(2,1)S(1)}, u32[]{:S(2)}, u32[]{:S(2)}) collective-permute-start(bf16[1,128,512]{2,1,0:T(8,128)(2,1)S(1)} %add_convert_fusion.11), channel_id=1, source_target_pairs={{0,16},{2,18},{4,20},{6,22},{8,24},{10,26},{12,28},{14,30},{16,0},... | collective-permute-start | bytes 393224 | tf_op jit(solution)/shard_map/ppermute | solution.py:307
  112.0 3.0 %collective-permute-done.12 = bf16[1,128,512]{2,1,0:T(8,128)(2,1)S(1)} collective-permute-done((bf16[1,128,512]{2,1,0:T(8,128)(2,1)S(1)}, bf16[1,128,512]{2,1,0:T(8,128)(2,1)S(1)}, u32[]{:S(2)}, u32[]{:S(2)}) %collective-permute-start.12) | collective-permute-done | bytes 131104 | tf_op jit(solution)/shard_map/ppermute | solution.py:307
  116.1 1.8 %collective-permute-done.7 = bf16[1,128,512]{2,1,0:T(8,128)(2,1)S(1)} collective-permute-done((bf16[1,128,512]{2,1,0:T(8,128)(2,1)S(1)}, bf16[1,128,512]{2,1,0:T(8,128)(2,1)S(1)}, u32[]{:S(2)}, u32[]{:S(2)}) %collective-permute-start.7) | collective-permute-done | bytes 131104 | tf_op jit(solution)/shard_map/ppermute | solution.py:307
  118.9 1.8 %collective-permute-done.13 = bf16[128,512]{1,0:T(8,128)(2,1)S(1)} collective-permute-done((bf16[128,512]{1,0:T(8,128)(2,1)S(1)}, bf16[128,512]{1,0:T(8,128)(2,1)S(1)}, u32[]{:S(2)}, u32[]{:S(2)}) %collective-permute-start.13) | collective-permute-done | bytes 131104 | tf_op jit(solution)/shard_map/ppermute | solution.py:307
  120.8 2.1 %collective-permute-done.8 = bf16[128,512]{1,0:T(8,128)(2,1)S(1)} collective-permute-done((bf16[128,512]{1,0:T(8,128)(2,1)S(1)}, bf16[128,512]{1,0:T(8,128)(2,1)S(1)}, u32[]{:S(2)}, u32[]{:S(2)}) %collective-permute-start.8) | collective-permute-done | bytes 131104 | tf_op jit(solution)/shard_map/ppermute | solution.py:307
  (133 shorter events, 43.2 us)
Async XLA Ops:
  2.3 5.9 %collective-permute-start = (bf16[32,512]{1,0:T(8,128)(2,1)S(1)}, bf16[32,512]{1,0:T(8,128)(2,1)S(1)}, u32[]{:S(2)}, u32[]{:S(2)}) collective-permute-start(bf16[32,512]{1,0:T(8,128)(2,1)S(1)} %shard_map.163), channel_id=1, source_target_pairs={{0,1},{1,0},{2,3},{3,2},{4,5},{5,4},{6,7},{7,6},{8,9},{9,8},{10,11... | collective-permute-start | bytes 98312 | tf_op jit(solution)/shard_map/ppermute | solution.py:297
  22.6 4.2 %collective-permute-start.1 = (bf16[32,512]{1,0:T(8,128)(2,1)}, bf16[32,512]{1,0:T(8,128)(2,1)}, u32[]{:S(2)}, u32[]{:S(2)}) collective-permute-start(bf16[32,512]{1,0:T(8,128)(2,1)} %get-tuple-element.50), channel_id=1, source_target_pairs={{0,1},{1,0},{2,3},{3,2},{4,5},{5,4},{6,7},{7,6},{8,9},{9,8},{10,11... | collective-permute-start | bytes 98312 | tf_op jit(solution)/shard_map/ppermute | solution.py:297
  40.5 3.9 %collective-permute-start.2 = (bf16[32,512]{1,0:T(8,128)(2,1)S(1)}, bf16[32,512]{1,0:T(8,128)(2,1)S(1)}, u32[]{:S(2)}, u32[]{:S(2)}) collective-permute-start(bf16[32,512]{1,0:T(8,128)(2,1)S(1)} %get-tuple-element.59), channel_id=1, source_target_pairs={{0,1},{1,0},{2,3},{3,2},{4,5},{5,4},{6,7},{7,6},{8,9},{9,8},{10,11... | collective-permute-start | bytes 98312 | tf_op jit(solution)/shard_map/ppermute | solution.py:297
  41.5 17.1 %collective-permute-start.19 = (bf16[8,96,512]{2,1,0:T(8,128)(2,1)S(1)}, bf16[8,96,512]{2,1,0:T(8,128)(2,1)}, u32[]{:S(2)}, u32[]{:S(2)}) collective-permute-start(bf16[8,96,512]{2,1,0:T(8,128)(2,1)S(1)} %get-tuple-element.83), channel_id=1, source_target_pairs={{0,2},{2,0},{4,6},{6,4},{8,10},{10,8},{12,14},{14,12},{16,18},{18,... | collective-permute-start | bytes 2359304 | tf_op jit(solution)/shard_map/ppermute | solution.py:307
  41.5 20.5 %collective-permute-start.9 = (bf16[8,128,512]{2,1,0:T(8,128)(2,1)}, bf16[8,128,512]{2,1,0:T(8,128)(2,1)S(1)}, u32[]{:S(2)}, u32[]{:S(2)}) collective-permute-start(bf16[8,128,512]{2,1,0:T(8,128)(2,1)} %get-tuple-element.79), channel_id=1, source_target_pairs={{0,2},{2,0},{4,6},{6,4},{8,10},{10,8},{12,14},{14,12},{16,18},{18,... | collective-permute-start | bytes 3145736 | tf_op jit(solution)/shard_map/ppermute | solution.py:307
  47.7 13.6 %collective-permute-start.14 = (bf16[8,96,512]{2,1,0:T(8,128)(2,1)S(1)}, bf16[8,96,512]{2,1,0:T(8,128)(2,1)S(1)}, u32[]{:S(2)}, u32[]{:S(2)}) collective-permute-start(bf16[8,96,512]{2,1,0:T(8,128)(2,1)S(1)} %get-tuple-element.81), channel_id=1, source_target_pairs={{0,2},{2,0},{4,6},{6,4},{8,10},{10,8},{12,14},{14,12},{16,18},{18,... | collective-permute-start | bytes 2359304 | tf_op jit(solution)/shard_map/ppermute | solution.py:307
  53.5 3.9 %collective-permute-start.3 = (bf16[32,512]{1,0:T(8,128)(2,1)S(1)}, bf16[32,512]{1,0:T(8,128)(2,1)S(1)}, u32[]{:S(2)}, u32[]{:S(2)}) collective-permute-start(bf16[32,512]{1,0:T(8,128)(2,1)S(1)} %get-tuple-element.74), channel_id=1, source_target_pairs={{0,1},{1,0},{2,3},{3,2},{4,5},{5,4},{6,7},{7,6},{8,9},{9,8},{10,11... | collective-permute-start | bytes 98312 | tf_op jit(solution)/shard_map/ppermute | solution.py:297
  54.5 9.2 %collective-permute-start.4 = (bf16[8,128,512]{2,1,0:T(8,128)(2,1)S(1)}, bf16[8,128,512]{2,1,0:T(8,128)(2,1)S(1)}, u32[]{:S(2)}, u32[]{:S(2)}) collective-permute-start(bf16[8,128,512]{2,1,0:T(8,128)(2,1)S(1)} %get-tuple-element.77), channel_id=1, source_target_pairs={{0,2},{2,0},{4,6},{6,4},{8,10},{10,8},{12,14},{14,12},{16,18},{18,... | collective-permute-start | bytes 3145736 | tf_op jit(solution)/shard_map/ppermute | solution.py:307
  59.7 12.1 %collective-permute-start.20 = (bf16[4,96,512]{2,1,0:T(8,128)(2,1)S(1)}, bf16[4,96,512]{2,1,0:T(8,128)(2,1)S(1)}, u32[]{:S(2)}, u32[]{:S(2)}) collective-permute-start(bf16[4,96,512]{2,1,0:T(8,128)(2,1)S(1)} %add_convert_fusion.2), channel_id=1, source_target_pairs={{0,4},{2,6},{4,0},{6,2},{8,12},{10,14},{12,8},{14,10},{16,20},{18,... | collective-permute-start | bytes 1179656 | tf_op jit(solution)/shard_map/ppermute | solution.py:307
  61.4 18.9 %collective-permute-start.15 = (bf16[4,96,512]{2,1,0:T(8,128)(2,1)S(1)}, bf16[4,96,512]{2,1,0:T(8,128)(2,1)S(1)}, u32[]{:S(2)}, u32[]{:S(2)}) collective-permute-start(bf16[4,96,512]{2,1,0:T(8,128)(2,1)S(1)} %add_convert_fusion.3), channel_id=1, source_target_pairs={{0,4},{2,6},{4,0},{6,2},{8,12},{10,14},{12,8},{14,10},{16,20},{18,... | collective-permute-start | bytes 1179656 | tf_op jit(solution)/shard_map/ppermute | solution.py:307
  62.1 33.4 %collective-permute-start.10 = (bf16[4,128,512]{2,1,0:T(8,128)(2,1)S(1)}, bf16[4,128,512]{2,1,0:T(8,128)(2,1)S(1)}, u32[]{:S(2)}, u32[]{:S(2)}) collective-permute-start(bf16[4,128,512]{2,1,0:T(8,128)(2,1)S(1)} %add_convert_fusion), channel_id=1, source_target_pairs={{0,4},{2,6},{4,0},{6,2},{8,12},{10,14},{12,8},{14,10},{16,20},{18,... | collective-permute-start | bytes 1572872 | tf_op jit(solution)/shard_map/ppermute | solution.py:307
  63.8 37.2 %collective-permute-start.5 = (bf16[4,128,512]{2,1,0:T(8,128)(2,1)S(1)}, bf16[4,128,512]{2,1,0:T(8,128)(2,1)S(1)}, u32[]{:S(2)}, u32[]{:S(2)}) collective-permute-start(bf16[4,128,512]{2,1,0:T(8,128)(2,1)S(1)} %add_convert_fusion.1), channel_id=1, source_target_pairs={{0,4},{2,6},{4,0},{6,2},{8,12},{10,14},{12,8},{14,10},{16,20},{18,... | collective-permute-start | bytes 1572872 | tf_op jit(solution)/shard_map/ppermute | solution.py:307
  72.8 9.2 %collective-permute-start.21 = (bf16[2,96,512]{2,1,0:T(8,128)(2,1)S(1)}, bf16[2,96,512]{2,1,0:T(8,128)(2,1)S(1)}, u32[]{:S(2)}, u32[]{:S(2)}) collective-permute-start(bf16[2,96,512]{2,1,0:T(8,128)(2,1)S(1)} %add_convert_fusion.6), channel_id=1, source_target_pairs={{0,8},{2,10},{4,12},{6,14},{8,0},{10,2},{12,4},{14,6},{16,24},{18,... | collective-permute-start | bytes 589832 | tf_op jit(solution)/shard_map/ppermute | solution.py:307
  80.3 6.8 %collective-permute-start.16 = (bf16[2,96,512]{2,1,0:T(8,128)(2,1)S(1)}, bf16[2,96,512]{2,1,0:T(8,128)(2,1)S(1)}, u32[]{:S(2)}, u32[]{:S(2)}) collective-permute-start(bf16[2,96,512]{2,1,0:T(8,128)(2,1)S(1)} %add_convert_fusion.7), channel_id=1, source_target_pairs={{0,8},{2,10},{4,12},{6,14},{8,0},{10,2},{12,4},{14,6},{16,24},{18,... | collective-permute-start | bytes 589832 | tf_op jit(solution)/shard_map/ppermute | solution.py:307
  82.9 6.9 %collective-permute-start.22 = (bf16[1,96,512]{2,1,0:T(8,128)(2,1)S(1)}, bf16[1,96,512]{2,1,0:T(8,128)(2,1)S(1)}, u32[]{:S(2)}, u32[]{:S(2)}) collective-permute-start(bf16[1,96,512]{2,1,0:T(8,128)(2,1)S(1)} %add_convert_fusion.13), channel_id=1, source_target_pairs={{0,16},{2,18},{4,20},{6,22},{8,24},{10,26},{12,28},{14,30},{16,0},... | collective-permute-start | bytes 294920 | tf_op jit(solution)/shard_map/ppermute | solution.py:307
  87.2 6.7 %collective-permute-start.17 = (bf16[1,96,512]{2,1,0:T(8,128)(2,1)S(1)}, bf16[1,96,512]{2,1,0:T(8,128)(2,1)S(1)}, u32[]{:S(2)}, u32[]{:S(2)}) collective-permute-start(bf16[1,96,512]{2,1,0:T(8,128)(2,1)S(1)} %add_convert_fusion.15), channel_id=1, source_target_pairs={{0,16},{2,18},{4,20},{6,22},{8,24},{10,26},{12,28},{14,30},{16,0},... | collective-permute-start | bytes 294920 | tf_op jit(solution)/shard_map/ppermute | solution.py:307
  90.8 4.7 %collective-permute-start.23 = (bf16[96,512]{1,0:T(8,128)(2,1)S(1)}, bf16[96,512]{1,0:T(8,128)(2,1)S(1)}, u32[]{:S(2)}, u32[]{:S(2)}) collective-permute-start(bf16[96,512]{1,0:T(8,128)(2,1)S(1)} %fusion.3), channel_id=1, source_target_pairs={{0,1},{1,0},{2,3},{3,2},{4,5},{5,4},{6,7},{7,6},{8,9},{9,8},{10,11... | collective-permute-start | bytes 294920 | tf_op jit(solution)/shard_map/ppermute | solution.py:307
  94.0 4.7 %collective-permute-start.18 = (bf16[96,512]{1,0:T(8,128)(2,1)S(1)}, bf16[96,512]{1,0:T(8,128)(2,1)S(1)}, u32[]{:S(2)}, u32[]{:S(2)}) collective-permute-start(bf16[96,512]{1,0:T(8,128)(2,1)S(1)} %fusion.2), channel_id=1, source_target_pairs={{0,1},{1,0},{2,3},{3,2},{4,5},{5,4},{6,7},{7,6},{8,9},{9,8},{10,11... | collective-permute-start | bytes 294920 | tf_op jit(solution)/shard_map/ppermute | solution.py:307
  95.7 8.5 %collective-permute-start.11 = (bf16[2,128,512]{2,1,0:T(8,128)(2,1)S(1)}, bf16[2,128,512]{2,1,0:T(8,128)(2,1)S(1)}, u32[]{:S(2)}, u32[]{:S(2)}) collective-permute-start(bf16[2,128,512]{2,1,0:T(8,128)(2,1)S(1)} %add_convert_fusion.4), channel_id=1, source_target_pairs={{0,8},{2,10},{4,12},{6,14},{8,0},{10,2},{12,4},{14,6},{16,24},{18,... | collective-permute-start | bytes 786440 | tf_op jit(solution)/shard_map/ppermute | solution.py:307
  101.1 8.5 %collective-permute-start.6 = (bf16[2,128,512]{2,1,0:T(8,128)(2,1)S(1)}, bf16[2,128,512]{2,1,0:T(8,128)(2,1)S(1)}, u32[]{:S(2)}, u32[]{:S(2)}) collective-permute-start(bf16[2,128,512]{2,1,0:T(8,128)(2,1)S(1)} %add_convert_fusion.5), channel_id=1, source_target_pairs={{0,8},{2,10},{4,12},{6,14},{8,0},{10,2},{12,4},{14,6},{16,24},{18,... | collective-permute-start | bytes 786440 | tf_op jit(solution)/shard_map/ppermute | solution.py:307
  104.3 10.7 %collective-permute-start.12 = (bf16[1,128,512]{2,1,0:T(8,128)(2,1)S(1)}, bf16[1,128,512]{2,1,0:T(8,128)(2,1)S(1)}, u32[]{:S(2)}, u32[]{:S(2)}) collective-permute-start(bf16[1,128,512]{2,1,0:T(8,128)(2,1)S(1)} %add_convert_fusion.9), channel_id=1, source_target_pairs={{0,16},{2,18},{4,20},{6,22},{8,24},{10,26},{12,28},{14,30},{16,0},... | collective-permute-start | bytes 393224 | tf_op jit(solution)/shard_map/ppermute | solution.py:307
  109.7 8.1 %collective-permute-start.7 = (bf16[1,128,512]{2,1,0:T(8,128)(2,1)S(1)}, bf16[1,128,512]{2,1,0:T(8,128)(2,1)S(1)}, u32[]{:S(2)}, u32[]{:S(2)}) collective-permute-start(bf16[1,128,512]{2,1,0:T(8,128)(2,1)S(1)} %add_convert_fusion.11), channel_id=1, source_target_pairs={{0,16},{2,18},{4,20},{6,22},{8,24},{10,26},{12,28},{14,30},{16,0},... | collective-permute-start | bytes 393224 | tf_op jit(solution)/shard_map/ppermute | solution.py:307
  115.1 5.7 %collective-permute-start.13 = (bf16[128,512]{1,0:T(8,128)(2,1)S(1)}, bf16[128,512]{1,0:T(8,128)(2,1)S(1)}, u32[]{:S(2)}, u32[]{:S(2)}) collective-permute-start(bf16[128,512]{1,0:T(8,128)(2,1)S(1)} %fusion.1), channel_id=1, source_target_pairs={{0,1},{1,0},{2,3},{3,2},{4,5},{5,4},{6,7},{7,6},{8,9},{9,8},{10,11... | collective-permute-start | bytes 393224 | tf_op jit(solution)/shard_map/ppermute | solution.py:307
  117.9 5.0 %collective-permute-start.8 = (bf16[128,512]{1,0:T(8,128)(2,1)S(1)}, bf16[128,512]{1,0:T(8,128)(2,1)S(1)}, u32[]{:S(2)}, u32[]{:S(2)}) collective-permute-start(bf16[128,512]{1,0:T(8,128)(2,1)S(1)} %fusion), channel_id=1, source_target_pairs={{0,1},{1,0},{2,3},{3,2},{4,5},{5,4},{6,7},{7,6},{8,9},{9,8},{10,11... | collective-permute-start | bytes 393224 | tf_op jit(solution)/shard_map/ppermute | solution.py:307
  (29 other events, 152.7 us)

commit v2 on v1

v2 whole, which is shorter than its diff:
```python
import functools

import jax
import jax.numpy as jnp
from jax import lax
from jax.experimental import pallas as pl
from jax.experimental.pallas import tpu as pltpu
from jax.sharding import PartitionSpec as P

F32 = jnp.float32
BF16 = jnp.bfloat16
VMEM = pltpu.VMEM
EPS = 1e-05
MIB = 1024 * 1024
LIMIT = 20 * MIB


def in_hbm(array):
    return pltpu.with_memory_space_constraint(array, pltpu.HBM)


class Part:
    def __init__(self, array, index=(), shape=None, pin=True):
        self.array, self.index = (in_hbm(array) if pin else array), index
        self.shape = tuple(array.shape if shape is None else shape)


def rows_of(weight, layer, start=0, stop=None):
    stop = weight.shape[1] if stop is None else stop
    return Part(weight, (layer, pl.ds(start, stop - start)), (stop - start, weight.shape[2]))


class Arriving:
    def __init__(self, copy, ref):
        self.copy, self.ref, self.shape, self.dtype = copy, ref, ref.shape, ref.dtype

    def __getitem__(self, index):
        if self.copy is not None:
            self.copy.wait()
            self.copy = None
        return self.ref[index]


class Leaving:
    def __init__(self, copy, ref):
        self.copy, self.ref, self.shape, self.dtype = copy, ref, ref.shape, ref.dtype
        self.started = False

    def __getitem__(self, index):
        return self.ref[index]

    def __setitem__(self, index, value):
        self.ref[index] = value

    def flush(self):
        if not self.started:
            self.copy.start()
            self.started = True


def far(shape, dtype):
    return (shape, dtype, True)


def call(kernel, operands, outs, scratch=(), smem=(), after=(), fetch=(), limit=LIMIT):
    shapes = [jax.ShapeDtypeStruct(out[0], out[1]) for out in outs]
    is_far = [len(out) > 2 for out in outs] + [False] * len(fetch)
    results = len(shapes)
    shapes += [jax.ShapeDtypeStruct(p.shape, p.array.dtype) for p in fetch]
    remote = [isinstance(p, Part) for p in operands]
    arrays = [p.array if r else p for p, r in zip(operands, remote)]
    buffers = [VMEM(p.shape, p.array.dtype) for p, r in zip(operands, remote) if r]
    buffers += [VMEM(s.shape, s.dtype) for s, r in zip(shapes, is_far) if r]
    copies = len(buffers) + len(fetch)
    sems = [pltpu.SemaphoreType.DMA((max(copies, 1),))]

    def run(*refs):
        refs = list(refs)

        def cut(count):
            taken = refs[:count]
            del refs[:count]
            return taken

        scalars, sources, origins = cut(len(smem)), cut(len(arrays)), cut(len(fetch))
        cut(len(after))
        targets, held, (sem,) = cut(len(shapes)), cut(len(buffers)), cut(1)
        sems = [sem.at[at] for at in range(copies)]
        ins, leaving, fetched = [], [], []
        for part, source, r in zip(operands, sources, remote):
            if r:
                view = source.at[part.index] if part.index else source
                ref = held.pop(0)
                copy = pltpu.make_async_copy(view, ref, sems.pop(0))
                copy.start()
                source = Arriving(copy, ref)
            ins.append(source)
        for part, origin, target in zip(fetch, origins, targets[results:]):
            view = origin.at[part.index] if part.index else origin
            copy = pltpu.make_async_copy(view, target, sems.pop(0))
            copy.start()
            fetched.append(copy)
        results_here = []
        for target, r in zip(targets[:results], is_far):
            if r:
                ref = held.pop(0)
                target = Leaving(pltpu.make_async_copy(ref, target, sems.pop(0)), ref)
                leaving.append(target)
            results_here.append(target)
        kernel(*scalars, *ins, *results_here, *refs)
        for ref in ins:
            if isinstance(ref, Arriving):
                ref[:1]
        for ref in leaving:
            ref.flush()
        for copy in fetched:
            copy.wait()
        for ref in leaving:
            ref.copy.wait()

    def space(r):
        return pl.BlockSpec(memory_space=pl.ANY if r else VMEM)

    return pl.pallas_call(
        run,
        in_specs=[pl.BlockSpec(memory_space=pltpu.SMEM)] * len(smem)
        + [space(r) for r in remote]
        + [space(True)] * len(fetch)
        + [pl.BlockSpec(memory_space=pl.ANY)] * len(after),
        out_specs=tuple(space(r) for r in is_far),
        out_shape=tuple((pltpu.HBM if r else VMEM)(s.shape, s.dtype) for s, r in zip(shapes, is_far)),
        scratch_shapes=buffers + sems + list(scratch),
        compiler_params=pltpu.CompilerParams(vmem_limit_bytes=limit),
        cost_estimate=pl.CostEstimate(flops=0, bytes_accessed=0, transcendentals=0),
    )(*smem, *arrays, *[p.array for p in fetch], *after)


def flush(*refs):
    for ref in refs:
        if isinstance(ref, Leaving):
            ref.flush()


def dot(a, b):
    return jnp.dot(a, b, preferred_element_type=F32)


def dot_nt(a, b):
    return lax.dot_general(a, b, (((1,), (1,)), ((), ())), preferred_element_type=F32)


def dot_tn(a, b):
    return lax.dot_general(a, b, (((0,), (0,)), ((), ())), preferred_element_type=F32)


def silu_and_slope(values):
    sigmoid = 0.5 * jnp.tanh(0.5 * values) + 0.5
    act = values * sigmoid
    return act, sigmoid + act * (1.0 - sigmoid)


def norm_parts(values):
    center = jnp.mean(values, axis=-1, keepdims=True)
    shifted = values - center
    inverse = lax.rsqrt(jnp.mean(shifted * shifted, axis=-1, keepdims=True) + EPS)
    return shifted * inverse, inverse


def norm_back(normed, inverse, upstream):
    return inverse * (
        upstream
        - jnp.mean(upstream, axis=-1, keepdims=True)
        - normed * jnp.mean(upstream * normed, axis=-1, keepdims=True)
    )


def halves(values):
    high = values.astype(BF16)
    low = (values - high.astype(F32)).astype(BF16)
    return jnp.concatenate([high, low], axis=0)


def node_of_edge(rows, nodes, slots):
    edge = lax.broadcasted_iota(jnp.int32, (rows, nodes), 0)
    node = lax.broadcasted_iota(jnp.int32, (rows, nodes), 1)
    return (edge // slots) == node


def pick_rows(send_ref, nodes):
    row = lax.broadcasted_iota(jnp.int32, (nodes, send_ref.shape[1]), 0)
    return (row == send_ref[...]).astype(F32).astype(BF16)


def pack_kernel(send_ref, h_ref, packed_ref):
    pick = pick_rows(send_ref, h_ref.shape[0])
    packed_ref[...] = dot_tn(pick, h_ref[...]).astype(BF16)


def prepare_kernel(
    table, chunk, nb_ref, count_ref, ocean_ref, h_ref, e_ref, we_ref, wr_ref,
    spread_ref, mask_ref, live_ref, wet_ref, pre_ref,
):
    slots, nodes = nb_ref.shape
    rows = nodes * slots
    owner = node_of_edge(rows, nodes, slots).astype(F32)
    owner16 = owner.astype(BF16)
    listed = dot_nt(owner16, nb_ref[...].astype(F32).astype(BF16))
    slot_here = lax.broadcasted_iota(jnp.int32, (rows, slots), 0) % slots
    slot_at = lax.broadcasted_iota(jnp.int32, (rows, slots), 1)
    source = jnp.sum(jnp.where(slot_here == slot_at, listed, 0.0), axis=1, keepdims=True)
    half = (table - nodes) // 2
    moved = jnp.where(source >= nodes + half, source - half, source + half)
    source = jnp.where(source >= nodes, moved, source)
    at = lax.broadcasted_iota(jnp.int32, (rows, table), 1).astype(F32)
    spread_ref[:, :table] = jnp.where(at == source, 1.0, 0.0).astype(BF16)
    spread_ref[:, table:] = owner16
    slot_of_row = lax.broadcasted_iota(jnp.int32, (rows, nodes), 0) % slots
    mask = jnp.where(slot_of_row < count_ref[...], owner, 0.0)
    mask_ref[...] = mask.astype(BF16)
    live_ref[...] = jnp.sum(mask, axis=1, keepdims=True)
    row = lax.broadcasted_iota(jnp.int32, (nodes, nodes), 0)
    column = lax.broadcasted_iota(jnp.int32, (nodes, nodes), 1)
    wet = jnp.where(row == column, ocean_ref[...].astype(F32), 0.0)
    wet_ref[...] = jnp.sum(wet, axis=1, keepdims=True)
    partial_kernel(chunk, h_ref, spread_ref, e_ref, we_ref, wr_ref, pre_ref)


def partial_kernel(chunk, h_ref, spread_ref, e_ref, we_ref, wr_ref, pre_ref):
    rows, width = e_ref.shape
    known = spread_ref.shape[1] - h_ref.shape[0]
    h = h_ref[...]
    for start in range(0, rows, chunk):
        at = pl.ds(start, chunk)
        own = dot(spread_ref[at, known:], h).astype(BF16)
        pre = dot(e_ref[at, :], we_ref[...])
        pre_ref[at, :] = pre + dot(own, wr_ref[...])


def forward_edges(chunk, pre_ref, e_ref, table, spread_ref, live_ref, ws_ref, wo_ref, put):
    rows, width = e_ref.shape
    known = table.shape[0]
    for start in range(0, rows, chunk):
        at = pl.ds(start, chunk)
        src = dot(spread_ref[at, :known], table).astype(BF16)
        pre = pre_ref[at, :] + dot(src, ws_ref[...])
        act, slope = silu_and_slope(pre)
        act = act.astype(BF16)
        normed, inverse = norm_parts(dot(act, wo_ref[...]))
        new_e = (e_ref[at, :].astype(F32) + live_ref[at, :] * normed).astype(BF16)
        put(at, act, slope, normed, inverse, new_e)


def forward_nodes(h, message, wi_ref, wo_ref):
    width = h.shape[1]
    pre = dot(h, wi_ref[:width, :]) + dot(message, wi_ref[width:, :])
    act, slope = silu_and_slope(pre)
    act = act.astype(BF16)
    normed, inverse = norm_parts(dot(act, wo_ref[...]))
    return act, slope, normed, inverse


def first_forward_kernel(
    chunk, pre_ref, e_ref, h_ref, halo_ref, spread_ref, mask_ref, live_ref, wet_ref, send_ref,
    ws_ref, weo_ref, wni_ref, wno_ref,
    act_ref, slope_ref, normed_ref, inverse_ref, new_e_ref,
    new_h_ref, message_ref, act_n_ref, slope_n_ref, normed_n_ref, inverse_n_ref, packed_ref,
):
    h = h_ref[...]
    table = jnp.concatenate([h, halo_ref[...]], axis=0)

    def put(at, act, slope, normed, inverse, new_e):
        act_ref[at, :] = act
        slope_ref[at, :] = slope.astype(BF16)
        normed_ref[at, :] = normed.astype(BF16)
        inverse_ref[at, :] = inverse
        new_e_ref[at, :] = new_e

    forward_edges(chunk, pre_ref, e_ref, table, spread_ref, live_ref, ws_ref, weo_ref, put)
    flush(act_ref, slope_ref, normed_ref, inverse_ref, new_e_ref)
    message = dot_tn(mask_ref[...], new_e_ref[...]).astype(BF16)
    act, slope, normed, inverse = forward_nodes(h, message, wni_ref, wno_ref)
    message_ref[...] = message
    act_n_ref[...] = act
    slope_n_ref[...] = slope.astype(BF16)
    normed_n_ref[...] = normed.astype(BF16)
    inverse_n_ref[...] = inverse
    flush(message_ref, act_n_ref, slope_n_ref, normed_n_ref, inverse_n_ref)
    new_h = (h.astype(F32) + wet_ref[...] * normed).astype(BF16)
    new_h_ref[...] = new_h
    packed_ref[...] = dot_tn(pick_rows(send_ref, h.shape[0]), new_h).astype(BF16)


def backward_nodes(gh, slope, normed, inverse, wet_ref, wi_ref, wo_ref, gout_ref, gpre_ref):
    gout = norm_back(normed, inverse, wet_ref[...] * gh).astype(BF16)
    gpre = (dot_nt(gout, wo_ref[...]) * slope).astype(BF16)
    gout_ref[...] = gout
    gpre_ref[...] = gpre
    ginput = dot_nt(gpre, wi_ref[...])
    width = gh.shape[1]
    return gh + ginput[:, :width], ginput[:, width:]


def backward_edges(
    chunk, known, gh, gmsg, ge_ref, spread_ref, live_ref, slope_ref, normed_ref, inverse_ref,
    we_ref, wr_ref, wo_ref, gh_out_ref, more_ref, own_ref, halo_out_ref, ge_out_ref, gedge_ref, gpe_ref, sums_ref,
):
    rows, width = ge_ref.shape
    nodes = gh.shape[0]
    gh_out_ref[...] = gh
    gmsg = halves(gmsg)
    for start in range(0, rows, chunk):
        at = pl.ds(start, chunk)
        live = live_ref[at, :]
        owner = spread_ref[at, known:]
        sent = dot(jnp.concatenate([owner, owner], axis=1), gmsg)
        ge = ge_ref[at, :].astype(F32) + live * sent
        gedge = norm_back(normed_ref[at, :].astype(F32), inverse_ref[at, :], live * ge)
        gedge = gedge.astype(BF16)
        gpe = (dot_nt(gedge, wo_ref[...]) * slope_ref[at, :].astype(F32)).astype(BF16)
        gedge_ref[at, :] = gedge
        gpe_ref[at, :] = gpe
        ge = ge + dot_nt(gpe, we_ref[...])
        ge_out_ref[at, :] = ge.astype(ge_out_ref.dtype)
    flush(gedge_ref, gpe_ref, ge_out_ref)
    gathered = dot_tn(spread_ref[...], gpe_ref[...])
    own_ref[...] = gathered[:nodes]
    halo_out_ref[...] = gathered[nodes:known].astype(BF16)
    sums_ref[...] = gathered.astype(BF16)
    both = dot_nt(halves(gathered[known:]), wr_ref[...])
    more_ref[...] = both[:nodes] + both[nodes:]


def middle_kernel(
    chunk, pre_ref, e_ref, h_ref, halo_ref, spread_ref, mask_ref, live_ref, wet_ref,
    gh_ref, ge_ref, ws_ref, weo_ref, wni_ref, wno_ref, we_ref, wr_ref,
    act_ref, message_ref, act_n_ref, gout_ref, gpre_ref,
    gh_out_ref, more_ref, own_ref, halo_out_ref, ge_out_ref, gedge_ref, gpe_ref, sums_ref,
    slope_ref, normed_ref, inverse_ref, new_e_ref,
):
    h = h_ref[...]
    table = jnp.concatenate([h, halo_ref[...]], axis=0)

    def put(at, act, slope, normed, inverse, new_e):
        act_ref[at, :] = act
        slope_ref[at, :] = slope.astype(BF16)
        normed_ref[at, :] = normed.astype(BF16)
        inverse_ref[at, :] = inverse
        new_e_ref[at, :] = new_e

    forward_edges(chunk, pre_ref, e_ref, table, spread_ref, live_ref, ws_ref, weo_ref, put)
    message = dot_tn(mask_ref[...], new_e_ref[...]).astype(BF16)
    act, slope, normed, inverse = forward_nodes(h, message, wni_ref, wno_ref)
    message_ref[...] = message
    act_n_ref[...] = act
    flush(act_ref)
    gh, gmsg = backward_nodes(
        gh_ref[...].astype(F32), slope, normed, inverse, wet_ref, wni_ref, wno_ref, gout_ref, gpre_ref
    )
    backward_edges(
        chunk, table.shape[0], gh, gmsg, ge_ref, spread_ref, live_ref, slope_ref, normed_ref,
        inverse_ref, we_ref, wr_ref, weo_ref, gh_out_ref, more_ref, own_ref, halo_out_ref, ge_out_ref,
        gedge_ref, gpe_ref, sums_ref,
    )


def return_halo(gh_ref, more_ref, own_ref, back_ref, send_ref, wei_ref):
    nodes, width = gh_ref.shape
    total = own_ref[...] + dot(pick_rows(send_ref, nodes), back_ref[...])
    both = dot_nt(halves(total), wei_ref[...])
    return gh_ref[...] + more_ref[...] + both[:nodes] + both[nodes:]


def first_backward_kernel(
    chunk, gh_ref, more_ref, own_ref, back_ref, send_ref, slope_n_ref, normed_n_ref, inverse_n_ref, wet_ref,
    ge_ref, spread_ref, live_ref, slope_ref, normed_ref, inverse_ref,
    ws_ref, wno_ref, wni_ref, weo_ref, we_ref, wr_ref,
    gout_ref, gpre_ref, gh_out_ref, more_out_ref, own_out_ref, halo_out_ref, ge_out_ref,
    gedge_ref, gpe_ref, sums_ref,
):
    gh = return_halo(gh_ref, more_ref, own_ref, back_ref, send_ref, ws_ref)
    gh, gmsg = backward_nodes(
        gh, slope_n_ref[...].astype(F32), normed_n_ref[...].astype(F32), inverse_n_ref[...],
        wet_ref, wni_ref, wno_ref, gout_ref, gpre_ref,
    )
    known = spread_ref.shape[1] - gh.shape[0]
    backward_edges(
        chunk, known, gh, gmsg, ge_ref, spread_ref, live_ref, slope_ref, normed_ref,
        inverse_ref, we_ref, wr_ref, weo_ref, gh_out_ref, more_out_ref, own_out_ref, halo_out_ref, ge_out_ref,
        gedge_ref, gpe_ref, sums_ref,
    )


def last_kernel(gh_ref, more_ref, own_ref, back_ref, send_ref, wei_ref, out_ref):
    out_ref[...] = return_halo(gh_ref, more_ref, own_ref, back_ref, send_ref, wei_ref)


def place(order, me_ref, first_ref, second_ref, keep_ref, sent_ref):
    rows = keep_ref.shape[1]
    count = keep_ref.shape[0]
    for bits in range(0, count, 2):
        spots = [order.index((bits, side)) for side in (0, 1)]
        for bit, out_ref in ((0, keep_ref), (1, sent_ref)):
            device = jnp.bitwise_xor(me_ref[0], bits + bit)
            row = 0
            for ref in (first_ref, second_ref):
                size = ref.shape[0] // count
                start = pl.multiple_of(device * size, 16)
                done = 0
                while done < size:
                    half, at = divmod(row, rows)
                    step = min(size - done, rows - at)
                    index = jnp.where(me_ref[1] == half, spots[0], spots[1])
                    piece = ref[pl.ds(pl.multiple_of(start + done, 16), step), :]
                    out_ref[index, at : at + step, :] = piece.astype(BF16)
                    row += step
                    done += step
            if row < 2 * rows:
                index = jnp.where(me_ref[1] == 1, spots[0], spots[1])
                filler = jnp.zeros((2 * rows - row, keep_ref.shape[2]), BF16)
                out_ref[index, row - rows :, :] = filler


def edge_weights_kernel(
    layout, me_ref, e_ref, h_ref, halo_ref, act_ref, gedge_ref, gpe_ref, sums_ref,
    keep_ref, sent_ref, grad_in_ref, grad_out_ref,
):
    width = e_ref.shape[1]
    h = h_ref[...]
    known = h.shape[0] + halo_ref.shape[0]
    table = jnp.concatenate([h, halo_ref[...]], axis=0)
    grad_in_ref[:width, :] = dot_tn(e_ref[...], gpe_ref[...])
    grad_in_ref[width : 2 * width, :] = dot_tn(table, sums_ref[:known, :])
    grad_in_ref[2 * width :, :] = dot_tn(h, sums_ref[known:, :])
    grad_out_ref[...] = dot_tn(act_ref[...], gedge_ref[...])
    place(layout, me_ref, grad_in_ref, grad_out_ref, keep_ref, sent_ref)


def node_weights_kernel(
    layout, me_ref, h_ref, message_ref, act_ref, gout_ref, gpre_ref,
    keep_ref, sent_ref, grad_in_ref, grad_out_ref,
):
    width = h_ref.shape[1]
    gpre = gpre_ref[...]
    grad_in_ref[:width, :] = dot_tn(h_ref[...], gpre)
    grad_in_ref[width:, :] = dot_tn(message_ref[...], gpre)
    grad_out_ref[...] = dot_tn(act_ref[...], gout_ref[...])
    place(layout, me_ref, grad_in_ref, grad_out_ref, keep_ref, sent_ref)


def trade(rows, back=False):
    count = lax.axis_size("mesh")
    if count == 2:
        return lax.ppermute(rows, "mesh", [(0, 1), (1, 0)])
    half = rows.shape[0] // 2
    up = [(i, (i + 1) % count) for i in range(count)]
    down = [(j, i) for i, j in up]
    first, second = (up, down) if back else (down, up)
    return jnp.concatenate(
        [lax.ppermute(rows[:half], "mesh", first), lax.ppermute(rows[half:], "mesh", second)], axis=0
    )


def flip(values, axis, bit):
    return lax.ppermute(values, axis, [(i, i ^ bit) for i in range(lax.axis_size(axis))])


def bits_of(axis):
    size = lax.axis_size(axis)
    return [1 << i for i in range(size.bit_length() - 1)]


def slot_order(route):
    order = [(0, 0)]
    for axis, bit in reversed(route):
        if axis == "dp":
            order = order + [(bits + bit, side) for bits, side in order]
        else:
            order = order + [(bits, 1) for bits, side in order]
    return order


class Sum:
    def __init__(self, keep):
        self.held = [(keep, 0)]
        self.slots, self.rows = keep.shape[0], keep.shape[1]

    def parts(self, start, stop):
        return [
            Part(
                array,
                (pl.ds(start, stop - start), pl.ds(row, self.rows)),
                (stop - start, self.rows, array.shape[2]),
                pin=at == 0,
            )
            for at, (array, row) in enumerate(self.held)
        ]


def add_kernel(groups, tail, *refs):
    refs = list(refs)
    count = sum(sum(group) for group in groups) + tail
    outs = refs[count:]
    if tail:
        more = refs[count - 1]
        outs[-1][outs[-1].shape[0] - 1, : more.shape[0], :] = more[...]
    for group, out in zip(groups, outs):
        row = 0
        for count in group:
            terms, refs = refs[:count], refs[count:]
            rows = terms[0].shape[1]
            total = sum(term[...].astype(F32) for term in terms)
            out[: terms[0].shape[0], row : row + rows, :] = total.astype(BF16)
            row += rows
        flush(out)


def add(wanted, after=(), tail=None):
    operands, groups, outs = [], [], []
    for sums in wanted:
        group, count = [], 0
        for one in sums:
            if one.slots > 1:
                one.slots //= 2
                span = (one.slots, 2 * one.slots)
            else:
                span = (0, 1)
            parts = one.parts(*span)
            operands += parts
            group.append(len(parts))
            count = span[1] - span[0]
        groups.append(group)
        outs.append(((count, sum(one.rows for one in sums), parts[0].shape[2]), BF16))
    if tail is not None:
        (count, size, depth), dtype = outs[-1]
        outs[-1] = ((count + 1, size, depth), dtype)
        operands.append(tail)
    return call(functools.partial(add_kernel, groups, tail is not None), operands, outs, after=after)


def take(sums, values):
    row = 0
    for one in sums:
        one.held.append((values, row))
        row += one.rows


def gather(values):
    mine = values[0]
    for bit in bits_of("mesh")[1:]:
        mine = (mine.astype(F32) + flip(mine, "mesh", bit).astype(F32)).astype(BF16)
    return mine, flip(mine, "mesh", 1)


def output_kernel(
    factor, splits, me_ref, mine0_ref, other0_ref, mine1_ref, other1_ref, *outs
):
    low = me_ref[1] == 0
    for layer, (mine, other) in enumerate(((mine0_ref, other0_ref), (mine1_ref, other1_ref))):
        row = 0
        for pair, rows in enumerate(splits):
            a = mine[row : row + rows, :].astype(F32) * factor
            b = other[row : row + rows, :].astype(F32) * factor
            both = jnp.concatenate([jnp.where(low, a, b), jnp.where(low, b, a)], axis=0)
            first, second = outs[2 * pair], outs[2 * pair + 1]
            cut, end = first.shape[1], first.shape[1] + second.shape[1]
            first[layer] = both[:cut]
            second[layer] = both[cut:end]
            row += rows


def body(
    node_feats,
    edge_feats,
    node_cot,
    edge_cot,
    w_edge_in,
    w_edge_out,
    w_node_in,
    w_node_out,
    neighbours,
    send_rows,
    edge_counts,
    ocean_mask,
):
    samples, nodes, width = node_feats.shape
    slots = neighbours.shape[1]
    rows = nodes * slots
    sent = send_rows.shape[1]
    known = nodes + sent
    chunk = rows // 2
    shards = lax.axis_size("dp")
    total_rows = samples * shards * nodes * lax.axis_size("mesh")
    factor = 1.0 / total_rows**0.5
    beyond = [("dp", bit) for bit in bits_of("dp")[2:]]
    edge_route = [("dp", 2), ("mesh", 1)] + beyond
    node_route = [("mesh", 1), ("dp", 2)] + beyond
    edge_order, node_order = slot_order(edge_route), slot_order(node_route)
    me = jnp.stack([lax.axis_index("dp"), lax.axis_index("mesh") % 2]).astype(jnp.int32)

    h0 = node_feats.reshape(nodes, width)
    e0 = edge_feats.reshape(rows, width)
    gh = node_cot.reshape(nodes, width)
    ge = edge_cot.reshape(rows, width)
    weights = (w_edge_in, w_edge_out, w_node_in, w_node_out)
    small, large, thin = (nodes, width), (rows, width), (sent, width)
    source = [rows_of(w_edge_in, layer, width, 2 * width) for layer in range(2)]
    edge = [rows_of(w_edge_in, layer, 0, width) for layer in range(2)]
    receiver = [rows_of(w_edge_in, layer, 2 * width) for layer in range(2)]
    edge_out = [rows_of(w_edge_out, layer) for layer in range(2)]
    node_in = [rows_of(w_node_in, layer) for layer in range(2)]
    node_out = [rows_of(w_node_out, layer) for layer in range(2)]

    (packed0,) = call(pack_kernel, (Part(send_rows), Part(h0)), [(thin, BF16)])
    halo0 = trade(packed0)
    spread, mask, live, wet, pre0, h0_near, e0_near, source0, edge_out0, node_in0, node_out0 = call(
        functools.partial(prepare_kernel, known, chunk),
        (Part(neighbours.T), Part(edge_counts.reshape(1, nodes)), Part(ocean_mask.reshape(1, nodes)))
        + (Part(h0), Part(e0), edge[0], receiver[0]),
        [
            ((rows, known + nodes), BF16), ((rows, nodes), BF16), ((rows, 1), F32),
            ((nodes, 1), F32), (large, F32),
        ],
        fetch=(Part(h0), Part(e0), source[0], edge_out[0], node_in[0], node_out[0]),
    )
    (
        act0, slope0, normed0, inverse0, e1,
        h1, message0, act_n0, slope_n0, normed_n0, inverse_n0, packed1,
        edge1_w, receiver1_w, source1_w,
    ) = call(
        functools.partial(first_forward_kernel, chunk),
        (pre0, e0_near, h0_near, halo0, spread, mask, live, wet, send_rows)
        + (source0, edge_out0, node_in0, node_out0),
        [far(large, BF16)] * 3 + [far((rows, 1), F32), (large, BF16), (small, BF16)]
        + [far(small, BF16)] * 4 + [far((nodes, 1), F32), (thin, BF16)],
        fetch=(edge[1], receiver[1], source[1]),
    )
    halo1 = trade(packed1)
    pre1, edge_out1, node_in1, node_out1, gh_near, ge_near = call(
        functools.partial(partial_kernel, chunk),
        (h1, spread, e1, edge1_w, receiver1_w),
        [(large, F32)],
        fetch=(edge_out[1], node_in[1], node_out[1], Part(gh), Part(ge)),
    )
    backward_outs = [(small, F32)] * 3 + [(thin, BF16)]
    backward_tail = [(large, BF16)] * 2 + [((known + nodes, width), BF16)]
    act1, message1, act_n1, gout1, gpre1, gh, more, own, halo_out, ge, gedge1, gpe1, sums1, *near_w = call(
        functools.partial(middle_kernel, chunk),
        (pre1, e1, h1, halo1, spread, mask, live, wet, gh_near, ge_near)
        + (source1_w, edge_out1, node_in1, node_out1, edge1_w, receiver1_w),
        [(large, BF16)] + [(small, BF16)] * 4 + backward_outs + [far(large, F32)] + backward_tail,
        scratch=[VMEM(large, BF16)] * 2 + [VMEM((rows, 1), F32), VMEM(large, BF16)],
        fetch=(node_out[0], node_in[0], edge_out[0], edge[0], receiver[0]),
    )
    back = trade(halo_out, back=True)

    def weight_sum(kernel, order, operands, kinds, after=(), fetch=()):
        size = sum(w.shape[1] // shards for w in kinds)
        size = -(-size // 32) * 32
        keep, send, *fetched = call(
            functools.partial(kernel, order),
            operands,
            [far((shards, size // 2, width), BF16), ((shards, size // 2, width), BF16)],
            scratch=[VMEM(w.shape[1:], F32) for w in kinds],
            smem=(me,),
            after=after,
            fetch=fetch,
        )
        one = Sum(keep)
        take([one], flip(send, "dp", 1))
        return one, fetched

    def edge_sum(e, h, halo, act, gedge, gpe, sums, **more):
        return weight_sum(
            edge_weights_kernel, edge_order,
            (e, h, halo, act, gedge, gpe, sums), (w_edge_in, w_edge_out), **more,
        )

    def node_sum(h, message, act, gout, gpre, **more):
        return weight_sum(
            node_weights_kernel, node_order,
            (h, message, act, gout, gpre), (w_node_in, w_node_out), **more,
        )

    needed = (Part(slope_n0), Part(normed_n0), Part(inverse_n0), Part(slope0), Part(normed0))
    edge1, near = edge_sum(e1, h1, halo1, act1, gedge1, gpe1, sums1)
    node1, near = node_sum(
        h1, message1, act_n1, gout1, gpre1, fetch=needed + (Part(inverse0), Part(ge))
    )
    both1 = [edge1, node1]
    (edge1_x,) = add([[edge1]])
    take([edge1], flip(edge1_x, "dp", 2))
    (node1_y,) = add([[node1]], after=(back,))
    take([node1], flip(node1_y, "mesh", 1))
    gout0, gpre0, gh, more, own, halo_out, ge, gedge0, gpe0, sums0, e0_near, act0, h0_near = call(
        functools.partial(first_backward_kernel, chunk),
        (gh, more, own, back, send_rows, near[0], near[1], near[2], wet)
        + (near[6], spread, live, near[3], near[4], near[5], source1_w, *near_w),
        [(small, BF16)] * 2 + backward_outs + [far(large, BF16)] + backward_tail,
        after=(edge1_x, node1_y),
        fetch=(Part(e0), Part(act0), Part(h0)),
    )
    edge0, _ = edge_sum(e0_near, h0_near, halo0, act0, gedge0, gpe0, sums0)
    node0, _ = node_sum(
        h0_near, Part(message0), Part(act_n0), gout0, gpre0, after=(edge1.held[-1][0], node1.held[-1][0])
    )
    both0 = [edge0, node0]
    edge1_y, edge0_x = add([[edge1], [edge0]])
    take([edge1], flip(edge1_y, "mesh", 1))
    take([edge0], flip(edge0_x, "dp", 2))
    joint = lax.axis_size("mesh") == 2 and sent <= node0.rows
    node1_x, node0_y = add(
        [[node1], [node0]], after=(edge0_x,), tail=halo_out if joint else None
    )
    take([node1], flip(node1_x, "dp", 2))
    arrived = flip(node0_y, "mesh", 1)
    take([node0], arrived)
    if joint:
        back = Part(arrived, (arrived.shape[0] - 1, pl.ds(0, sent)), thin, pin=False)
    else:
        back = trade(halo_out, back=True)
    bits = bits_of("dp")[2:]
    edge0_y, node0_x, near1 = add([[edge0], [node0], both1])
    take([node0], flip(node0_x, "dp", 2))
    take([edge0], flip(edge0_y, "mesh", 1))
    take(both1, flip(near1, "dp", bits[0]))
    (gh,) = call(
        last_kernel, (gh, more, own, back, send_rows, source[0]), [far(small, F32)],
        after=(edge0_y,),
    )
    done = (gh,)
    for at, bit in enumerate(bits):
        near0, near1 = add([both0, both1], after=done)
        take(both0, flip(near0, "dp", bit))
        if at + 1 < len(bits):
            take(both1, flip(near1, "dp", bits[at + 1]))
        done = ()
    mine1, other1 = gather(near1)
    (near0,) = add([both0])
    mine0, other0 = gather(near0)
    grads = call(
        functools.partial(output_kernel, factor, [one.rows for one in both0]),
        (mine0, other0, mine1, other1),
        [far((2, w.shape[1] // shards, width), F32) for w in weights],
        smem=(me,),
    )
    return (
        gh.reshape(samples, nodes, width),
        ge.reshape(samples, nodes, slots, width),
        *grads,
    )


def solution(mesh):
    placed = (
        P("dp", "mesh", None),
        P("dp", "mesh", None, None),
        P("dp", "mesh", None),
        P("dp", "mesh", None, None),
        P(),
        P(),
        P(),
        P(),
        P("mesh", None),
        P("mesh", None),
        P("mesh"),
        P("mesh"),
    )
    return jax.shard_map(
        body,
        mesh=mesh,
        in_specs=placed,
        out_specs=(
            P("dp", "mesh", None),
            P("dp", "mesh", None, None),
            P(None, "dp", None),
            P(None, "dp", None),
            P(None, "dp", None),
            P(None, "dp", None),
        ),
        check_vma=False,
    )
```

time: 125 us -> 110 us (0.88)
  Pallas kernels: 28 us -> 49.1 us
  local copies, waits for them, and re-layouts: 14.6 us -> 0.91 us
  other arithmetic: 8.07 us -> 0.07 us
  waiting for transfers between devices: 41.3 us -> 33.4 us
  starting transfers between devices: 31.3 us -> 24.9 us
    pallas_call x8 -> x20, Pallas kernels: 28 us -> 49.1 us  [call(): pl.pallas_call(run, in_specs=[pl.BlockSpec(memory_space=pltpu.SMEM)] * le...]
    unnamed x59 -> x4, local copies, waits for them, and re-layouts: 12.3 us -> 0.91 us
    ppermute x20 -> x18, starting transfers between devices: 25.5 us -> 19.2 us  [flip(): lax.ppermute(values, axis, [(i, i ^ bit) for i in range(lax.axis_size(axi...]
    ppermute x4 -> x3, waiting for transfers between devices: 8.46 us -> 2.67 us  [trade(): return lax.ppermute(rows, 'mesh', [(0, 1), (1, 0)])]
    convert_element_type x16 -> x0, other arithmetic: 5.1 us -> none  [the longest x12 3.9 us: scatter_sum(): held.append(flip(total(slots, 2 * slots).astype(BF16), 'dp', bit))]
    mul x4 -> x0, other arithmetic: 2.85 us -> none  [joined(): return jnp.stack([first[start:stop], last[start:stop]]) * factor]
    ppermute x20 -> x18, waiting for transfers between devices: 32.9 us -> 30.7 us  [flip(): lax.ppermute(values, axis, [(i, i ^ bit) for i in range(lax.axis_size(axi...]
    reshape x2 -> x0, local copies, waits for them, and re-layouts: 1.49 us -> none  [the longest x1 0.74 us: body(): ocean = ocean_mask.reshape(nodes, 1)]
  transfers between devices with their start and end apart: 24 -> 21, of which waited for: 15 -> 11; matrix products, arithmetic and copies ran while one was open for 7% -> 0% of each run, Pallas kernels for 9% -> 24%
where the time goes in v2:
time: 110 us; the launch traced here: 109 us
  Pallas kernels  49.1 us (45%)
  waiting for transfers between devices  33.4 us (30%)
  starting transfers between devices  24.9 us (23%)
    pallas_call x20, Pallas kernels, call(): pl.pallas_call(run, in_specs=[pl.BlockSpec(memory_space=pltpu.SMEM)] * le...  49.1 us
    ppermute x18, waiting for transfers between devices, flip(): lax.ppermute(values, axis, [(i, i ^ bit) for i in range(lax.axis_size(axi...  30.7 us
    ppermute x18, starting transfers between devices, flip(): lax.ppermute(values, axis, [(i, i ^ bit) for i in range(lax.axis_size(axi...  19.2 us
    ppermute x3, starting transfers between devices, trade(): return lax.ppermute(rows, 'mesh', [(0, 1), (1, 0)])  5.75 us
    ppermute x3, waiting for transfers between devices, trade(): return lax.ppermute(rows, 'mesh', [(0, 1), (1, 0)])  2.67 us
  transfers between devices with their start and end apart: 21, of which 11 were waited for; matrix products, arithmetic and copies ran while one was open for 0% of the time, Pallas kernels for 24%

profile of v2, /device:TPU:0, one launch (start us, length us, event | category | flops | bytes accessed | tf_op | source)
XLA Modules:
  0.0 109.4 jit_solution(4952339090259230834)
XLA Ops:
  1.7 3.0 %collective-permute-start = (bf16[32,512]{1,0:T(8,128)(2,1)S(1)}, bf16[32,512]{1,0:T(8,128)(2,1)S(1)}, u32[]{:S(2)}, u32[]{:S(2)}) collective-permute-start(bf16[32,512]{1,0:T(8,128)(2,1)S(1)} %shard_map.164), channel_id=1, source_target_pairs={{0,1},{1,0},{2,3},{3,2},{4,5},{5,4},{6,7},{7,6},{8,9},{9,8},{10,11... | collective-permute-start | bytes 98312 | tf_op jit(solution)/shard_map/ppermute | solution.py:453
  4.7 2.5 %shard_map.163 = (bf16[512,160]{1,0:T(8,128)(2,1)S(1)}, bf16[512,64]{1,0:T(8,128)(2,1)S(1)}, f32[512,1]{1,0:T(8,128)S(1)}, f32[64,1]{1,0:T(8,128)S(1)}, f32[512,...) custom-call(s32[8,64]{1,0:T(8,128)} %bitcast.27, ...), custom_call_target="tpu_custom_call" | custom-call | tf_op jit(solution)/shard_map/pallas_call | solution.py:124
  7.3 4.7 %shard_map.165 = (bf16[512,512]{1,0:T(8,128)(2,1)}, bf16[512,512]{1,0:T(8,128)(2,1)}, bf16[512,512]{1,0:T(8,128)(2,1)}, f32[512,1]{1,0:T(8,128)}, bf16[512,512]{...) custom-call(f32[512,512]{1,0:T(8,128)S(1)} %get-tuple-element.99.ref, ...), custom_call_target="tpu_custom_call" | custom-call | tf_op jit(solution)/shard_map/pallas_call | solution.py:124
  13.4 2.4 %shard_map.166 = (f32[512,512]{1,0:T(8,128)S(1)}, bf16[512,512]{1,0:T(8,128)(2,1)S(1)}, bf16[1024,512]{1,0:T(8,128)(2,1)S(1)}, bf16[512,512]{1,0:T(8,128)(2,1)S(...) custom-call(bf16[64,512]{1,0:T(8,128)(2,1)S(1)} %get-tuple-element.110.refs_0_.refs_2_.refs_1_, ...), custom_call_target="tpu_custom_call" | custom-call | tf_op jit(solution)/shard_map/pallas_call | solution.py:124
  15.9 6.6 %shard_map.167 = (bf16[512,512]{1,0:T(8,128)(2,1)S(1)}, bf16[64,512]{1,0:T(8,128)(2,1)S(1)}, bf16[64,512]{1,0:T(8,128)(2,1)S(1)}, bf16[64,512]{1,0:T(8,128)(2,1)...) custom-call(f32[512,512]{1,0:T(8,128)S(1)} %get-tuple-element.114.re, ...), custom_call_target="tpu_custom_call" | custom-call | tf_op jit(solution)/shard_map/pallas_call | solution.py:124
  22.5 2.6 %shard_map.169 = (bf16[16,64,512]{2,1,0:T(8,128)(2,1)}, bf16[16,64,512]{2,1,0:T(8,128)(2,1)S(1)}) custom-call(s32[2]{0:T(128)S(1)} %pad_add_fusion.refs_0_, bf16[512,512]{1,0:T(8,128)(2,1)S(1)} %get-tuple-element.111.refs_2_.refs_1_, bf16[64,512]{1,0:T(8,128)(2,1)S(1)} %get-tuple-element.110.refs_0_.refs_2_.refs_1_, ...), custom_call_target="tpu_custom_call" | custom-call | tf_op jit(solution)/shard_map/pallas_call | solution.py:124
  25.2 3.2 %shard_map.168 = (bf16[16,48,512]{2,1,0:T(8,128)(2,1)}, bf16[16,48,512]{2,1,0:T(8,128)(2,1)S(1)}, bf16[64,512]{1,0:T(8,128)(2,1)S(1)}, bf16[64,512]{1,0:T(8,128)...) custom-call(s32[2]{0:T(128)S(1)} %pad_add_fusion.refs_0_, ...), custom_call_target="tpu_custom_call" | custom-call | tf_op jit(solution)/shard_map/pallas_call | solution.py:124
  33.0 2.6 %collective-permute-done.2.refs_2_.refs_3_ = bf16[32,512]{1,0:T(8,128)(2,1)S(1)} collective-permute-done((bf16[32,512]{1,0:T(8,128)(2,1)S(1)}, bf16[32,512]{1,0:T(8,128)(2,1)S(1)}, u32[]{:S(2)}, u32[]{:S(2)}) %collective-permute-start.2) | collective-permute-done | bytes 32800 | tf_op jit(solution)/shard_map/ppermute | solution.py:453
  38.2 3.7 %shard_map.172 = (bf16[64,512]{1,0:T(8,128)(2,1)S(1)}, bf16[64,512]{1,0:T(8,128)(2,1)S(1)}, f32[64,512]{1,0:T(8,128)S(1)}, f32[64,512]{1,0:T(8,128)S(1)}, f32[64...) custom-call(f32[64,512]{1,0:T(8,128)S(1)} %get-tuple-element.122.ref, ...), custom_call_target="tpu_custom_call" | custom-call | tf_op jit(solution)/shard_map/pallas_call | solution.py:124
  41.8 2.6 %shard_map.174 = (bf16[16,64,512]{2,1,0:T(8,128)(2,1)}, bf16[16,64,512]{2,1,0:T(8,128)(2,1)S(1)}) custom-call(s32[2]{0:T(128)S(1)} %pad_add_fusion.refs_0_, bf16[512,512]{1,0:T(8,128)(2,1)S(1)} %get-tuple-element.169.refs_1_, bf16[64,512]{1,0:T(8,128)(2,1)S(1)} %get-tuple-element.161.refs_1_.refs_2_, bf16[32,512]{1,0:T(8,128)(2,1)S(1)} %collective-permute-done.refs_3_, ...), custom_call_target="tpu_custom_call" | custom-call | tf_op jit(solution)/shard_map/pallas_call | solution.py:124
  44.5 2.2 %collective-permute-done.5.refs_7_.refs_2_.refs_12_.refs_15_.refs_18_ = bf16[8,48,512]{2,1,0:T(8,128)(2,1)S(1)} collective-permute-done((bf16[8,48,512]{2,1,0:T(8,128)(2,1)S(1)}, bf16[8,48,512]{2,1,0:T(8,128)(2,1)S(1)}, u32[]{:S(2)}, u32[]{:S(2)}) %collective-permute-start.5) | collective-permute-done | bytes 393248 | tf_op jit(solution)/shard_map/ppermute | solution.py:464
  46.7 3.0 %shard_map.173 = (bf16[16,48,512]{2,1,0:T(8,128)(2,1)}, bf16[16,48,512]{2,1,0:T(8,128)(2,1)S(1)}) custom-call(s32[2]{0:T(128)S(1)} %pad_add_fusion.refs_0_, bf16[64,512]{1,0:T(8,128)(2,1)S(1)} %get-tuple-element.161.refs_1_.refs_2_, bf16[64,512]{1,0:T(8,128)(2,1)} %get-tuple-element.162.refs_2_, bf16[64,512]{1,0:T(8,128)(2,1)} %get-tuple-element.163.refs_3_, ...), custom_call_target="tpu_custom_call" | custom-call | tf_op jit(solution)/shard_map/pallas_call | solution.py:124
  52.1 1.7 %shard_map.176 = (bf16[4,48,512]{2,1,0:T(8,128)(2,1)S(1)}, bf16[9,48,512]{2,1,0:T(8,128)(2,1)S(1)}) custom-call(bf16[16,48,512]{2,1,0:T(8,128)(2,1)} %get-tuple-element.156.refs_0_.refs_10_.refs_13_.refs_16_, bf16[16,48,512]{2,1,0:T(8,128)(2,1)S(1)} %collective-permute-done.4.refs_1_.refs_11_.refs_14_.refs_17_, ...), custom_call_target="tpu_custom_call" | custom-call | tf_op jit(solution)/shard_map/pallas_call | solution.py:124
  57.0 14.6 %collective-permute-done.11.refs_9_.refs_11_.refs_13_ = bf16[4,64,512]{2,1,0:T(8,128)(2,1)S(1)} collective-permute-done((bf16[4,64,512]{2,1,0:T(8,128)(2,1)S(1)}, bf16[4,64,512]{2,1,0:T(8,128)(2,1)S(1)}, u32[]{:S(2)}, u32[]{:S(2)}) %collective-permute-start.11) | collective-permute-done | bytes 262176 | tf_op jit(solution)/shard_map/ppermute | solution.py:464
  71.7 2.2 %shard_map.177 = (bf16[4,64,512]{2,1,0:T(8,128)(2,1)S(1)}, bf16[4,48,512]{2,1,0:T(8,128)(2,1)S(1)}, bf16[2,112,512]{2,1,0:T(8,128)(2,1)S(1)}) custom-call(bf16[16,64,512]{2,1,0:T(8,128)(2,1)} %get-tuple-element.174.refs_3_.refs_0_, bf16[16,64,512]{2,1,0:T(8,128)(2,1)S(1)} %collective-permute-done.8.refs_4_.refs_1_, ...), custom_call_target="tpu_custom_call" | custom-call | tf_op jit(solution)/shard_map/pallas_call | solution.py:124
  78.1 2.0 %shard_map.178.refs_18_ = f32[64,512]{1,0:T(8,128)} custom-call(f32[64,512]{1,0:T(8,128)S(1)} %get-tuple-element.158.refs_0_, f32[64,512]{1,0:T(8,128)S(1)} %get-tuple-element.159.refs_1_, f32[64,512]{1,0:T(8,128)S(1)} %get-tuple-element.160.refs_2_, bf16[9,48,512]{2,1,0:T(8,128)(2,1)S(1)} %collective-permute-done.9.refs_5_.refs_3_.refs_6_.refs_7_.refs_8_, ...), custom_call_target="tpu_custom_call" | custom-call | tf_op jit(solution)/shard_map/pallas_call | solution.py:124
  80.1 2.4 %collective-permute-done.14.refs_7_.refs_8_.refs_9_ = bf16[4,48,512]{2,1,0:T(8,128)(2,1)S(1)} collective-permute-done((bf16[4,48,512]{2,1,0:T(8,128)(2,1)S(1)}, bf16[4,48,512]{2,1,0:T(8,128)(2,1)S(1)}, u32[]{:S(2)}, u32[]{:S(2)}) %collective-permute-start.14) | collective-permute-done | bytes 196640 | tf_op jit(solution)/shard_map/ppermute | solution.py:464
  83.4 2.3 %shard_map.179 = (bf16[2,112,512]{2,1,0:T(8,128)(2,1)S(1)}, bf16[1,112,512]{2,1,0:T(8,128)(2,1)S(1)}) custom-call(bf16[16,64,512]{2,1,0:T(8,128)(2,1)} %get-tuple-element.174.refs_3_.refs_0_, bf16[16,64,512]{2,1,0:T(8,128)(2,1)S(1)} %collective-permute-done.8.refs_4_.refs_1_, bf16[8,64,512]{2,1,0:T(8,128)(2,1)S(1)} %collective-permute-done.10.refs_2_, ...), custom_call_target="tpu_custom_call" | custom-call | tf_op jit(solution)/shard_map/pallas_call | solution.py:124
  86.6 2.6 %collective-permute-start.17 = (bf16[1,112,512]{2,1,0:T(8,128)(2,1)S(1)}, bf16[1,112,512]{2,1,0:T(8,128)(2,1)S(1)}, u32[]{:S(2)}, u32[]{:S(2)}) collective-permute-start(bf16[1,112,512]{2,1,0:T(8,128)(2,1)S(1)} %get-tuple-element.185), channel_id=1, source_target_pairs={{0,16},{2,18},{4,20},{6,22},{8,24},{10,26},{12,28},{14,30},{16,0},... | collective-permute-start | bytes 344072 | tf_op jit(solution)/shard_map/ppermute | solution.py:464
  89.2 4.1 %collective-permute-done.17.refs_15_.refs_21_ = bf16[1,112,512]{2,1,0:T(8,128)(2,1)S(1)} collective-permute-done((bf16[1,112,512]{2,1,0:T(8,128)(2,1)S(1)}, bf16[1,112,512]{2,1,0:T(8,128)(2,1)S(1)}, u32[]{:S(2)}, u32[]{:S(2)}) %collective-permute-start.17) | collective-permute-done | bytes 114720 | tf_op jit(solution)/shard_map/ppermute | solution.py:464
  93.6 2.1 %shard_map.180 = (bf16[1,112,512]{2,1,0:T(8,128)(2,1)S(1)}, bf16[1,112,512]{2,1,0:T(8,128)(2,1)S(1)}) custom-call(bf16[16,64,512]{2,1,0:T(8,128)(2,1)} %get-tuple-element.174.refs_3_.refs_0_, bf16[16,64,512]{2,1,0:T(8,128)(2,1)S(1)} %collective-permute-done.8.refs_4_.refs_1_, bf16[8,64,512]{2,1,0:T(8,128)(2,1)S(1)} %collective-permute-done.10.refs_2_, ...), custom_call_target="tpu_custom_call" | custom-call | tf_op jit(solution)/shard_map/pallas_call | solution.py:124
  95.8 2.2 %collective-permute-start.18 = (bf16[1,112,512]{2,1,0:T(8,128)(2,1)S(1)}, bf16[1,112,512]{2,1,0:T(8,128)(2,1)S(1)}, u32[]{:S(2)}, u32[]{:S(2)}) collective-permute-start(bf16[1,112,512]{2,1,0:T(8,128)(2,1)S(1)} %get-tuple-element.186), channel_id=1, source_target_pairs={{0,16},{2,18},{4,20},{6,22},{8,24},{10,26},{12,28},{14,30},{16,0},... | collective-permute-start | bytes 344072 | tf_op jit(solution)/shard_map/ppermute | solution.py:464
  99.1 2.4 %collective-permute-done.18.refs_5_.refs_11_ = bf16[1,112,512]{2,1,0:T(8,128)(2,1)S(1)} collective-permute-done((bf16[1,112,512]{2,1,0:T(8,128)(2,1)S(1)}, bf16[1,112,512]{2,1,0:T(8,128)(2,1)S(1)}, u32[]{:S(2)}, u32[]{:S(2)}) %collective-permute-start.18) | collective-permute-done | bytes 114720 | tf_op jit(solution)/shard_map/ppermute | solution.py:464
  103.8 3.9 %collective-permute-done.19.refs_2_ = bf16[112,512]{1,0:T(8,128)(2,1)S(1)} collective-permute-done((bf16[112,512]{1,0:T(8,128)(2,1)S(1)}, bf16[112,512]{1,0:T(8,128)(2,1)S(1)}, u32[]{:S(2)}, u32[]{:S(2)}) %collective-permute-start.19) | collective-permute-done | bytes 114720 | tf_op jit(solution)/shard_map/ppermute | solution.py:464
  (43 shorter events, 26.9 us)
Async XLA Ops:
  1.7 5.6 %collective-permute-start = (bf16[32,512]{1,0:T(8,128)(2,1)S(1)}, bf16[32,512]{1,0:T(8,128)(2,1)S(1)}, u32[]{:S(2)}, u32[]{:S(2)}) collective-permute-start(bf16[32,512]{1,0:T(8,128)(2,1)S(1)} %shard_map.164), channel_id=1, source_target_pairs={{0,1},{1,0},{2,3},{3,2},{4,5},{5,4},{6,7},{7,6},{8,9},{9,8},{10,11... | collective-permute-start | bytes 98312 | tf_op jit(solution)/shard_map/ppermute | solution.py:453
  4.7 2.6 %copy-start.1 = (s32[1,32]{1,0:T(1,128)S(1)}, s32[1,32]{1,0:T(1,128)}, u32[]{:S(2)}) copy-start(s32[1,32]{1,0:T(1,128)} %refs_4_.3) | copy-start | bytes 388
  12.0 4.0 %collective-permute-start.1 = (bf16[32,512]{1,0:T(8,128)(2,1)S(1)}, bf16[32,512]{1,0:T(8,128)(2,1)S(1)}, u32[]{:S(2)}, u32[]{:S(2)}) collective-permute-start(bf16[32,512]{1,0:T(8,128)(2,1)S(1)} %get-tuple-element.115), channel_id=1, source_target_pairs={{0,1},{1,0},{2,3},{3,2},{4,5},{5,4},{6,7},{7,6},{8,9},{9,8},{10,11... | collective-permute-start | bytes 98312 | tf_op jit(solution)/shard_map/ppermute | solution.py:453
  25.1 3.8 %collective-permute-start.3 = (bf16[16,64,512]{2,1,0:T(8,128)(2,1)S(1)}, bf16[16,64,512]{2,1,0:T(8,128)(2,1)S(1)}, u32[]{:S(2)}, u32[]{:S(2)}) collective-permute-start(bf16[16,64,512]{2,1,0:T(8,128)(2,1)S(1)} %get-tuple-element.155), channel_id=1, source_target_pairs={{0,2},{2,0},{4,6},{6,4},{8,10},{10,8},{12,14},{14,12},{16,18},{18,... | collective-permute-start | bytes 3145736 | tf_op jit(solution)/shard_map/ppermute | solution.py:464
  28.4 7.2 %collective-permute-start.4 = (bf16[16,48,512]{2,1,0:T(8,128)(2,1)S(1)}, bf16[16,48,512]{2,1,0:T(8,128)(2,1)S(1)}, u32[]{:S(2)}, u32[]{:S(2)}) collective-permute-start(bf16[16,48,512]{2,1,0:T(8,128)(2,1)S(1)} %get-tuple-element.157), channel_id=1, source_target_pairs={{0,2},{2,0},{4,6},{6,4},{8,10},{10,8},{12,14},{14,12},{16,18},{18,... | collective-permute-start | bytes 2359304 | tf_op jit(solution)/shard_map/ppermute | solution.py:464
  30.1 16.6 %collective-permute-start.6 = (bf16[8,64,512]{2,1,0:T(8,128)(2,1)S(1)}, bf16[8,64,512]{2,1,0:T(8,128)(2,1)S(1)}, u32[]{:S(2)}, u32[]{:S(2)}) collective-permute-start(bf16[8,64,512]{2,1,0:T(8,128)(2,1)S(1)} %shard_map.170.refs_24_), channel_id=1, source_target_pairs={{0,4},{2,6},{4,0},{6,2},{8,12},{10,14},{12,8},{14,10},{16,20},{18,... | collective-permute-start | bytes 1572872 | tf_op jit(solution)/shard_map/ppermute | solution.py:464
  31.7 3.9 %collective-permute-start.2 = (bf16[32,512]{1,0:T(8,128)(2,1)S(1)}, bf16[32,512]{1,0:T(8,128)(2,1)S(1)}, u32[]{:S(2)}, u32[]{:S(2)}) collective-permute-start(bf16[32,512]{1,0:T(8,128)(2,1)S(1)} %get-tuple-element.125), channel_id=1, source_target_pairs={{0,1},{1,0},{2,3},{3,2},{4,5},{5,4},{6,7},{7,6},{8,9},{9,8},{10,11... | collective-permute-start | bytes 98312 | tf_op jit(solution)/shard_map/ppermute | solution.py:453
  36.8 10.0 %collective-permute-start.5 = (bf16[8,48,512]{2,1,0:T(8,128)(2,1)S(1)}, bf16[8,48,512]{2,1,0:T(8,128)(2,1)S(1)}, u32[]{:S(2)}, u32[]{:S(2)}) collective-permute-start(bf16[8,48,512]{2,1,0:T(8,128)(2,1)S(1)} %shard_map.171.refs_25_), channel_id=1, source_target_pairs={{0,1},{1,0},{2,3},{3,2},{4,5},{5,4},{6,7},{7,6},{8,9},{9,8},{10,11... | collective-permute-start | bytes 1179656 | tf_op jit(solution)/shard_map/ppermute | solution.py:464
  44.4 5.4 %collective-permute-start.8 = (bf16[16,64,512]{2,1,0:T(8,128)(2,1)S(1)}, bf16[16,64,512]{2,1,0:T(8,128)(2,1)S(1)}, u32[]{:S(2)}, u32[]{:S(2)}) collective-permute-start(bf16[16,64,512]{2,1,0:T(8,128)(2,1)S(1)} %get-tuple-element.175), channel_id=1, source_target_pairs={{0,2},{2,0},{4,6},{6,4},{8,10},{10,8},{12,14},{14,12},{16,18},{18,... | collective-permute-start | bytes 3145736 | tf_op jit(solution)/shard_map/ppermute | solution.py:464
  49.8 2.4 %collective-permute-start.7 = (bf16[16,48,512]{2,1,0:T(8,128)(2,1)S(1)}, bf16[16,48,512]{2,1,0:T(8,128)(2,1)S(1)}, u32[]{:S(2)}, u32[]{:S(2)}) collective-permute-start(bf16[16,48,512]{2,1,0:T(8,128)(2,1)S(1)} %get-tuple-element.167), channel_id=1, source_target_pairs={{0,2},{2,0},{4,6},{6,4},{8,10},{10,8},{12,14},{14,12},{16,18},{18,... | collective-permute-start | bytes 2359304 | tf_op jit(solution)/shard_map/ppermute | solution.py:464
  51.2 20.5 %collective-permute-start.10 = (bf16[8,64,512]{2,1,0:T(8,128)(2,1)S(1)}, bf16[8,64,512]{2,1,0:T(8,128)(2,1)S(1)}, u32[]{:S(2)}, u32[]{:S(2)}) collective-permute-start(bf16[8,64,512]{2,1,0:T(8,128)(2,1)S(1)} %get-tuple-element.176.refs_6_), channel_id=1, source_target_pairs={{0,4},{2,6},{4,0},{6,2},{8,12},{10,14},{12,8},{14,10},{16,20},{18,... | collective-permute-start | bytes 1572872 | tf_op jit(solution)/shard_map/ppermute | solution.py:464
  53.8 17.9 %collective-permute-start.9 = (bf16[9,48,512]{2,1,0:T(8,128)(2,1)S(1)}, bf16[9,48,512]{2,1,0:T(8,128)(2,1)S(1)}, u32[]{:S(2)}, u32[]{:S(2)}) collective-permute-start(bf16[9,48,512]{2,1,0:T(8,128)(2,1)S(1)} %get-tuple-element.177), channel_id=1, source_target_pairs={{0,1},{1,0},{2,3},{3,2},{4,5},{5,4},{6,7},{7,6},{8,9},{9,8},{10,11... | collective-permute-start | bytes 1327112 | tf_op jit(solution)/shard_map/ppermute | solution.py:464
  55.2 16.5 %collective-permute-start.11 = (bf16[4,64,512]{2,1,0:T(8,128)(2,1)S(1)}, bf16[4,64,512]{2,1,0:T(8,128)(2,1)S(1)}, u32[]{:S(2)}, u32[]{:S(2)}) collective-permute-start(bf16[4,64,512]{2,1,0:T(8,128)(2,1)S(1)} %get-tuple-element.178), channel_id=1, source_target_pairs={{0,1},{1,0},{2,3},{3,2},{4,5},{5,4},{6,7},{7,6},{8,9},{9,8},{10,11... | collective-permute-start | bytes 786440 | tf_op jit(solution)/shard_map/ppermute | solution.py:464
  55.9 15.8 %collective-permute-start.12 = (bf16[4,48,512]{2,1,0:T(8,128)(2,1)S(1)}, bf16[4,48,512]{2,1,0:T(8,128)(2,1)S(1)}, u32[]{:S(2)}, u32[]{:S(2)}) collective-permute-start(bf16[4,48,512]{2,1,0:T(8,128)(2,1)S(1)} %get-tuple-element.179), channel_id=1, source_target_pairs={{0,4},{2,6},{4,0},{6,2},{8,12},{10,14},{12,8},{14,10},{16,20},{18,... | collective-permute-start | bytes 589832 | tf_op jit(solution)/shard_map/ppermute | solution.py:464
  73.8 8.6 %collective-permute-start.13 = (bf16[4,64,512]{2,1,0:T(8,128)(2,1)S(1)}, bf16[4,64,512]{2,1,0:T(8,128)(2,1)S(1)}, u32[]{:S(2)}, u32[]{:S(2)}) collective-permute-start(bf16[4,64,512]{2,1,0:T(8,128)(2,1)S(1)} %get-tuple-element.180.refs_6_), channel_id=1, source_target_pairs={{0,1},{1,0},{2,3},{3,2},{4,5},{5,4},{6,7},{7,6},{8,9},{9,8},{10,11... | collective-permute-start | bytes 786440 | tf_op jit(solution)/shard_map/ppermute | solution.py:464
  75.2 7.2 %collective-permute-start.15 = (bf16[2,112,512]{2,1,0:T(8,128)(2,1)S(1)}, bf16[2,112,512]{2,1,0:T(8,128)(2,1)S(1)}, u32[]{:S(2)}, u32[]{:S(2)}) collective-permute-start(bf16[2,112,512]{2,1,0:T(8,128)(2,1)S(1)} %get-tuple-element.183), channel_id=1, source_target_pairs={{0,8},{2,10},{4,12},{6,14},{8,0},{10,2},{12,4},{14,6},{16,24},{18,... | collective-permute-start | bytes 688136 | tf_op jit(solution)/shard_map/ppermute | solution.py:464
  76.8 5.7 %collective-permute-start.14 = (bf16[4,48,512]{2,1,0:T(8,128)(2,1)S(1)}, bf16[4,48,512]{2,1,0:T(8,128)(2,1)S(1)}, u32[]{:S(2)}, u32[]{:S(2)}) collective-permute-start(bf16[4,48,512]{2,1,0:T(8,128)(2,1)S(1)} %get-tuple-element.182), channel_id=1, source_target_pairs={{0,4},{2,6},{4,0},{6,2},{8,12},{10,14},{12,8},{14,10},{16,20},{18,... | collective-permute-start | bytes 589832 | tf_op jit(solution)/shard_map/ppermute | solution.py:464
  82.5 0.9 copy-start
  85.7 7.9 %collective-permute-start.16 = (bf16[2,112,512]{2,1,0:T(8,128)(2,1)S(1)}, bf16[2,112,512]{2,1,0:T(8,128)(2,1)S(1)}, u32[]{:S(2)}, u32[]{:S(2)}) collective-permute-start(bf16[2,112,512]{2,1,0:T(8,128)(2,1)S(1)} %get-tuple-element.184), channel_id=1, source_target_pairs={{0,8},{2,10},{4,12},{6,14},{8,0},{10,2},{12,4},{14,6},{16,24},{18,... | collective-permute-start | bytes 688136 | tf_op jit(solution)/shard_map/ppermute | solution.py:464
  86.6 6.7 %collective-permute-start.17 = (bf16[1,112,512]{2,1,0:T(8,128)(2,1)S(1)}, bf16[1,112,512]{2,1,0:T(8,128)(2,1)S(1)}, u32[]{:S(2)}, u32[]{:S(2)}) collective-permute-start(bf16[1,112,512]{2,1,0:T(8,128)(2,1)S(1)} %get-tuple-element.185), channel_id=1, source_target_pairs={{0,16},{2,18},{4,20},{6,22},{8,24},{10,26},{12,28},{14,30},{16,0},... | collective-permute-start | bytes 344072 | tf_op jit(solution)/shard_map/ppermute | solution.py:464
  95.8 5.8 %collective-permute-start.18 = (bf16[1,112,512]{2,1,0:T(8,128)(2,1)S(1)}, bf16[1,112,512]{2,1,0:T(8,128)(2,1)S(1)}, u32[]{:S(2)}, u32[]{:S(2)}) collective-permute-start(bf16[1,112,512]{2,1,0:T(8,128)(2,1)S(1)} %get-tuple-element.186), channel_id=1, source_target_pairs={{0,16},{2,18},{4,20},{6,22},{8,24},{10,26},{12,28},{14,30},{16,0},... | collective-permute-start | bytes 344072 | tf_op jit(solution)/shard_map/ppermute | solution.py:464
  97.9 5.9 %collective-permute-start.20 = (bf16[112,512]{1,0:T(8,128)(2,1)S(1)}, bf16[112,512]{1,0:T(8,128)(2,1)S(1)}, u32[]{:S(2)}, u32[]{:S(2)}) collective-permute-start(bf16[112,512]{1,0:T(8,128)(2,1)S(1)} %bitcast.16), channel_id=1, source_target_pairs={{0,1},{1,0},{2,3},{3,2},{4,5},{5,4},{6,7},{7,6},{8,9},{9,8},{10,11... | collective-permute-start | bytes 344072 | tf_op jit(solution)/shard_map/ppermute | solution.py:464
  102.9 4.9 %collective-permute-start.19 = (bf16[112,512]{1,0:T(8,128)(2,1)S(1)}, bf16[112,512]{1,0:T(8,128)(2,1)S(1)}, u32[]{:S(2)}, u32[]{:S(2)}) collective-permute-start(bf16[112,512]{1,0:T(8,128)(2,1)S(1)} %bitcast.14), channel_id=1, source_target_pairs={{0,1},{1,0},{2,3},{3,2},{4,5},{5,4},{6,7},{7,6},{8,9},{9,8},{10,11... | collective-permute-start | bytes 344072 | tf_op jit(solution)/shard_map/ppermute | solution.py:464

commit v3 on v2

--- a/solution.py
+++ b/solution.py
@@ -396,28 +396,31 @@
 
 def place(order, me_ref, first_ref, second_ref, keep_ref, sent_ref):
     rows = keep_ref.shape[1]
-    count = keep_ref.shape[0]
-    for bits in range(0, count, 2):
-        spots = [order.index((bits, side)) for side in (0, 1)]
+    blocks = sorted({bits for bits, _ in order})
+    sides = len(order) // len(blocks)
+    for bits in blocks:
+        spots = [order.index((bits, side)) for side in range(sides)]
+
+        def spot(half):
+            return jnp.where(me_ref[1] == half, spots[0], spots[1]) if sides == 2 else spots[0]
+
         for bit, out_ref in ((0, keep_ref), (1, sent_ref)):
             device = jnp.bitwise_xor(me_ref[0], bits + bit)
             row = 0
             for ref in (first_ref, second_ref):
-                size = ref.shape[0] // count
+                size = ref.shape[0] // (2 * len(blocks))
                 start = pl.multiple_of(device * size, 16)
                 done = 0
                 while done < size:
                     half, at = divmod(row, rows)
                     step = min(size - done, rows - at)
-                    index = jnp.where(me_ref[1] == half, spots[0], spots[1])
                     piece = ref[pl.ds(pl.multiple_of(start + done, 16), step), :]
-                    out_ref[index, at : at + step, :] = piece.astype(BF16)
+                    out_ref[spot(half), at : at + step, :] = piece.astype(BF16)
                     row += step
                     done += step
-            if row < 2 * rows:
-                index = jnp.where(me_ref[1] == 1, spots[0], spots[1])
-                filler = jnp.zeros((2 * rows - row, keep_ref.shape[2]), BF16)
-                out_ref[index, row - rows :, :] = filler
+            if row < sides * rows:
+                filler = jnp.zeros((sides * rows - row, keep_ref.shape[2]), BF16)
+                out_ref[spot(sides - 1), row - (sides - 1) * rows :, :] = filler
 
 
 def edge_weights_kernel(
@@ -480,71 +483,81 @@
 
 
 class Sum:
-    def __init__(self, keep):
-        self.held = [(keep, 0)]
-        self.slots, self.rows = keep.shape[0], keep.shape[1]
-
-    def parts(self, start, stop):
-        return [
-            Part(
-                array,
-                (pl.ds(start, stop - start), pl.ds(row, self.rows)),
-                (stop - start, self.rows, array.shape[2]),
-                pin=at == 0,
-            )
-            for at, (array, row) in enumerate(self.held)
-        ]
+    def __init__(self, keep, route):
+        self.base, self.arrived, self.row = Part(keep), None, 0
+        self.slots, self.rows, self.width = keep.shape
+        self.route = list(route)
 
 
 def add_kernel(groups, tail, *refs):
     refs = list(refs)
-    count = sum(sum(group) for group in groups) + tail
-    outs = refs[count:]
+    flat = [group for output in groups for group in output]
+    terms, refs = refs[: 2 * len(flat)], refs[2 * len(flat) :]
     if tail:
-        more = refs[count - 1]
+        more, refs = refs[0], refs[1:]
+    outs, kept = refs[: len(groups)], refs[len(groups) :]
+    if tail:
         outs[-1][outs[-1].shape[0] - 1, : more.shape[0], :] = more[...]
-    for group, out in zip(groups, outs):
+    for output, out in zip(groups, outs):
+        at = 0
+        for rows, row, slots in output:
+            base, arrived, terms = terms[0], terms[1], terms[2:]
+            half = slots // 2
+            low, high = (0, 1) if slots == 1 else (half, slots)
+            total = base[low:high].astype(F32) + arrived[low:high, row : row + rows, :].astype(F32)
+            out[: high - low, at : at + rows, :] = total.astype(BF16)
+            at += rows
+            if half:
+                left, kept = kept[0], kept[1:]
+                left[...] = base[:half].astype(F32) + arrived[:half, row : row + rows, :].astype(F32)
+
+
+def add(wanted, after=(), tail=None):
+    operands, groups, outs, kept = [], [], [], []
+    for sums in wanted:
+        group = []
+        for one in sums:
+            operands += [one.base, one.arrived]
+            group.append((one.rows, one.row, one.slots))
+            half = one.slots // 2
+            if half:
+                kept.append((one, ((half, one.rows, one.width), F32)))
+        groups.append(group)
+        outs.append(((max(half, 1), sum(one.rows for one in sums), one.width), BF16))
+    if tail is not None:
+        (count, size, width), dtype = outs[-1]
+        outs[-1] = ((count + 1, size, width), dtype)
+        operands.append(tail)
+    results = call(
+        functools.partial(add_kernel, groups, tail is not None),
+        operands,
+        outs + [shape for _, shape in kept],
+        after=after,
+    )
+    for (one, _), base in zip(kept, results[len(outs) :]):
+        one.base = base
+        one.slots //= 2
+    return results[: len(outs)]
+
+
+def advance(wanted, after=(), tail=None):
+    sent = add(wanted, after, tail)
+    arrived = []
+    for sums, values in zip(wanted, sent):
+        steps = [one.route.pop(0) for one in sums if one.route]
+        if not steps:
+            arrived.append(None)
+            continue
+        other = flip(values, *steps[0])
         row = 0
-        for count in group:
-            terms, refs = refs[:count], refs[count:]
-            rows = terms[0].shape[1]
-            total = sum(term[...].astype(F32) for term in terms)
-            out[: terms[0].shape[0], row : row + rows, :] = total.astype(BF16)
-            row += rows
-        flush(out)
-
-
-def add(wanted, after=(), tail=None):
-    operands, groups, outs = [], [], []
-    for sums in wanted:
-        group, count = [], 0
         for one in sums:
-            if one.slots > 1:
-                one.slots //= 2
-                span = (one.slots, 2 * one.slots)
-            else:
-                span = (0, 1)
-            parts = one.parts(*span)
-            operands += parts
-            group.append(len(parts))
-            count = span[1] - span[0]
-        groups.append(group)
-        outs.append(((count, sum(one.rows for one in sums), parts[0].shape[2]), BF16))
-    if tail is not None:
-        (count, size, depth), dtype = outs[-1]
-        outs[-1] = ((count + 1, size, depth), dtype)
-        operands.append(tail)
-    return call(functools.partial(add_kernel, groups, tail is not None), operands, outs, after=after)
-
-
-def take(sums, values):
-    row = 0
-    for one in sums:
-        one.held.append((values, row))
-        row += one.rows
-
-
-def gather(values):
+            one.arrived, one.row = other, row
+            row += one.rows
+        arrived.append(other)
+    return sent, arrived
+
+
+def across(values):
     mine = values[0]
     for bit in bits_of("mesh")[1:]:
         mine = (mine.astype(F32) + flip(mine, "mesh", bit).astype(F32)).astype(BF16)
@@ -552,20 +565,24 @@
 
 
 def output_kernel(
-    factor, splits, me_ref, mine0_ref, other0_ref, mine1_ref, other1_ref, *outs
+    factor, halves_of, me_ref, mine0_ref, other0_ref, mine1_ref, other1_ref, *outs
 ):
     low = me_ref[1] == 0
-    for layer, (mine, other) in enumerate(((mine0_ref, other0_ref), (mine1_ref, other1_ref))):
-        row = 0
-        for pair, rows in enumerate(splits):
-            a = mine[row : row + rows, :].astype(F32) * factor
-            b = other[row : row + rows, :].astype(F32) * factor
-            both = jnp.concatenate([jnp.where(low, a, b), jnp.where(low, b, a)], axis=0)
-            first, second = outs[2 * pair], outs[2 * pair + 1]
-            cut, end = first.shape[1], first.shape[1] + second.shape[1]
-            first[layer] = both[:cut]
-            second[layer] = both[cut:end]
-            row += rows
+    row0 = row1 = 0
+    for pair, rows in enumerate(halves_of):
+        first, second = outs[2 * pair], outs[2 * pair + 1]
+        cut, end = first.shape[1], first.shape[1] + second.shape[1]
+        a = mine0_ref[row0 : row0 + rows, :].astype(F32) * factor
+        b = other0_ref[row0 : row0 + rows, :].astype(F32) * factor
+        both = jnp.concatenate([jnp.where(low, a, b), jnp.where(low, b, a)], axis=0)
+        first[0] = both[:cut]
+        second[0] = both[cut:end]
+        a = mine1_ref[row1 : row1 + end, :].astype(F32)
+        both = (a + other1_ref[row1 : row1 + end, :].astype(F32)) * factor
+        first[1] = both[:cut]
+        second[1] = both[cut:end]
+        row0 += rows
+        row1 += end
 
 
 def body(
@@ -592,9 +609,9 @@
     total_rows = samples * shards * nodes * lax.axis_size("mesh")
     factor = 1.0 / total_rows**0.5
     beyond = [("dp", bit) for bit in bits_of("dp")[2:]]
-    edge_route = [("dp", 2), ("mesh", 1)] + beyond
-    node_route = [("mesh", 1), ("dp", 2)] + beyond
-    edge_order, node_order = slot_order(edge_route), slot_order(node_route)
+    along = [("dp", 2)]
+    edge_routes = (along + [("mesh", 1)] + beyond, along + beyond)
+    node_routes = ([("mesh", 1)] + along + beyond, beyond + along)
     me = jnp.stack([lax.axis_index("dp"), lax.axis_index("mesh") % 2]).astype(jnp.int32)
 
     h0 = node_feats.reshape(nodes, width)
@@ -653,92 +670,74 @@
     )
     back = trade(halo_out, back=True)
 
-    def weight_sum(kernel, order, operands, kinds, after=(), fetch=()):
+    def weight_sum(kernel, route, operands, kinds, **more):
+        order = slot_order(route)
         size = sum(w.shape[1] // shards for w in kinds)
-        size = -(-size // 32) * 32
+        rows_in = size if ("mesh", 1) not in route else -(-size // 32) * 16
+        shape = (len(order), rows_in, width)
         keep, send, *fetched = call(
             functools.partial(kernel, order),
             operands,
-            [far((shards, size // 2, width), BF16), ((shards, size // 2, width), BF16)],
+            [far(shape, BF16), (shape, BF16)],
             scratch=[VMEM(w.shape[1:], F32) for w in kinds],
             smem=(me,),
-            after=after,
-            fetch=fetch,
+            **more,
         )
-        one = Sum(keep)
-        take([one], flip(send, "dp", 1))
+        one = Sum(keep, route)
+        one.arrived = flip(send, "dp", 1)
         return one, fetched
 
-    def edge_sum(e, h, halo, act, gedge, gpe, sums, **more):
+    def edge_sum(layer, operands, **more):
         return weight_sum(
-            edge_weights_kernel, edge_order,
-            (e, h, halo, act, gedge, gpe, sums), (w_edge_in, w_edge_out), **more,
+            edge_weights_kernel, edge_routes[layer], operands, (w_edge_in, w_edge_out), **more
         )
 
-    def node_sum(h, message, act, gout, gpre, **more):
+    def node_sum(layer, operands, **more):
         return weight_sum(
-            node_weights_kernel, node_order,
-            (h, message, act, gout, gpre), (w_node_in, w_node_out), **more,
+            node_weights_kernel, node_routes[layer], operands, (w_node_in, w_node_out), **more
         )
 
     needed = (Part(slope_n0), Part(normed_n0), Part(inverse_n0), Part(slope0), Part(normed0))
-    edge1, near = edge_sum(e1, h1, halo1, act1, gedge1, gpe1, sums1)
+    edge1, _ = edge_sum(1, (e1, h1, halo1, act1, gedge1, gpe1, sums1))
     node1, near = node_sum(
-        h1, message1, act_n1, gout1, gpre1, fetch=needed + (Part(inverse0), Part(ge))
-    )
-    both1 = [edge1, node1]
-    (edge1_x,) = add([[edge1]])
-    take([edge1], flip(edge1_x, "dp", 2))
-    (node1_y,) = add([[node1]], after=(back,))
-    take([node1], flip(node1_y, "mesh", 1))
+        1, (h1, message1, act_n1, gout1, gpre1), fetch=needed + (Part(inverse0), Part(ge))
+    )
+    first, arrived = advance([[edge1], [node1]])
     gout0, gpre0, gh, more, own, halo_out, ge, gedge0, gpe0, sums0, e0_near, act0, h0_near = call(
         functools.partial(first_backward_kernel, chunk),
         (gh, more, own, back, send_rows, near[0], near[1], near[2], wet)
         + (near[6], spread, live, near[3], near[4], near[5], source1_w, *near_w),
         [(small, BF16)] * 2 + backward_outs + [far(large, BF16)] + backward_tail,
-        after=(edge1_x, node1_y),
+        after=tuple(first),
         fetch=(Part(e0), Part(act0), Part(h0)),
     )
-    edge0, _ = edge_sum(e0_near, h0_near, halo0, act0, gedge0, gpe0, sums0)
+    edge0, _ = edge_sum(0, (e0_near, h0_near, halo0, act0, gedge0, gpe0, sums0))
     node0, _ = node_sum(
-        h0_near, Part(message0), Part(act_n0), gout0, gpre0, after=(edge1.held[-1][0], node1.held[-1][0])
-    )
-    both0 = [edge0, node0]
-    edge1_y, edge0_x = add([[edge1], [edge0]])
-    take([edge1], flip(edge1_y, "mesh", 1))
-    take([edge0], flip(edge0_x, "dp", 2))
+        0, (h0_near, Part(message0), Part(act_n0), gout0, gpre0), after=tuple(arrived)
+    )
     joint = lax.axis_size("mesh") == 2 and sent <= node0.rows
-    node1_x, node0_y = add(
-        [[node1], [node0]], after=(edge0_x,), tail=halo_out if joint else None
-    )
-    take([node1], flip(node1_x, "dp", 2))
-    arrived = flip(node0_y, "mesh", 1)
-    take([node0], arrived)
+    wanted = [[edge0], [edge1], [node1], [node0]]
+    _, arrived = advance(wanted, tail=halo_out if joint else None)
     if joint:
-        back = Part(arrived, (arrived.shape[0] - 1, pl.ds(0, sent)), thin, pin=False)
+        back = Part(arrived[-1], (arrived[-1].shape[0] - 1, pl.ds(0, sent)), thin, pin=False)
     else:
         back = trade(halo_out, back=True)
-    bits = bits_of("dp")[2:]
-    edge0_y, node0_x, near1 = add([[edge0], [node0], both1])
-    take([node0], flip(node0_x, "dp", 2))
-    take([edge0], flip(edge0_y, "mesh", 1))
-    take(both1, flip(near1, "dp", bits[0]))
+    out, _ = advance(wanted)
     (gh,) = call(
-        last_kernel, (gh, more, own, back, send_rows, source[0]), [far(small, F32)],
-        after=(edge0_y,),
+        last_kernel, (gh, more, own, back, send_rows, source[0]), [far(small, F32)], after=(out[0],)
     )
     done = (gh,)
-    for at, bit in enumerate(bits):
-        near0, near1 = add([both0, both1], after=done)
-        take(both0, flip(near0, "dp", bit))
-        if at + 1 < len(bits):
-            take(both1, flip(near1, "dp", bits[at + 1]))
+    while edge1.route:
+        advance([[edge0, node0], [edge1], [node1]], after=done)
         done = ()
-    mine1, other1 = gather(near1)
-    (near0,) = add([both0])
-    mine0, other0 = gather(near0)
+    (_, value1), _ = advance([[edge0, node0], [edge1, node1]], after=done)
+    mine1, other1 = across(value1)
+    while edge0.route:
+        advance([[edge0, node0]])
+    ((value0,), _) = advance([[edge0, node0]])
+    mine0, other0 = across(value0)
     grads = call(
-        functools.partial(output_kernel, factor, [one.rows for one in both0]),
+        functools.partial(output_kernel, factor, (edge0.rows, node0.rows)),
         (mine0, other0, mine1, other1),
         [far((2, w.shape[1] // shards, width), F32) for w in weights],
         smem=(me,),

time: 110 us -> 101 us (0.918)
  Pallas kernels: 49.1 us -> 39.9 us
  starting transfers between devices: 24.9 us -> 27.8 us
  waiting for transfers between devices: 33.4 us -> 30.5 us
    pallas_call x20 -> x18, Pallas kernels: 49.1 us -> 39.9 us  [call(): pl.pallas_call(run, in_specs=[pl.BlockSpec(memory_space=pltpu.SMEM)] * le...]
    ppermute x18, waiting for transfers between devices: 30.7 us -> 27.9 us  [flip(): lax.ppermute(values, axis, [(i, i ^ bit) for i in range(lax.axis_size(axi...]
    ppermute x18, starting transfers between devices: 19.2 us -> 22 us  [flip(): lax.ppermute(values, axis, [(i, i ^ bit) for i in range(lax.axis_size(axi...]
  transfers between devices with their start and end apart: 21 -> 21, of which waited for: 11 -> 13; matrix products, arithmetic and copies ran while one was open for 0% -> 0% of each run, Pallas kernels for 24% -> 20%
where the time goes in v3:
time: 101 us; the launch traced here: 100 us
  Pallas kernels  39.9 us (40%)
  waiting for transfers between devices  30.5 us (30%)
  starting transfers between devices  27.8 us (28%)
    pallas_call x18, Pallas kernels, call(): pl.pallas_call(run, in_specs=[pl.BlockSpec(memory_space=pltpu.SMEM)] * le...  39.9 us
    ppermute x18, waiting for transfers between devices, flip(): lax.ppermute(values, axis, [(i, i ^ bit) for i in range(lax.axis_size(axi...  27.9 us
    ppermute x18, starting transfers between devices, flip(): lax.ppermute(values, axis, [(i, i ^ bit) for i in range(lax.axis_size(axi...  22 us
    ppermute x3, starting transfers between devices, trade(): return lax.ppermute(rows, 'mesh', [(0, 1), (1, 0)])  5.76 us
    ppermute x3, waiting for transfers between devices, trade(): return lax.ppermute(rows, 'mesh', [(0, 1), (1, 0)])  2.66 us
  transfers between devices with their start and end apart: 21, of which 13 were waited for; matrix products, arithmetic and copies ran while one was open for 0% of the time, Pallas kernels for 20%

profile of v3, /device:TPU:0, one launch (start us, length us, event | category | flops | bytes accessed | tf_op | source)
XLA Modules:
  0.0 100.2 jit_solution(11603033489610184298)
XLA Ops:
  1.7 3.0 %collective-permute-start = (bf16[32,512]{1,0:T(8,128)(2,1)S(1)}, bf16[32,512]{1,0:T(8,128)(2,1)S(1)}, u32[]{:S(2)}, u32[]{:S(2)}) collective-permute-start(bf16[32,512]{1,0:T(8,128)(2,1)S(1)} %shard_map.164), channel_id=1, source_target_pairs={{0,1},{1,0},{2,3},{3,2},{4,5},{5,4},{6,7},{7,6},{8,9},{9,8},{10,11... | collective-permute-start | bytes 98312 | tf_op jit(solution)/shard_map/ppermute | solution.py:456
  4.7 2.5 %shard_map.163 = (bf16[512,160]{1,0:T(8,128)(2,1)S(1)}, bf16[512,64]{1,0:T(8,128)(2,1)S(1)}, f32[512,1]{1,0:T(8,128)S(1)}, f32[64,1]{1,0:T(8,128)S(1)}, f32[512,...) custom-call(s32[8,64]{1,0:T(8,128)} %bitcast.27, ...), custom_call_target="tpu_custom_call" | custom-call | tf_op jit(solution)/shard_map/pallas_call | solution.py:124
  7.3 4.7 %shard_map.165 = (bf16[512,512]{1,0:T(8,128)(2,1)}, bf16[512,512]{1,0:T(8,128)(2,1)}, bf16[512,512]{1,0:T(8,128)(2,1)}, f32[512,1]{1,0:T(8,128)}, bf16[512,512]{...) custom-call(f32[512,512]{1,0:T(8,128)S(1)} %get-tuple-element.115.re, ...), custom_call_target="tpu_custom_call" | custom-call | tf_op jit(solution)/shard_map/pallas_call | solution.py:124
  13.4 2.4 %shard_map.166 = (f32[512,512]{1,0:T(8,128)S(1)}, bf16[512,512]{1,0:T(8,128)(2,1)S(1)}, bf16[1024,512]{1,0:T(8,128)(2,1)S(1)}, bf16[512,512]{1,0:T(8,128)(2,1)S(...) custom-call(bf16[64,512]{1,0:T(8,128)(2,1)S(1)} %get-tuple-element.126.refs_0_.refs_2_.refs_1_, ...), custom_call_target="tpu_custom_call" | custom-call | tf_op jit(solution)/shard_map/pallas_call | solution.py:124
  15.9 6.6 %shard_map.167 = (bf16[512,512]{1,0:T(8,128)(2,1)S(1)}, bf16[64,512]{1,0:T(8,128)(2,1)S(1)}, bf16[64,512]{1,0:T(8,128)(2,1)S(1)}, bf16[64,512]{1,0:T(8,128)(2,1)...) custom-call(f32[512,512]{1,0:T(8,128)S(1)} %get-tuple-element.130.re, ...), custom_call_target="tpu_custom_call" | custom-call | tf_op jit(solution)/shard_map/pallas_call | solution.py:124
  22.5 2.6 %shard_map.169 = (bf16[8,128,512]{2,1,0:T(8,128)(2,1)}, bf16[8,128,512]{2,1,0:T(8,128)(2,1)S(1)}) custom-call(s32[2]{0:T(128)S(1)} %pad_add_fusion.refs_0_, bf16[512,512]{1,0:T(8,128)(2,1)S(1)} %get-tuple-element.127.refs_2_.refs_1_, bf16[64,512]{1,0:T(8,128)(2,1)S(1)} %get-tuple-element.126.refs_0_.refs_2_.refs_1_, ...), custom_call_target="tpu_custom_call" | custom-call | tf_op jit(solution)/shard_map/pallas_call | solution.py:124
  25.2 3.1 %shard_map.168 = (bf16[8,96,512]{2,1,0:T(8,128)(2,1)}, bf16[8,96,512]{2,1,0:T(8,128)(2,1)S(1)}, bf16[64,512]{1,0:T(8,128)(2,1)S(1)}, bf16[64,512]{1,0:T(8,128)(2...) custom-call(s32[2]{0:T(128)S(1)} %pad_add_fusion.refs_0_, ...), custom_call_target="tpu_custom_call" | custom-call | tf_op jit(solution)/shard_map/pallas_call | solution.py:124
  28.9 1.9 %collective-permute-done.4.refs_3_ = bf16[8,96,512]{2,1,0:T(8,128)(2,1)S(1)} collective-permute-done((bf16[8,96,512]{2,1,0:T(8,128)(2,1)S(1)}, bf16[8,96,512]{2,1,0:T(8,128)(2,1)S(1)}, u32[]{:S(2)}, u32[]{:S(2)}) %collective-permute-start.4) | collective-permute-done | bytes 786464 | tf_op jit(solution)/shard_map/ppermute | solution.py:467
  36.9 2.6 %collective-permute-done.2.refs_3_ = bf16[32,512]{1,0:T(8,128)(2,1)S(1)} collective-permute-done((bf16[32,512]{1,0:T(8,128)(2,1)S(1)}, bf16[32,512]{1,0:T(8,128)(2,1)S(1)}, u32[]{:S(2)}, u32[]{:S(2)}) %collective-permute-start.2) | collective-permute-done | bytes 32800 | tf_op jit(solution)/shard_map/ppermute | solution.py:456
  39.5 3.7 %shard_map.171 = (bf16[64,512]{1,0:T(8,128)(2,1)S(1)}, bf16[64,512]{1,0:T(8,128)(2,1)S(1)}, f32[64,512]{1,0:T(8,128)S(1)}, f32[64,512]{1,0:T(8,128)S(1)}, f32[64...) custom-call(f32[64,512]{1,0:T(8,128)S(1)} %get-tuple-element.138.ref, ...), custom_call_target="tpu_custom_call" | custom-call | tf_op jit(solution)/shard_map/pallas_call | solution.py:124
  43.1 2.6 %shard_map.172 = (bf16[16,64,512]{2,1,0:T(8,128)(2,1)}, bf16[16,64,512]{2,1,0:T(8,128)(2,1)S(1)}) custom-call(s32[2]{0:T(128)S(1)} %pad_add_fusion.refs_0_, bf16[512,512]{1,0:T(8,128)(2,1)S(1)} %get-tuple-element.179.refs_1_, bf16[64,512]{1,0:T(8,128)(2,1)S(1)} %get-tuple-element.180.refs_2_.refs_1_, bf16[32,512]{1,0:T(8,128)(2,1)S(1)} %collective-permute-done.refs_3_, ...), custom_call_target="tpu_custom_call" | custom-call | tf_op jit(solution)/shard_map/pallas_call | solution.py:124
  46.7 3.2 %shard_map.173 = (bf16[16,48,512]{2,1,0:T(8,128)(2,1)}, bf16[16,48,512]{2,1,0:T(8,128)(2,1)S(1)}) custom-call(s32[2]{0:T(128)S(1)} %pad_add_fusion.refs_0_, bf16[64,512]{1,0:T(8,128)(2,1)S(1)} %get-tuple-element.180.refs_2_.refs_1_, bf16[64,512]{1,0:T(8,128)(2,1)} %get-tuple-element.189.refs_2_, bf16[64,512]{1,0:T(8,128)(2,1)} %get-tuple-element.190.refs_3_, ...), custom_call_target="tpu_custom_call" | custom-call | tf_op jit(solution)/shard_map/pallas_call | solution.py:124
  50.0 2.3 %collective-permute-done.8.refs_7_ = bf16[16,48,512]{2,1,0:T(8,128)(2,1)S(1)} collective-permute-done((bf16[16,48,512]{2,1,0:T(8,128)(2,1)S(1)}, bf16[16,48,512]{2,1,0:T(8,128)(2,1)S(1)}, u32[]{:S(2)}, u32[]{:S(2)}) %collective-permute-start.8) | collective-permute-done | bytes 786464 | tf_op jit(solution)/shard_map/ppermute | solution.py:467
  52.2 1.9 %shard_map.174 = (bf16[8,64,512]{2,1,0:T(8,128)(2,1)S(1)}, bf16[2,128,512]{2,1,0:T(8,128)(2,1)S(1)}, bf16[2,96,512]{2,1,0:T(8,128)(2,1)S(1)}, bf16[9,48,512]{2,1...) custom-call(bf16[16,64,512]{2,1,0:T(8,128)(2,1)} %get-tuple-element., ...), custom_call_target="tpu_custom_call" | custom-call | tf_op jit(solution)/shard_map/pallas_call | solution.py:124
  58.6 2.6 %collective-permute-start.12 = (bf16[2,96,512]{2,1,0:T(8,128)(2,1)S(1)}, bf16[2,96,512]{2,1,0:T(8,128)(2,1)S(1)}, u32[]{:S(2)}, u32[]{:S(2)}) collective-permute-start(bf16[2,96,512]{2,1,0:T(8,128)(2,1)S(1)} %get-tuple-element.202), channel_id=1, source_target_pairs={{0,16},{2,18},{4,20},{6,22},{8,24},{10,26},{12,28},{14,30},{16,0},... | collective-permute-start | bytes 589832 | tf_op jit(solution)/shard_map/ppermute | solution.py:467
  61.2 6.9 %collective-permute-done.12.refs_5_ = bf16[2,96,512]{2,1,0:T(8,128)(2,1)S(1)} collective-permute-done((bf16[2,96,512]{2,1,0:T(8,128)(2,1)S(1)}, bf16[2,96,512]{2,1,0:T(8,128)(2,1)S(1)}, u32[]{:S(2)}, u32[]{:S(2)}) %collective-permute-start.12) | collective-permute-done | bytes 196640 | tf_op jit(solution)/shard_map/ppermute | solution.py:467
  71.3 2.6 %collective-permute-start.15 = (bf16[1,128,512]{2,1,0:T(8,128)(2,1)S(1)}, bf16[1,128,512]{2,1,0:T(8,128)(2,1)S(1)}, u32[]{:S(2)}, u32[]{:S(2)}) collective-permute-start(bf16[1,128,512]{2,1,0:T(8,128)(2,1)S(1)} %get-tuple-element.210), channel_id=1, source_target_pairs={{0,16},{2,18},{4,20},{6,22},{8,24},{10,26},{12,28},{14,30},{16,0},... | collective-permute-start | bytes 393224 | tf_op jit(solution)/shard_map/ppermute | solution.py:467
  74.5 2.0 %shard_map.176.refs_8_ = f32[64,512]{1,0:T(8,128)} custom-call(f32[64,512]{1,0:T(8,128)S(1)} %get-tuple-element.176.refs_0_, f32[64,512]{1,0:T(8,128)S(1)} %get-tuple-element.177.refs_1_, f32[64,512]{1,0:T(8,128)S(1)} %get-tuple-element.178.refs_2_, bf16[9,48,512]{2,1,0:T(8,128)(2,1)S(1)} %collective-permute-done.9.refs_7_.refs_3_, s32[1,32]{1,0:T(1,128)S(1)} %copy-done.1, ...), custom_call_target="tpu_custom_call" | custom-call | tf_op jit(solution)/shard_map/pallas_call | solution.py:124
  76.6 1.9 %collective-permute-done.16.refs_7_ = bf16[1,96,512]{2,1,0:T(8,128)(2,1)S(1)} collective-permute-done((bf16[1,96,512]{2,1,0:T(8,128)(2,1)S(1)}, bf16[1,96,512]{2,1,0:T(8,128)(2,1)S(1)}, u32[]{:S(2)}, u32[]{:S(2)}) %collective-permute-start.16) | collective-permute-done | bytes 98336 | tf_op jit(solution)/shard_map/ppermute | solution.py:467
  81.5 4.8 %collective-permute-done.17.refs_1_.refs_3_ = bf16[2,112,512]{2,1,0:T(8,128)(2,1)S(1)} collective-permute-done((bf16[2,112,512]{2,1,0:T(8,128)(2,1)S(1)}, bf16[2,112,512]{2,1,0:T(8,128)(2,1)S(1)}, u32[]{:S(2)}, u32[]{:S(2)}) %collective-permute-start.17) | collective-permute-done | bytes 229408 | tf_op jit(solution)/shard_map/ppermute | solution.py:467
  86.3 3.0 %collective-permute-start.18 = (bf16[1,112,512]{2,1,0:T(8,128)(2,1)S(1)}, bf16[1,112,512]{2,1,0:T(8,128)(2,1)S(1)}, u32[]{:S(2)}, u32[]{:S(2)}) collective-permute-start(bf16[1,112,512]{2,1,0:T(8,128)(2,1)S(1)} %get-tuple-element.217), channel_id=1, source_target_pairs={{0,16},{2,18},{4,20},{6,22},{8,24},{10,26},{12,28},{14,30},{16,0},... | collective-permute-start | bytes 344072 | tf_op jit(solution)/shard_map/ppermute | solution.py:467
  90.0 3.6 %collective-permute-done.18.refs_1_.refs_3_ = bf16[1,112,512]{2,1,0:T(8,128)(2,1)S(1)} collective-permute-done((bf16[1,112,512]{2,1,0:T(8,128)(2,1)S(1)}, bf16[1,112,512]{2,1,0:T(8,128)(2,1)S(1)}, u32[]{:S(2)}, u32[]{:S(2)}) %collective-permute-start.18) | collective-permute-done | bytes 114720 | tf_op jit(solution)/shard_map/ppermute | solution.py:467
  94.4 2.2 %collective-permute-done.20.refs_4_ = bf16[224,512]{1,0:T(8,128)(2,1)S(1)} collective-permute-done((bf16[224,512]{1,0:T(8,128)(2,1)S(1)}, bf16[224,512]{1,0:T(8,128)(2,1)S(1)}, u32[]{:S(2)}, u32[]{:S(2)}) %collective-permute-start.20) | collective-permute-done | bytes 229408 | tf_op jit(solution)/shard_map/ppermute | solution.py:467
  96.6 1.9 %collective-permute-done.19.refs_2_ = bf16[112,512]{1,0:T(8,128)(2,1)S(1)} collective-permute-done((bf16[112,512]{1,0:T(8,128)(2,1)S(1)}, bf16[112,512]{1,0:T(8,128)(2,1)S(1)}, u32[]{:S(2)}, u32[]{:S(2)}) %collective-permute-start.19) | collective-permute-done | bytes 114720 | tf_op jit(solution)/shard_map/ppermute | solution.py:467
  (41 shorter events, 24.7 us)
Async XLA Ops:
  1.7 5.6 %collective-permute-start = (bf16[32,512]{1,0:T(8,128)(2,1)S(1)}, bf16[32,512]{1,0:T(8,128)(2,1)S(1)}, u32[]{:S(2)}, u32[]{:S(2)}) collective-permute-start(bf16[32,512]{1,0:T(8,128)(2,1)S(1)} %shard_map.164), channel_id=1, source_target_pairs={{0,1},{1,0},{2,3},{3,2},{4,5},{5,4},{6,7},{7,6},{8,9},{9,8},{10,11... | collective-permute-start | bytes 98312 | tf_op jit(solution)/shard_map/ppermute | solution.py:456
  4.7 2.6 %copy-start.1 = (s32[1,32]{1,0:T(1,128)S(1)}, s32[1,32]{1,0:T(1,128)}, u32[]{:S(2)}) copy-start(s32[1,32]{1,0:T(1,128)} %refs_4_.3) | copy-start | bytes 388
  11.9 4.0 %collective-permute-start.1 = (bf16[32,512]{1,0:T(8,128)(2,1)S(1)}, bf16[32,512]{1,0:T(8,128)(2,1)S(1)}, u32[]{:S(2)}, u32[]{:S(2)}) collective-permute-start(bf16[32,512]{1,0:T(8,128)(2,1)S(1)} %get-tuple-element.131), channel_id=1, source_target_pairs={{0,1},{1,0},{2,3},{3,2},{4,5},{5,4},{6,7},{7,6},{8,9},{9,8},{10,11... | collective-permute-start | bytes 98312 | tf_op jit(solution)/shard_map/ppermute | solution.py:456
  25.1 5.7 %collective-permute-start.3 = (bf16[8,128,512]{2,1,0:T(8,128)(2,1)S(1)}, bf16[8,128,512]{2,1,0:T(8,128)(2,1)S(1)}, u32[]{:S(2)}, u32[]{:S(2)}) collective-permute-start(bf16[8,128,512]{2,1,0:T(8,128)(2,1)S(1)} %get-tuple-element.171), channel_id=1, source_target_pairs={{0,2},{2,0},{4,6},{6,4},{8,10},{10,8},{12,14},{14,12},{16,18},{18,... | collective-permute-start | bytes 3145736 | tf_op jit(solution)/shard_map/ppermute | solution.py:467
  28.3 2.5 %collective-permute-start.4 = (bf16[8,96,512]{2,1,0:T(8,128)(2,1)S(1)}, bf16[8,96,512]{2,1,0:T(8,128)(2,1)S(1)}, u32[]{:S(2)}, u32[]{:S(2)}) collective-permute-start(bf16[8,96,512]{2,1,0:T(8,128)(2,1)S(1)} %get-tuple-element.173), channel_id=1, source_target_pairs={{0,2},{2,0},{4,6},{6,4},{8,10},{10,8},{12,14},{14,12},{16,18},{18,... | collective-permute-start | bytes 2359304 | tf_op jit(solution)/shard_map/ppermute | solution.py:467
  32.4 14.3 %collective-permute-start.6 = (bf16[4,128,512]{2,1,0:T(8,128)(2,1)S(1)}, bf16[4,128,512]{2,1,0:T(8,128)(2,1)S(1)}, u32[]{:S(2)}, u32[]{:S(2)}) collective-permute-start(bf16[4,128,512]{2,1,0:T(8,128)(2,1)S(1)} %get-tuple-element.174.refs_24_), channel_id=1, source_target_pairs={{0,4},{2,6},{4,0},{6,2},{8,12},{10,14},{12,8},{14,10},{16,20},{18,... | collective-permute-start | bytes 1572872 | tf_op jit(solution)/shard_map/ppermute | solution.py:467
  34.0 11.8 %collective-permute-start.7 = (bf16[4,96,512]{2,1,0:T(8,128)(2,1)S(1)}, bf16[4,96,512]{2,1,0:T(8,128)(2,1)S(1)}, u32[]{:S(2)}, u32[]{:S(2)}) collective-permute-start(bf16[4,96,512]{2,1,0:T(8,128)(2,1)S(1)} %get-tuple-element.175.refs_25_), channel_id=1, source_target_pairs={{0,8},{2,10},{4,12},{6,14},{8,0},{10,2},{12,4},{14,6},{16,24},{18,... | collective-permute-start | bytes 1179656 | tf_op jit(solution)/shard_map/ppermute | solution.py:467
  35.6 3.9 %collective-permute-start.2 = (bf16[32,512]{1,0:T(8,128)(2,1)S(1)}, bf16[32,512]{1,0:T(8,128)(2,1)S(1)}, u32[]{:S(2)}, u32[]{:S(2)}) collective-permute-start(bf16[32,512]{1,0:T(8,128)(2,1)S(1)} %get-tuple-element.141), channel_id=1, source_target_pairs={{0,1},{1,0},{2,3},{3,2},{4,5},{5,4},{6,7},{7,6},{8,9},{9,8},{10,11... | collective-permute-start | bytes 98312 | tf_op jit(solution)/shard_map/ppermute | solution.py:456
  45.7 4.2 %collective-permute-start.5 = (bf16[16,64,512]{2,1,0:T(8,128)(2,1)S(1)}, bf16[16,64,512]{2,1,0:T(8,128)(2,1)S(1)}, u32[]{:S(2)}, u32[]{:S(2)}) collective-permute-start(bf16[16,64,512]{2,1,0:T(8,128)(2,1)S(1)} %get-tuple-element.186), channel_id=1, source_target_pairs={{0,2},{2,0},{4,6},{6,4},{8,10},{10,8},{12,14},{14,12},{16,18},{18,... | collective-permute-start | bytes 3145736 | tf_op jit(solution)/shard_map/ppermute | solution.py:467
  49.9 2.4 %collective-permute-start.8 = (bf16[16,48,512]{2,1,0:T(8,128)(2,1)S(1)}, bf16[16,48,512]{2,1,0:T(8,128)(2,1)S(1)}, u32[]{:S(2)}, u32[]{:S(2)}) collective-permute-start(bf16[16,48,512]{2,1,0:T(8,128)(2,1)S(1)} %get-tuple-element.194), channel_id=1, source_target_pairs={{0,2},{2,0},{4,6},{6,4},{8,10},{10,8},{12,14},{14,12},{16,18},{18,... | collective-permute-start | bytes 2359304 | tf_op jit(solution)/shard_map/ppermute | solution.py:467
  54.1 14.9 %collective-permute-start.10 = (bf16[8,64,512]{2,1,0:T(8,128)(2,1)S(1)}, bf16[8,64,512]{2,1,0:T(8,128)(2,1)S(1)}, u32[]{:S(2)}, u32[]{:S(2)}) collective-permute-start(bf16[8,64,512]{2,1,0:T(8,128)(2,1)S(1)} %get-tuple-element.198), channel_id=1, source_target_pairs={{0,4},{2,6},{4,0},{6,2},{8,12},{10,14},{12,8},{14,10},{16,20},{18,... | collective-permute-start | bytes 1572872 | tf_op jit(solution)/shard_map/ppermute | solution.py:467
  55.7 13.3 %collective-permute-start.9 = (bf16[9,48,512]{2,1,0:T(8,128)(2,1)S(1)}, bf16[9,48,512]{2,1,0:T(8,128)(2,1)S(1)}, u32[]{:S(2)}, u32[]{:S(2)}) collective-permute-start(bf16[9,48,512]{2,1,0:T(8,128)(2,1)S(1)} %get-tuple-element.196), channel_id=1, source_target_pairs={{0,1},{1,0},{2,3},{3,2},{4,5},{5,4},{6,7},{7,6},{8,9},{9,8},{10,11... | collective-permute-start | bytes 1327112 | tf_op jit(solution)/shard_map/ppermute | solution.py:467
  57.0 12.0 %collective-permute-start.11 = (bf16[2,128,512]{2,1,0:T(8,128)(2,1)S(1)}, bf16[2,128,512]{2,1,0:T(8,128)(2,1)S(1)}, u32[]{:S(2)}, u32[]{:S(2)}) collective-permute-start(bf16[2,128,512]{2,1,0:T(8,128)(2,1)S(1)} %get-tuple-element.200), channel_id=1, source_target_pairs={{0,8},{2,10},{4,12},{6,14},{8,0},{10,2},{12,4},{14,6},{16,24},{18,... | collective-permute-start | bytes 786440 | tf_op jit(solution)/shard_map/ppermute | solution.py:467
  58.6 9.5 %collective-permute-start.12 = (bf16[2,96,512]{2,1,0:T(8,128)(2,1)S(1)}, bf16[2,96,512]{2,1,0:T(8,128)(2,1)S(1)}, u32[]{:S(2)}, u32[]{:S(2)}) collective-permute-start(bf16[2,96,512]{2,1,0:T(8,128)(2,1)S(1)} %get-tuple-element.202), channel_id=1, source_target_pairs={{0,16},{2,18},{4,20},{6,22},{8,24},{10,26},{12,28},{14,30},{16,0},... | collective-permute-start | bytes 589832 | tf_op jit(solution)/shard_map/ppermute | solution.py:467
  69.3 9.9 %collective-permute-start.13 = (bf16[4,64,512]{2,1,0:T(8,128)(2,1)S(1)}, bf16[4,64,512]{2,1,0:T(8,128)(2,1)S(1)}, u32[]{:S(2)}, u32[]{:S(2)}) collective-permute-start(bf16[4,64,512]{2,1,0:T(8,128)(2,1)S(1)} %get-tuple-element.204.refs_6_), channel_id=1, source_target_pairs={{0,1},{1,0},{2,3},{3,2},{4,5},{5,4},{6,7},{7,6},{8,9},{9,8},{10,11... | collective-permute-start | bytes 786440 | tf_op jit(solution)/shard_map/ppermute | solution.py:467
  70.0 9.1 %collective-permute-start.14 = (bf16[4,48,512]{2,1,0:T(8,128)(2,1)S(1)}, bf16[4,48,512]{2,1,0:T(8,128)(2,1)S(1)}, u32[]{:S(2)}, u32[]{:S(2)}) collective-permute-start(bf16[4,48,512]{2,1,0:T(8,128)(2,1)S(1)} %get-tuple-element.208), channel_id=1, source_target_pairs={{0,4},{2,6},{4,0},{6,2},{8,12},{10,14},{12,8},{14,10},{16,20},{18,... | collective-permute-start | bytes 589832 | tf_op jit(solution)/shard_map/ppermute | solution.py:467
  71.3 7.9 %collective-permute-start.15 = (bf16[1,128,512]{2,1,0:T(8,128)(2,1)S(1)}, bf16[1,128,512]{2,1,0:T(8,128)(2,1)S(1)}, u32[]{:S(2)}, u32[]{:S(2)}) collective-permute-start(bf16[1,128,512]{2,1,0:T(8,128)(2,1)S(1)} %get-tuple-element.210), channel_id=1, source_target_pairs={{0,16},{2,18},{4,20},{6,22},{8,24},{10,26},{12,28},{14,30},{16,0},... | collective-permute-start | bytes 393224 | tf_op jit(solution)/shard_map/ppermute | solution.py:467
  73.9 4.6 %collective-permute-start.16 = (bf16[1,96,512]{2,1,0:T(8,128)(2,1)S(1)}, bf16[1,96,512]{2,1,0:T(8,128)(2,1)S(1)}, u32[]{:S(2)}, u32[]{:S(2)}) collective-permute-start(bf16[1,96,512]{2,1,0:T(8,128)(2,1)S(1)} %get-tuple-element.212), channel_id=1, source_target_pairs={{0,4},{2,6},{4,0},{6,2},{8,12},{10,14},{12,8},{14,10},{16,20},{18,... | collective-permute-start | bytes 294920 | tf_op jit(solution)/shard_map/ppermute | solution.py:467
  79.1 0.9 copy-start
  80.2 6.1 %collective-permute-start.17 = (bf16[2,112,512]{2,1,0:T(8,128)(2,1)S(1)}, bf16[2,112,512]{2,1,0:T(8,128)(2,1)S(1)}, u32[]{:S(2)}, u32[]{:S(2)}) collective-permute-start(bf16[2,112,512]{2,1,0:T(8,128)(2,1)S(1)} %get-tuple-element.214), channel_id=1, source_target_pairs={{0,8},{2,10},{4,12},{6,14},{8,0},{10,2},{12,4},{14,6},{16,24},{18,... | collective-permute-start | bytes 688136 | tf_op jit(solution)/shard_map/ppermute | solution.py:467
  86.3 7.3 %collective-permute-start.18 = (bf16[1,112,512]{2,1,0:T(8,128)(2,1)S(1)}, bf16[1,112,512]{2,1,0:T(8,128)(2,1)S(1)}, u32[]{:S(2)}, u32[]{:S(2)}) collective-permute-start(bf16[1,112,512]{2,1,0:T(8,128)(2,1)S(1)} %get-tuple-element.217), channel_id=1, source_target_pairs={{0,16},{2,18},{4,20},{6,22},{8,24},{10,26},{12,28},{14,30},{16,0},... | collective-permute-start | bytes 344072 | tf_op jit(solution)/shard_map/ppermute | solution.py:467
  89.3 7.2 %collective-permute-start.20 = (bf16[224,512]{1,0:T(8,128)(2,1)S(1)}, bf16[224,512]{1,0:T(8,128)(2,1)S(1)}, u32[]{:S(2)}, u32[]{:S(2)}) collective-permute-start(bf16[224,512]{1,0:T(8,128)(2,1)S(1)} %bitcast.16), channel_id=1, source_target_pairs={{0,1},{1,0},{2,3},{3,2},{4,5},{5,4},{6,7},{7,6},{8,9},{9,8},{10,11... | collective-permute-start | bytes 688136 | tf_op jit(solution)/shard_map/ppermute | solution.py:467
  93.6 4.9 %collective-permute-start.19 = (bf16[112,512]{1,0:T(8,128)(2,1)S(1)}, bf16[112,512]{1,0:T(8,128)(2,1)S(1)}, u32[]{:S(2)}, u32[]{:S(2)}) collective-permute-start(bf16[112,512]{1,0:T(8,128)(2,1)S(1)} %bitcast.14), channel_id=1, source_target_pairs={{0,1},{1,0},{2,3},{3,2},{4,5},{5,4},{6,7},{7,6},{8,9},{9,8},{10,11... | collective-permute-start | bytes 344072 | tf_op jit(solution)/shard_map/ppermute | solution.py:467

commit v4 on v3

--- a/solution.py
+++ b/solution.py
@@ -484,7 +484,7 @@
 
 class Sum:
     def __init__(self, keep, route):
-        self.base, self.arrived, self.row = Part(keep), None, 0
+        self.base, self.arrived, self.row = keep, None, 0
         self.slots, self.rows, self.width = keep.shape
         self.route = list(route)
 
@@ -604,7 +604,7 @@
     rows = nodes * slots
     sent = send_rows.shape[1]
     known = nodes + sent
-    chunk = rows // 2
+    chunk = rows
     shards = lax.axis_size("dp")
     total_rows = samples * shards * nodes * lax.axis_size("mesh")
     factor = 1.0 / total_rows**0.5
@@ -647,8 +647,8 @@
         functools.partial(first_forward_kernel, chunk),
         (pre0, e0_near, h0_near, halo0, spread, mask, live, wet, send_rows)
         + (source0, edge_out0, node_in0, node_out0),
-        [far(large, BF16)] * 3 + [far((rows, 1), F32), (large, BF16), (small, BF16)]
-        + [far(small, BF16)] * 4 + [far((nodes, 1), F32), (thin, BF16)],
+        [(large, BF16)] * 3 + [((rows, 1), F32), (large, BF16), (small, BF16)]
+        + [(small, BF16)] * 4 + [((nodes, 1), F32), (thin, BF16)],
         fetch=(edge[1], receiver[1], source[1]),
     )
     halo1 = trade(packed1)
@@ -664,7 +664,7 @@
         functools.partial(middle_kernel, chunk),
         (pre1, e1, h1, halo1, spread, mask, live, wet, gh_near, ge_near)
         + (source1_w, edge_out1, node_in1, node_out1, edge1_w, receiver1_w),
-        [(large, BF16)] + [(small, BF16)] * 4 + backward_outs + [far(large, F32)] + backward_tail,
+        [(large, BF16)] + [(small, BF16)] * 4 + backward_outs + [(large, F32)] + backward_tail,
         scratch=[VMEM(large, BF16)] * 2 + [VMEM((rows, 1), F32), VMEM(large, BF16)],
         fetch=(node_out[0], node_in[0], edge_out[0], edge[0], receiver[0]),
     )
@@ -678,7 +678,7 @@
         keep, send, *fetched = call(
             functools.partial(kernel, order),
             operands,
-            [far(shape, BF16), (shape, BF16)],
+            [(shape, BF16)] * 2,
             scratch=[VMEM(w.shape[1:], F32) for w in kinds],
             smem=(me,),
             **more,
@@ -697,23 +697,22 @@
             node_weights_kernel, node_routes[layer], operands, (w_node_in, w_node_out), **more
         )
 
-    needed = (Part(slope_n0), Part(normed_n0), Part(inverse_n0), Part(slope0), Part(normed0))
     edge1, _ = edge_sum(1, (e1, h1, halo1, act1, gedge1, gpe1, sums1))
-    node1, near = node_sum(
-        1, (h1, message1, act_n1, gout1, gpre1), fetch=needed + (Part(inverse0), Part(ge))
-    )
-    first, arrived = advance([[edge1], [node1]])
-    gout0, gpre0, gh, more, own, halo_out, ge, gedge0, gpe0, sums0, e0_near, act0, h0_near = call(
+    node1, _ = node_sum(1, (h1, message1, act_n1, gout1, gpre1))
+    _, arrived = advance([[edge1]])
+    first, arrived_n = advance([[node1]])
+    arrived += arrived_n
+    gout0, gpre0, gh, more, own, halo_out, ge, gedge0, gpe0, sums0, e0_near, h0_near = call(
         functools.partial(first_backward_kernel, chunk),
-        (gh, more, own, back, send_rows, near[0], near[1], near[2], wet)
-        + (near[6], spread, live, near[3], near[4], near[5], source1_w, *near_w),
+        (gh, more, own, back, send_rows, slope_n0, normed_n0, inverse_n0, wet)
+        + (ge, spread, live, slope0, normed0, inverse0, source1_w, *near_w),
         [(small, BF16)] * 2 + backward_outs + [far(large, BF16)] + backward_tail,
         after=tuple(first),
-        fetch=(Part(e0), Part(act0), Part(h0)),
+        fetch=(Part(e0), Part(h0)),
     )
     edge0, _ = edge_sum(0, (e0_near, h0_near, halo0, act0, gedge0, gpe0, sums0))
     node0, _ = node_sum(
-        0, (h0_near, Part(message0), Part(act_n0), gout0, gpre0), after=tuple(arrived)
+        0, (h0_near, message0, act_n0, gout0, gpre0), after=tuple(arrived)
     )
     joint = lax.axis_size("mesh") == 2 and sent <= node0.rows
     wanted = [[edge0], [edge1], [node1], [node0]]
@@ -726,7 +725,7 @@
     (gh,) = call(
         last_kernel, (gh, more, own, back, send_rows, source[0]), [far(small, F32)], after=(out[0],)
     )
-    done = (gh,)
+    done = (in_hbm(gh),)
     while edge1.route:
         advance([[edge0, node0], [edge1], [node1]], after=done)
         done = ()
@@ -734,7 +733,7 @@
     mine1, other1 = across(value1)
     while edge0.route:
         advance([[edge0, node0]])
-    ((value0,), _) = advance([[edge0, node0]])
+    ((value0,), _) = advance([[edge0, node0]], after=(other1,))
     mine0, other0 = across(value0)
     grads = call(
         functools.partial(output_kernel, factor, (edge0.rows, node0.rows)),

time: 101 us -> 88.6 us (0.88)
  Pallas kernels: 39.9 us -> 28.6 us
    pallas_call x18 -> x19, Pallas kernels: 39.9 us -> 28.6 us  [call(): pl.pallas_call(run, in_specs=[pl.BlockSpec(memory_space=pltpu.SMEM)] * le...]
  transfers between devices with their start and end apart: 21 -> 21, of which waited for: 13 -> 13; matrix products, arithmetic and copies ran while one was open for 0% -> 0% of each run, Pallas kernels for 20% -> 16%
where the time goes in v4:
time: 88.6 us; the launch traced here: 88.2 us
  waiting for transfers between devices  30.5 us (34%)
  Pallas kernels  28.6 us (32%)
  starting transfers between devices  28.2 us (32%)
    pallas_call x19, Pallas kernels, call(): pl.pallas_call(run, in_specs=[pl.BlockSpec(memory_space=pltpu.SMEM)] * le...  28.6 us
    ppermute x18, waiting for transfers between devices, flip(): lax.ppermute(values, axis, [(i, i ^ bit) for i in range(lax.axis_size(axi...  27.2 us
    ppermute x18, starting transfers between devices, flip(): lax.ppermute(values, axis, [(i, i ^ bit) for i in range(lax.axis_size(axi...  22.4 us
    ppermute x3, starting transfers between devices, trade(): return lax.ppermute(rows, 'mesh', [(0, 1), (1, 0)])  5.78 us
    ppermute x3, waiting for transfers between devices, trade(): return lax.ppermute(rows, 'mesh', [(0, 1), (1, 0)])  3.32 us
  transfers between devices with their start and end apart: 21, of which 13 were waited for; matrix products, arithmetic and copies ran while one was open for 0% of the time, Pallas kernels for 16%

profile of v4, /device:TPU:0, one launch (start us, length us, event | category | flops | bytes accessed | tf_op | source)
XLA Modules:
  0.0 88.2 jit_solution(15466610828431337308)
XLA Ops:
  1.7 3.0 %collective-permute-start = (bf16[32,512]{1,0:T(8,128)(2,1)S(1)}, bf16[32,512]{1,0:T(8,128)(2,1)S(1)}, u32[]{:S(2)}, u32[]{:S(2)}) collective-permute-start(bf16[32,512]{1,0:T(8,128)(2,1)S(1)} %shard_map.164), channel_id=1, source_target_pairs={{0,1},{1,0},{2,3},{3,2},{4,5},{5,4},{6,7},{7,6},{8,9},{9,8},{10,11... | collective-permute-start | bytes 98312 | tf_op jit(solution)/shard_map/ppermute | solution.py:456
  4.7 2.5 %shard_map.163 = (bf16[512,160]{1,0:T(8,128)(2,1)S(1)}, bf16[512,64]{1,0:T(8,128)(2,1)S(1)}, f32[512,1]{1,0:T(8,128)S(1)}, f32[64,1]{1,0:T(8,128)S(1)}, f32[512,...) custom-call(s32[8,64]{1,0:T(8,128)} %bitcast.27, ...), custom_call_target="tpu_custom_call" | custom-call | tf_op jit(solution)/shard_map/pallas_call | solution.py:124
  7.3 3.6 %shard_map.165 = (bf16[512,512]{1,0:T(8,128)(2,1)S(1)}, bf16[512,512]{1,0:T(8,128)(2,1)S(1)}, bf16[512,512]{1,0:T(8,128)(2,1)S(1)}, f32[512,1]{1,0:T(8,128)S(1)}...) custom-call(f32[512,512]{1,0:T(8,128)S(1)} %get-tuple-element.107.re, ...), custom_call_target="tpu_custom_call" | custom-call | tf_op jit(solution)/shard_map/pallas_call | solution.py:124
  12.3 1.7 %shard_map.166 = (f32[512,512]{1,0:T(8,128)S(1)}, bf16[512,512]{1,0:T(8,128)(2,1)S(1)}, bf16[1024,512]{1,0:T(8,128)(2,1)S(1)}, bf16[512,512]{1,0:T(8,128)(2,1)S(...) custom-call(bf16[64,512]{1,0:T(8,128)(2,1)S(1)} %get-tuple-element.118.refs_0_.refs_2_.refs_1_, ...), custom_call_target="tpu_custom_call" | custom-call | tf_op jit(solution)/shard_map/pallas_call | solution.py:124
  14.8 5.4 %shard_map.167 = (bf16[512,512]{1,0:T(8,128)(2,1)S(1)}, bf16[64,512]{1,0:T(8,128)(2,1)S(1)}, bf16[64,512]{1,0:T(8,128)(2,1)S(1)}, bf16[64,512]{1,0:T(8,128)(2,1)...) custom-call(f32[512,512]{1,0:T(8,128)S(1)} %get-tuple-element.122.re, ...), custom_call_target="tpu_custom_call" | custom-call | tf_op jit(solution)/shard_map/pallas_call | solution.py:124
  20.3 1.8 %shard_map.172 = (bf16[8,128,512]{2,1,0:T(8,128)(2,1)S(1)}, bf16[8,128,512]{2,1,0:T(8,128)(2,1)S(1)}) custom-call(s32[2]{0:T(128)S(1)} %pad_add_fusion.refs_0_, bf16[512,512]{1,0:T(8,128)(2,1)S(1)} %get-tuple-element.119.refs_2_.refs_1_, bf16[64,512]{1,0:T(8,128)(2,1)S(1)} %get-tuple-element.118.refs_0_.refs_2_.refs_1_, ...), custom_call_target="tpu_custom_call" | custom-call | tf_op jit(solution)/shard_map/pallas_call | solution.py:124
  25.1 1.6 %collective-permute-start.6 = (bf16[4,128,512]{2,1,0:T(8,128)(2,1)S(1)}, bf16[4,128,512]{2,1,0:T(8,128)(2,1)S(1)}, u32[]{:S(2)}, u32[]{:S(2)}) collective-permute-start(bf16[4,128,512]{2,1,0:T(8,128)(2,1)S(1)} %get-tuple-element.171), channel_id=1, source_target_pairs={{0,4},{2,6},{4,0},{6,2},{8,12},{10,14},{12,8},{14,10},{16,20},{18,... | collective-permute-start | bytes 1572872 | tf_op jit(solution)/shard_map/ppermute | solution.py:467
  26.8 1.6 %collective-permute-start.7 = (bf16[4,96,512]{2,1,0:T(8,128)(2,1)S(1)}, bf16[4,96,512]{2,1,0:T(8,128)(2,1)S(1)}, u32[]{:S(2)}, u32[]{:S(2)}) collective-permute-start(bf16[4,96,512]{2,1,0:T(8,128)(2,1)S(1)} %get-tuple-element.152.refs_23_), channel_id=1, source_target_pairs={{0,8},{2,10},{4,12},{6,14},{8,0},{10,2},{12,4},{14,6},{16,24},{18,... | collective-permute-start | bytes 1179656 | tf_op jit(solution)/shard_map/ppermute | solution.py:467
  29.8 2.6 %collective-permute-done.2.refs_3_ = bf16[32,512]{1,0:T(8,128)(2,1)S(1)} collective-permute-done((bf16[32,512]{1,0:T(8,128)(2,1)S(1)}, bf16[32,512]{1,0:T(8,128)(2,1)S(1)}, u32[]{:S(2)}, u32[]{:S(2)}) %collective-permute-start.2) | collective-permute-done | bytes 32800 | tf_op jit(solution)/shard_map/ppermute | solution.py:456
  32.4 3.2 %shard_map.170 = (bf16[64,512]{1,0:T(8,128)(2,1)S(1)}, bf16[64,512]{1,0:T(8,128)(2,1)S(1)}, f32[64,512]{1,0:T(8,128)S(1)}, f32[64,512]{1,0:T(8,128)S(1)}, f32[64...) custom-call(f32[64,512]{1,0:T(8,128)S(1)} %get-tuple-element.130.ref, ...), custom_call_target="tpu_custom_call" | custom-call | tf_op jit(solution)/shard_map/pallas_call | solution.py:124
  35.6 1.8 %shard_map.171 = (bf16[16,64,512]{2,1,0:T(8,128)(2,1)S(1)}, bf16[16,64,512]{2,1,0:T(8,128)(2,1)S(1)}) custom-call(s32[2]{0:T(128)S(1)} %pad_add_fusion.refs_0_, bf16[512,512]{1,0:T(8,128)(2,1)S(1)} %get-tuple-element.156.refs_1_, bf16[64,512]{1,0:T(8,128)(2,1)S(1)} %get-tuple-element.157.refs_2_.refs_1_, bf16[32,512]{1,0:T(8,128)(2,1)S(1)} %collective-permute-done.refs_3_, ...), custom_call_target="tpu_custom_call" | custom-call | tf_op jit(solution)/shard_map/pallas_call | solution.py:124
  40.4 2.3 %collective-permute-done.8.refs_7_ = bf16[16,48,512]{2,1,0:T(8,128)(2,1)S(1)} collective-permute-done((bf16[16,48,512]{2,1,0:T(8,128)(2,1)S(1)}, bf16[16,48,512]{2,1,0:T(8,128)(2,1)S(1)}, u32[]{:S(2)}, u32[]{:S(2)}) %collective-permute-start.8) | collective-permute-done | bytes 786464 | tf_op jit(solution)/shard_map/ppermute | solution.py:467
  43.2 1.6 %collective-permute-start.10 = (bf16[8,64,512]{2,1,0:T(8,128)(2,1)S(1)}, bf16[8,64,512]{2,1,0:T(8,128)(2,1)S(1)}, u32[]{:S(2)}, u32[]{:S(2)}) collective-permute-start(bf16[8,64,512]{2,1,0:T(8,128)(2,1)S(1)} %get-tuple-element.182), channel_id=1, source_target_pairs={{0,4},{2,6},{4,0},{6,2},{8,12},{10,14},{12,8},{14,10},{16,20},{18,... | collective-permute-start | bytes 1572872 | tf_op jit(solution)/shard_map/ppermute | solution.py:467
  46.1 1.6 %collective-permute-start.11 = (bf16[2,128,512]{2,1,0:T(8,128)(2,1)S(1)}, bf16[2,128,512]{2,1,0:T(8,128)(2,1)S(1)}, u32[]{:S(2)}, u32[]{:S(2)}) collective-permute-start(bf16[2,128,512]{2,1,0:T(8,128)(2,1)S(1)} %get-tuple-element.184), channel_id=1, source_target_pairs={{0,8},{2,10},{4,12},{6,14},{8,0},{10,2},{12,4},{14,6},{16,24},{18,... | collective-permute-start | bytes 786440 | tf_op jit(solution)/shard_map/ppermute | solution.py:467
  47.7 2.6 %collective-permute-start.12 = (bf16[2,96,512]{2,1,0:T(8,128)(2,1)S(1)}, bf16[2,96,512]{2,1,0:T(8,128)(2,1)S(1)}, u32[]{:S(2)}, u32[]{:S(2)}) collective-permute-start(bf16[2,96,512]{2,1,0:T(8,128)(2,1)S(1)} %get-tuple-element.186), channel_id=1, source_target_pairs={{0,16},{2,18},{4,20},{6,22},{8,24},{10,26},{12,28},{14,30},{16,0},... | collective-permute-start | bytes 589832 | tf_op jit(solution)/shard_map/ppermute | solution.py:467
  50.3 6.9 %collective-permute-done.12.refs_5_ = bf16[2,96,512]{2,1,0:T(8,128)(2,1)S(1)} collective-permute-done((bf16[2,96,512]{2,1,0:T(8,128)(2,1)S(1)}, bf16[2,96,512]{2,1,0:T(8,128)(2,1)S(1)}, u32[]{:S(2)}, u32[]{:S(2)}) %collective-permute-start.12) | collective-permute-done | bytes 196640 | tf_op jit(solution)/shard_map/ppermute | solution.py:467
  60.4 2.6 %collective-permute-start.15 = (bf16[1,128,512]{2,1,0:T(8,128)(2,1)S(1)}, bf16[1,128,512]{2,1,0:T(8,128)(2,1)S(1)}, u32[]{:S(2)}, u32[]{:S(2)}) collective-permute-start(bf16[1,128,512]{2,1,0:T(8,128)(2,1)S(1)} %get-tuple-element.194), channel_id=1, source_target_pairs={{0,16},{2,18},{4,20},{6,22},{8,24},{10,26},{12,28},{14,30},{16,0},... | collective-permute-start | bytes 393224 | tf_op jit(solution)/shard_map/ppermute | solution.py:467
  63.6 2.0 %shard_map.177.refs_8_ = f32[64,512]{1,0:T(8,128)} custom-call(f32[64,512]{1,0:T(8,128)S(1)} %get-tuple-element.153.refs_0_, f32[64,512]{1,0:T(8,128)S(1)} %get-tuple-element.154.refs_1_, f32[64,512]{1,0:T(8,128)S(1)} %get-tuple-element.155.refs_2_, bf16[9,48,512]{2,1,0:T(8,128)(2,1)S(1)} %collective-permute-done.9.refs_7_.refs_3_, s32[1,32]{1,0:T(1,128)S(1)} %copy-done, ...), custom_call_target="tpu_custom_call" | custom-call | tf_op jit(solution)/shard_map/pallas_call | solution.py:124
  65.7 1.9 %collective-permute-done.16.refs_7_ = bf16[1,96,512]{2,1,0:T(8,128)(2,1)S(1)} collective-permute-done((bf16[1,96,512]{2,1,0:T(8,128)(2,1)S(1)}, bf16[1,96,512]{2,1,0:T(8,128)(2,1)S(1)}, u32[]{:S(2)}, u32[]{:S(2)}) %collective-permute-start.16) | collective-permute-done | bytes 98336 | tf_op jit(solution)/shard_map/ppermute | solution.py:467
  70.7 3.7 %collective-permute-done.17.refs_1_.refs_3_ = bf16[2,112,512]{2,1,0:T(8,128)(2,1)S(1)} collective-permute-done((bf16[2,112,512]{2,1,0:T(8,128)(2,1)S(1)}, bf16[2,112,512]{2,1,0:T(8,128)(2,1)S(1)}, u32[]{:S(2)}, u32[]{:S(2)}) %collective-permute-start.17) | collective-permute-done | bytes 229408 | tf_op jit(solution)/shard_map/ppermute | solution.py:467
  74.5 3.0 %collective-permute-start.18 = (bf16[1,112,512]{2,1,0:T(8,128)(2,1)S(1)}, bf16[1,112,512]{2,1,0:T(8,128)(2,1)S(1)}, u32[]{:S(2)}, u32[]{:S(2)}) collective-permute-start(bf16[1,112,512]{2,1,0:T(8,128)(2,1)S(1)} %get-tuple-element.201), channel_id=1, source_target_pairs={{0,16},{2,18},{4,20},{6,22},{8,24},{10,26},{12,28},{14,30},{16,0},... | collective-permute-start | bytes 344072 | tf_op jit(solution)/shard_map/ppermute | solution.py:467
  77.5 4.3 %collective-permute-done.18.refs_1_.refs_3_ = bf16[1,112,512]{2,1,0:T(8,128)(2,1)S(1)} collective-permute-done((bf16[1,112,512]{2,1,0:T(8,128)(2,1)S(1)}, bf16[1,112,512]{2,1,0:T(8,128)(2,1)S(1)}, u32[]{:S(2)}, u32[]{:S(2)}) %collective-permute-start.18) | collective-permute-done | bytes 114720 | tf_op jit(solution)/shard_map/ppermute | solution.py:467
  82.6 4.1 %collective-permute-done.20.refs_2_ = bf16[112,512]{1,0:T(8,128)(2,1)S(1)} collective-permute-done((bf16[112,512]{1,0:T(8,128)(2,1)S(1)}, bf16[112,512]{1,0:T(8,128)(2,1)S(1)}, u32[]{:S(2)}, u32[]{:S(2)}) %collective-permute-start.20) | collective-permute-done | bytes 114720 | tf_op jit(solution)/shard_map/ppermute | solution.py:467
  86.7 1.5 %shard_map.181 = (f32[2,96,512]{2,1,0:T(8,128)}, f32[2,32,512]{2,1,0:T(8,128)}, f32[2,64,512]{2,1,0:T(8,128)}, f32[2,32,512]{2,1,0:T(8,128)}) custom-call(s32[2]{0:T(128)S(1)} %pad_add_fusion.refs_0_, bf16[112,512]{1,0:T(8,128)(2,1)S(1)} %bitcast.14, bf16[112,512]{1,0:T(8,128)(2,1)S(1)} %collective-permute-done.20.refs_2_, bf16[224,512]{1,0:T(8,128)(2,1)S(1)} %bitcast.16, ...), custom_call_target="tpu_custom_call" | custom-call | tf_op jit(solution)/shard_map/pallas_call | solution.py:124
  (40 shorter events, 20.4 us)
Async XLA Ops:
  1.7 5.6 %collective-permute-start = (bf16[32,512]{1,0:T(8,128)(2,1)S(1)}, bf16[32,512]{1,0:T(8,128)(2,1)S(1)}, u32[]{:S(2)}, u32[]{:S(2)}) collective-permute-start(bf16[32,512]{1,0:T(8,128)(2,1)S(1)} %shard_map.164), channel_id=1, source_target_pairs={{0,1},{1,0},{2,3},{3,2},{4,5},{5,4},{6,7},{7,6},{8,9},{9,8},{10,11... | collective-permute-start | bytes 98312 | tf_op jit(solution)/shard_map/ppermute | solution.py:456
  4.7 2.6 %copy-start = (s32[1,32]{1,0:T(1,128)S(1)}, s32[1,32]{1,0:T(1,128)}, u32[]{:S(2)}) copy-start(s32[1,32]{1,0:T(1,128)} %refs_4_.3) | copy-start | bytes 388
  10.9 4.0 %collective-permute-start.1 = (bf16[32,512]{1,0:T(8,128)(2,1)S(1)}, bf16[32,512]{1,0:T(8,128)(2,1)S(1)}, u32[]{:S(2)}, u32[]{:S(2)}) collective-permute-start(bf16[32,512]{1,0:T(8,128)(2,1)S(1)} %get-tuple-element.123), channel_id=1, source_target_pairs={{0,1},{1,0},{2,3},{3,2},{4,5},{5,4},{6,7},{7,6},{8,9},{9,8},{10,11... | collective-permute-start | bytes 98312 | tf_op jit(solution)/shard_map/ppermute | solution.py:456
  22.1 2.7 %collective-permute-start.5 = (bf16[8,128,512]{2,1,0:T(8,128)(2,1)S(1)}, bf16[8,128,512]{2,1,0:T(8,128)(2,1)S(1)}, u32[]{:S(2)}, u32[]{:S(2)}) collective-permute-start(bf16[8,128,512]{2,1,0:T(8,128)(2,1)S(1)} %get-tuple-element.169), channel_id=1, source_target_pairs={{0,2},{2,0},{4,6},{6,4},{8,10},{10,8},{12,14},{14,12},{16,18},{18,... | collective-permute-start | bytes 3145736 | tf_op jit(solution)/shard_map/ppermute | solution.py:467
  23.4 3.2 %collective-permute-start.3 = (bf16[8,96,512]{2,1,0:T(8,128)(2,1)S(1)}, bf16[8,96,512]{2,1,0:T(8,128)(2,1)S(1)}, u32[]{:S(2)}, u32[]{:S(2)}) collective-permute-start(bf16[8,96,512]{2,1,0:T(8,128)(2,1)S(1)} %get-tuple-element.151), channel_id=1, source_target_pairs={{0,2},{2,0},{4,6},{6,4},{8,10},{10,8},{12,14},{14,12},{16,18},{18,... | collective-permute-start | bytes 2359304 | tf_op jit(solution)/shard_map/ppermute | solution.py:467
  25.1 14.0 %collective-permute-start.6 = (bf16[4,128,512]{2,1,0:T(8,128)(2,1)S(1)}, bf16[4,128,512]{2,1,0:T(8,128)(2,1)S(1)}, u32[]{:S(2)}, u32[]{:S(2)}) collective-permute-start(bf16[4,128,512]{2,1,0:T(8,128)(2,1)S(1)} %get-tuple-element.171), channel_id=1, source_target_pairs={{0,4},{2,6},{4,0},{6,2},{8,12},{10,14},{12,8},{14,10},{16,20},{18,... | collective-permute-start | bytes 1572872 | tf_op jit(solution)/shard_map/ppermute | solution.py:467
  26.8 10.9 %collective-permute-start.7 = (bf16[4,96,512]{2,1,0:T(8,128)(2,1)S(1)}, bf16[4,96,512]{2,1,0:T(8,128)(2,1)S(1)}, u32[]{:S(2)}, u32[]{:S(2)}) collective-permute-start(bf16[4,96,512]{2,1,0:T(8,128)(2,1)S(1)} %get-tuple-element.152.refs_23_), channel_id=1, source_target_pairs={{0,8},{2,10},{4,12},{6,14},{8,0},{10,2},{12,4},{14,6},{16,24},{18,... | collective-permute-start | bytes 1179656 | tf_op jit(solution)/shard_map/ppermute | solution.py:467
  28.5 3.9 %collective-permute-start.2 = (bf16[32,512]{1,0:T(8,128)(2,1)S(1)}, bf16[32,512]{1,0:T(8,128)(2,1)S(1)}, u32[]{:S(2)}, u32[]{:S(2)}) collective-permute-start(bf16[32,512]{1,0:T(8,128)(2,1)S(1)} %get-tuple-element.133), channel_id=1, source_target_pairs={{0,1},{1,0},{2,3},{3,2},{4,5},{5,4},{6,7},{7,6},{8,9},{9,8},{10,11... | collective-permute-start | bytes 98312 | tf_op jit(solution)/shard_map/ppermute | solution.py:456
  37.4 3.0 %collective-permute-start.4 = (bf16[16,64,512]{2,1,0:T(8,128)(2,1)S(1)}, bf16[16,64,512]{2,1,0:T(8,128)(2,1)S(1)}, u32[]{:S(2)}, u32[]{:S(2)}) collective-permute-start(bf16[16,64,512]{2,1,0:T(8,128)(2,1)S(1)} %get-tuple-element.163), channel_id=1, source_target_pairs={{0,2},{2,0},{4,6},{6,4},{8,10},{10,8},{12,14},{14,12},{16,18},{18,... | collective-permute-start | bytes 3145736 | tf_op jit(solution)/shard_map/ppermute | solution.py:467
  40.3 2.4 %collective-permute-start.8 = (bf16[16,48,512]{2,1,0:T(8,128)(2,1)S(1)}, bf16[16,48,512]{2,1,0:T(8,128)(2,1)S(1)}, u32[]{:S(2)}, u32[]{:S(2)}) collective-permute-start(bf16[16,48,512]{2,1,0:T(8,128)(2,1)S(1)} %get-tuple-element.178), channel_id=1, source_target_pairs={{0,2},{2,0},{4,6},{6,4},{8,10},{10,8},{12,14},{14,12},{16,18},{18,... | collective-permute-start | bytes 2359304 | tf_op jit(solution)/shard_map/ppermute | solution.py:467
  43.2 14.9 %collective-permute-start.10 = (bf16[8,64,512]{2,1,0:T(8,128)(2,1)S(1)}, bf16[8,64,512]{2,1,0:T(8,128)(2,1)S(1)}, u32[]{:S(2)}, u32[]{:S(2)}) collective-permute-start(bf16[8,64,512]{2,1,0:T(8,128)(2,1)S(1)} %get-tuple-element.182), channel_id=1, source_target_pairs={{0,4},{2,6},{4,0},{6,2},{8,12},{10,14},{12,8},{14,10},{16,20},{18,... | collective-permute-start | bytes 1572872 | tf_op jit(solution)/shard_map/ppermute | solution.py:467
  44.8 13.3 %collective-permute-start.9 = (bf16[9,48,512]{2,1,0:T(8,128)(2,1)S(1)}, bf16[9,48,512]{2,1,0:T(8,128)(2,1)S(1)}, u32[]{:S(2)}, u32[]{:S(2)}) collective-permute-start(bf16[9,48,512]{2,1,0:T(8,128)(2,1)S(1)} %get-tuple-element.180), channel_id=1, source_target_pairs={{0,1},{1,0},{2,3},{3,2},{4,5},{5,4},{6,7},{7,6},{8,9},{9,8},{10,11... | collective-permute-start | bytes 1327112 | tf_op jit(solution)/shard_map/ppermute | solution.py:467
  46.1 12.0 %collective-permute-start.11 = (bf16[2,128,512]{2,1,0:T(8,128)(2,1)S(1)}, bf16[2,128,512]{2,1,0:T(8,128)(2,1)S(1)}, u32[]{:S(2)}, u32[]{:S(2)}) collective-permute-start(bf16[2,128,512]{2,1,0:T(8,128)(2,1)S(1)} %get-tuple-element.184), channel_id=1, source_target_pairs={{0,8},{2,10},{4,12},{6,14},{8,0},{10,2},{12,4},{14,6},{16,24},{18,... | collective-permute-start | bytes 786440 | tf_op jit(solution)/shard_map/ppermute | solution.py:467
  47.7 9.5 %collective-permute-start.12 = (bf16[2,96,512]{2,1,0:T(8,128)(2,1)S(1)}, bf16[2,96,512]{2,1,0:T(8,128)(2,1)S(1)}, u32[]{:S(2)}, u32[]{:S(2)}) collective-permute-start(bf16[2,96,512]{2,1,0:T(8,128)(2,1)S(1)} %get-tuple-element.186), channel_id=1, source_target_pairs={{0,16},{2,18},{4,20},{6,22},{8,24},{10,26},{12,28},{14,30},{16,0},... | collective-permute-start | bytes 589832 | tf_op jit(solution)/shard_map/ppermute | solution.py:467
  58.4 9.9 %collective-permute-start.13 = (bf16[4,64,512]{2,1,0:T(8,128)(2,1)S(1)}, bf16[4,64,512]{2,1,0:T(8,128)(2,1)S(1)}, u32[]{:S(2)}, u32[]{:S(2)}) collective-permute-start(bf16[4,64,512]{2,1,0:T(8,128)(2,1)S(1)} %get-tuple-element.188.refs_6_), channel_id=1, source_target_pairs={{0,1},{1,0},{2,3},{3,2},{4,5},{5,4},{6,7},{7,6},{8,9},{9,8},{10,11... | collective-permute-start | bytes 786440 | tf_op jit(solution)/shard_map/ppermute | solution.py:467
  59.1 9.1 %collective-permute-start.14 = (bf16[4,48,512]{2,1,0:T(8,128)(2,1)S(1)}, bf16[4,48,512]{2,1,0:T(8,128)(2,1)S(1)}, u32[]{:S(2)}, u32[]{:S(2)}) collective-permute-start(bf16[4,48,512]{2,1,0:T(8,128)(2,1)S(1)} %get-tuple-element.192), channel_id=1, source_target_pairs={{0,4},{2,6},{4,0},{6,2},{8,12},{10,14},{12,8},{14,10},{16,20},{18,... | collective-permute-start | bytes 589832 | tf_op jit(solution)/shard_map/ppermute | solution.py:467
  60.4 7.9 %collective-permute-start.15 = (bf16[1,128,512]{2,1,0:T(8,128)(2,1)S(1)}, bf16[1,128,512]{2,1,0:T(8,128)(2,1)S(1)}, u32[]{:S(2)}, u32[]{:S(2)}) collective-permute-start(bf16[1,128,512]{2,1,0:T(8,128)(2,1)S(1)} %get-tuple-element.194), channel_id=1, source_target_pairs={{0,16},{2,18},{4,20},{6,22},{8,24},{10,26},{12,28},{14,30},{16,0},... | collective-permute-start | bytes 393224 | tf_op jit(solution)/shard_map/ppermute | solution.py:467
  63.0 4.6 %collective-permute-start.16 = (bf16[1,96,512]{2,1,0:T(8,128)(2,1)S(1)}, bf16[1,96,512]{2,1,0:T(8,128)(2,1)S(1)}, u32[]{:S(2)}, u32[]{:S(2)}) collective-permute-start(bf16[1,96,512]{2,1,0:T(8,128)(2,1)S(1)} %get-tuple-element.196), channel_id=1, source_target_pairs={{0,4},{2,6},{4,0},{6,2},{8,12},{10,14},{12,8},{14,10},{16,20},{18,... | collective-permute-start | bytes 294920 | tf_op jit(solution)/shard_map/ppermute | solution.py:467
  68.4 6.1 %collective-permute-start.17 = (bf16[2,112,512]{2,1,0:T(8,128)(2,1)S(1)}, bf16[2,112,512]{2,1,0:T(8,128)(2,1)S(1)}, u32[]{:S(2)}, u32[]{:S(2)}) collective-permute-start(bf16[2,112,512]{2,1,0:T(8,128)(2,1)S(1)} %get-tuple-element.198), channel_id=1, source_target_pairs={{0,8},{2,10},{4,12},{6,14},{8,0},{10,2},{12,4},{14,6},{16,24},{18,... | collective-permute-start | bytes 688136 | tf_op jit(solution)/shard_map/ppermute | solution.py:467
  69.7 7.8 %collective-permute-start.19 = (bf16[224,512]{1,0:T(8,128)(2,1)S(1)}, bf16[224,512]{1,0:T(8,128)(2,1)S(1)}, u32[]{:S(2)}, u32[]{:S(2)}) collective-permute-start(bf16[224,512]{1,0:T(8,128)(2,1)S(1)} %bitcast.15), channel_id=1, source_target_pairs={{0,1},{1,0},{2,3},{3,2},{4,5},{5,4},{6,7},{7,6},{8,9},{9,8},{10,11... | collective-permute-start | bytes 688136 | tf_op jit(solution)/shard_map/ppermute | solution.py:467
  74.5 7.3 %collective-permute-start.18 = (bf16[1,112,512]{2,1,0:T(8,128)(2,1)S(1)}, bf16[1,112,512]{2,1,0:T(8,128)(2,1)S(1)}, u32[]{:S(2)}, u32[]{:S(2)}) collective-permute-start(bf16[1,112,512]{2,1,0:T(8,128)(2,1)S(1)} %get-tuple-element.201), channel_id=1, source_target_pairs={{0,16},{2,18},{4,20},{6,22},{8,24},{10,26},{12,28},{14,30},{16,0},... | collective-permute-start | bytes 344072 | tf_op jit(solution)/shard_map/ppermute | solution.py:467
  81.8 4.9 %collective-permute-start.20 = (bf16[112,512]{1,0:T(8,128)(2,1)S(1)}, bf16[112,512]{1,0:T(8,128)(2,1)S(1)}, u32[]{:S(2)}, u32[]{:S(2)}) collective-permute-start(bf16[112,512]{1,0:T(8,128)(2,1)S(1)} %bitcast.13), channel_id=1, source_target_pairs={{0,1},{1,0},{2,3},{3,2},{4,5},{5,4},{6,7},{7,6},{8,9},{9,8},{10,11... | collective-permute-start | bytes 344072 | tf_op jit(solution)/shard_map/ppermute | solution.py:467

commit v5 on v4

--- a/solution.py
+++ b/solution.py
@@ -365,7 +365,9 @@
 
 def return_halo(gh_ref, more_ref, own_ref, back_ref, send_ref, wei_ref):
     nodes, width = gh_ref.shape
-    total = own_ref[...] + dot(pick_rows(send_ref, nodes), back_ref[...])
+    sent = send_ref.shape[1]
+    first = 0 if back_ref.shape[0] == sent else nodes
+    total = own_ref[...] + dot(pick_rows(send_ref, nodes), back_ref[first : first + sent, :])
     both = dot_nt(halves(total), wei_ref[...])
     return gh_ref[...] + more_ref[...] + both[:nodes] + both[nodes:]
 
@@ -668,7 +670,7 @@
         scratch=[VMEM(large, BF16)] * 2 + [VMEM((rows, 1), F32), VMEM(large, BF16)],
         fetch=(node_out[0], node_in[0], edge_out[0], edge[0], receiver[0]),
     )
-    back = trade(halo_out, back=True)
+    back = trade(halo_out if lax.axis_size("mesh") > 2 else sums1, back=True)
 
     def weight_sum(kernel, route, operands, kinds, **more):
         order = slot_order(route)
@@ -716,7 +718,8 @@
     )
     joint = lax.axis_size("mesh") == 2 and sent <= node0.rows
     wanted = [[edge0], [edge1], [node1], [node0]]
-    _, arrived = advance(wanted, tail=halo_out if joint else None)
+    out, _ = advance([[edge0], [edge1]])
+    _, arrived = advance([[node1], [node0]], after=(out[0],), tail=halo_out if joint else None)
     if joint:
         back = Part(arrived[-1], (arrived[-1].shape[0] - 1, pl.ds(0, sent)), thin, pin=False)
     else:

time: 88.6 us -> 86.8 us (0.980)
    pallas_call x19 -> x20, Pallas kernels: 28.6 us -> 28.2 us  [call(): pl.pallas_call(run, in_specs=[pl.BlockSpec(memory_space=pltpu.SMEM)] * le...]
  transfers between devices with their start and end apart: 21 -> 21, of which waited for: 13 -> 12; matrix products, arithmetic and copies ran while one was open for 0% -> 0% of each run, Pallas kernels for 16% -> 17%
where the time goes in v5:
time: 86.8 us; the launch traced here: 86.5 us
  waiting for transfers between devices  29.9 us (34%)
  Pallas kernels  28.2 us (32%)
  starting transfers between devices  27.6 us (32%)
    pallas_call x20, Pallas kernels, call(): pl.pallas_call(run, in_specs=[pl.BlockSpec(memory_space=pltpu.SMEM)] * le...  28.2 us
    ppermute x18, waiting for transfers between devices, flip(): lax.ppermute(values, axis, [(i, i ^ bit) for i in range(lax.axis_size(axi...  26.3 us
    ppermute x18, starting transfers between devices, flip(): lax.ppermute(values, axis, [(i, i ^ bit) for i in range(lax.axis_size(axi...  21.8 us
    ppermute x3, starting transfers between devices, trade(): return lax.ppermute(rows, 'mesh', [(0, 1), (1, 0)])  5.77 us
    ppermute x3, waiting for transfers between devices, trade(): return lax.ppermute(rows, 'mesh', [(0, 1), (1, 0)])  3.55 us
  transfers between devices with their start and end apart: 21, of which 12 were waited for; matrix products, arithmetic and copies ran while one was open for 0% of the time, Pallas kernels for 17%

profile of v5, /device:TPU:0, one launch (start us, length us, event | category | flops | bytes accessed | tf_op | source)
XLA Modules:
  0.0 86.5 jit_solution(12645645435849017159)
XLA Ops:
  1.7 3.0 %collective-permute-start = (bf16[32,512]{1,0:T(8,128)(2,1)S(1)}, bf16[32,512]{1,0:T(8,128)(2,1)S(1)}, u32[]{:S(2)}, u32[]{:S(2)}) collective-permute-start(bf16[32,512]{1,0:T(8,128)(2,1)S(1)} %shard_map.164), channel_id=1, source_target_pairs={{0,1},{1,0},{2,3},{3,2},{4,5},{5,4},{6,7},{7,6},{8,9},{9,8},{10,11... | collective-permute-start | bytes 98312 | tf_op jit(solution)/shard_map/ppermute | solution.py:458
  4.7 2.5 %shard_map.163 = (bf16[512,160]{1,0:T(8,128)(2,1)S(1)}, bf16[512,64]{1,0:T(8,128)(2,1)S(1)}, f32[512,1]{1,0:T(8,128)S(1)}, f32[64,1]{1,0:T(8,128)S(1)}, f32[512,...) custom-call(s32[8,64]{1,0:T(8,128)} %bitcast.27, ...), custom_call_target="tpu_custom_call" | custom-call | tf_op jit(solution)/shard_map/pallas_call | solution.py:124
  7.3 3.6 %shard_map.165 = (bf16[512,512]{1,0:T(8,128)(2,1)S(1)}, bf16[512,512]{1,0:T(8,128)(2,1)S(1)}, bf16[512,512]{1,0:T(8,128)(2,1)S(1)}, f32[512,1]{1,0:T(8,128)S(1)}...) custom-call(f32[512,512]{1,0:T(8,128)S(1)} %get-tuple-element.106.re, ...), custom_call_target="tpu_custom_call" | custom-call | tf_op jit(solution)/shard_map/pallas_call | solution.py:124
  12.3 1.7 %shard_map.166 = (f32[512,512]{1,0:T(8,128)S(1)}, bf16[512,512]{1,0:T(8,128)(2,1)S(1)}, bf16[1024,512]{1,0:T(8,128)(2,1)S(1)}, bf16[512,512]{1,0:T(8,128)(2,1)S(...) custom-call(bf16[64,512]{1,0:T(8,128)(2,1)S(1)} %get-tuple-element.117.refs_0_.refs_2_.refs_1_, ...), custom_call_target="tpu_custom_call" | custom-call | tf_op jit(solution)/shard_map/pallas_call | solution.py:124
  14.8 4.9 %shard_map.167 = (bf16[512,512]{1,0:T(8,128)(2,1)S(1)}, bf16[64,512]{1,0:T(8,128)(2,1)S(1)}, bf16[64,512]{1,0:T(8,128)(2,1)S(1)}, bf16[64,512]{1,0:T(8,128)(2,1)...) custom-call(f32[512,512]{1,0:T(8,128)S(1)} %get-tuple-element.121.re, ...), custom_call_target="tpu_custom_call" | custom-call | tf_op jit(solution)/shard_map/pallas_call | solution.py:124
  19.8 1.8 %shard_map.171 = (bf16[8,128,512]{2,1,0:T(8,128)(2,1)S(1)}, bf16[8,128,512]{2,1,0:T(8,128)(2,1)S(1)}) custom-call(s32[2]{0:T(128)S(1)} %pad_add_fusion.refs_0_, bf16[512,512]{1,0:T(8,128)(2,1)S(1)} %get-tuple-element.118.refs_2_.refs_1_, bf16[64,512]{1,0:T(8,128)(2,1)S(1)} %get-tuple-element.117.refs_0_.refs_2_.refs_1_, ...), custom_call_target="tpu_custom_call" | custom-call | tf_op jit(solution)/shard_map/pallas_call | solution.py:124
  24.6 1.6 %collective-permute-start.6 = (bf16[4,128,512]{2,1,0:T(8,128)(2,1)S(1)}, bf16[4,128,512]{2,1,0:T(8,128)(2,1)S(1)}, u32[]{:S(2)}, u32[]{:S(2)}) collective-permute-start(bf16[4,128,512]{2,1,0:T(8,128)(2,1)S(1)} %get-tuple-element.166), channel_id=1, source_target_pairs={{0,4},{2,6},{4,0},{6,2},{8,12},{10,14},{12,8},{14,10},{16,20},{18,... | collective-permute-start | bytes 1572872 | tf_op jit(solution)/shard_map/ppermute | solution.py:469
  27.7 1.6 %collective-permute-start.4 = (bf16[4,96,512]{2,1,0:T(8,128)(2,1)S(1)}, bf16[4,96,512]{2,1,0:T(8,128)(2,1)S(1)}, u32[]{:S(2)}, u32[]{:S(2)}) collective-permute-start(bf16[4,96,512]{2,1,0:T(8,128)(2,1)S(1)} %get-tuple-element.151.refs_23_), channel_id=1, source_target_pairs={{0,8},{2,10},{4,12},{6,14},{8,0},{10,2},{12,4},{14,6},{16,24},{18,... | collective-permute-start | bytes 1179656 | tf_op jit(solution)/shard_map/ppermute | solution.py:469
  29.3 2.8 %collective-permute-done.2.refs_3_ = bf16[160,512]{1,0:T(8,128)(2,1)S(1)} collective-permute-done((bf16[160,512]{1,0:T(8,128)(2,1)S(1)}, bf16[160,512]{1,0:T(8,128)(2,1)S(1)}, u32[]{:S(2)}, u32[]{:S(2)}) %collective-permute-start.2) | collective-permute-done | bytes 163872 | tf_op jit(solution)/shard_map/ppermute | solution.py:458
  32.1 3.2 %shard_map.170 = (bf16[64,512]{1,0:T(8,128)(2,1)S(1)}, bf16[64,512]{1,0:T(8,128)(2,1)S(1)}, f32[64,512]{1,0:T(8,128)S(1)}, f32[64,512]{1,0:T(8,128)S(1)}, f32[64...) custom-call(f32[64,512]{1,0:T(8,128)S(1)} %get-tuple-element.129.ref, ...), custom_call_target="tpu_custom_call" | custom-call | tf_op jit(solution)/shard_map/pallas_call | solution.py:124
  35.3 1.8 %shard_map.174 = (bf16[16,64,512]{2,1,0:T(8,128)(2,1)S(1)}, bf16[16,64,512]{2,1,0:T(8,128)(2,1)S(1)}) custom-call(s32[2]{0:T(128)S(1)} %pad_add_fusion.refs_0_, bf16[512,512]{1,0:T(8,128)(2,1)S(1)} %get-tuple-element.170.refs_1_, bf16[64,512]{1,0:T(8,128)(2,1)S(1)} %get-tuple-element.156.refs_1_.refs_2_, bf16[32,512]{1,0:T(8,128)(2,1)S(1)} %collective-permute-done.refs_3_, ...), custom_call_target="tpu_custom_call" | custom-call | tf_op jit(solution)/shard_map/pallas_call | solution.py:124
  40.3 1.6 %collective-permute-start.10 = (bf16[8,64,512]{2,1,0:T(8,128)(2,1)S(1)}, bf16[8,64,512]{2,1,0:T(8,128)(2,1)S(1)}, u32[]{:S(2)}, u32[]{:S(2)}) collective-permute-start(bf16[8,64,512]{2,1,0:T(8,128)(2,1)S(1)} %get-tuple-element.178.refs_5_), channel_id=1, source_target_pairs={{0,4},{2,6},{4,0},{6,2},{8,12},{10,14},{12,8},{14,10},{16,20},{18,... | collective-permute-start | bytes 1572872 | tf_op jit(solution)/shard_map/ppermute | solution.py:469
  43.9 1.6 %collective-permute-start.11 = (bf16[2,128,512]{2,1,0:T(8,128)(2,1)S(1)}, bf16[2,128,512]{2,1,0:T(8,128)(2,1)S(1)}, u32[]{:S(2)}, u32[]{:S(2)}) collective-permute-start(bf16[2,128,512]{2,1,0:T(8,128)(2,1)S(1)} %get-tuple-element.182), channel_id=1, source_target_pairs={{0,8},{2,10},{4,12},{6,14},{8,0},{10,2},{12,4},{14,6},{16,24},{18,... | collective-permute-start | bytes 786440 | tf_op jit(solution)/shard_map/ppermute | solution.py:469
  45.5 2.6 %collective-permute-start.12 = (bf16[2,96,512]{2,1,0:T(8,128)(2,1)S(1)}, bf16[2,96,512]{2,1,0:T(8,128)(2,1)S(1)}, u32[]{:S(2)}, u32[]{:S(2)}) collective-permute-start(bf16[2,96,512]{2,1,0:T(8,128)(2,1)S(1)} %get-tuple-element.184), channel_id=1, source_target_pairs={{0,16},{2,18},{4,20},{6,22},{8,24},{10,26},{12,28},{14,30},{16,0},... | collective-permute-start | bytes 589832 | tf_op jit(solution)/shard_map/ppermute | solution.py:469
  48.1 8.1 %collective-permute-done.11.refs_3_ = bf16[2,128,512]{2,1,0:T(8,128)(2,1)S(1)} collective-permute-done((bf16[2,128,512]{2,1,0:T(8,128)(2,1)S(1)}, bf16[2,128,512]{2,1,0:T(8,128)(2,1)S(1)}, u32[]{:S(2)}, u32[]{:S(2)}) %collective-permute-start.11) | collective-permute-done | bytes 262176 | tf_op jit(solution)/shard_map/ppermute | solution.py:469
  57.2 1.5 %collective-permute-start.14 = (bf16[4,48,512]{2,1,0:T(8,128)(2,1)S(1)}, bf16[4,48,512]{2,1,0:T(8,128)(2,1)S(1)}, u32[]{:S(2)}, u32[]{:S(2)}) collective-permute-start(bf16[4,48,512]{2,1,0:T(8,128)(2,1)S(1)} %get-tuple-element.190), channel_id=1, source_target_pairs={{0,4},{2,6},{4,0},{6,2},{8,12},{10,14},{12,8},{14,10},{16,20},{18,... | collective-permute-start | bytes 589832 | tf_op jit(solution)/shard_map/ppermute | solution.py:469
  58.7 2.5 %collective-permute-start.15 = (bf16[1,128,512]{2,1,0:T(8,128)(2,1)S(1)}, bf16[1,128,512]{2,1,0:T(8,128)(2,1)S(1)}, u32[]{:S(2)}, u32[]{:S(2)}) collective-permute-start(bf16[1,128,512]{2,1,0:T(8,128)(2,1)S(1)} %get-tuple-element.192), channel_id=1, source_target_pairs={{0,16},{2,18},{4,20},{6,22},{8,24},{10,26},{12,28},{14,30},{16,0},... | collective-permute-start | bytes 393224 | tf_op jit(solution)/shard_map/ppermute | solution.py:469
  61.7 2.0 %shard_map.178.refs_8_ = f32[64,512]{1,0:T(8,128)} custom-call(f32[64,512]{1,0:T(8,128)S(1)} %get-tuple-element.152.refs_0_, f32[64,512]{1,0:T(8,128)S(1)} %get-tuple-element.153.refs_1_, f32[64,512]{1,0:T(8,128)S(1)} %get-tuple-element.154.refs_2_, bf16[9,48,512]{2,1,0:T(8,128)(2,1)S(1)} %collective-permute-done.9.refs_7_.refs_3_, s32[1,32]{1,0:T(1,128)S(1)} %copy-done, ...), custom_call_target="tpu_custom_call" | custom-call | tf_op jit(solution)/shard_map/pallas_call | solution.py:124
  63.7 2.0 %collective-permute-done.16.refs_7_ = bf16[1,96,512]{2,1,0:T(8,128)(2,1)S(1)} collective-permute-done((bf16[1,96,512]{2,1,0:T(8,128)(2,1)S(1)}, bf16[1,96,512]{2,1,0:T(8,128)(2,1)S(1)}, u32[]{:S(2)}, u32[]{:S(2)}) %collective-permute-start.16) | collective-permute-done | bytes 98336 | tf_op jit(solution)/shard_map/ppermute | solution.py:469
  69.1 4.0 %collective-permute-done.17.refs_1_.refs_3_ = bf16[2,112,512]{2,1,0:T(8,128)(2,1)S(1)} collective-permute-done((bf16[2,112,512]{2,1,0:T(8,128)(2,1)S(1)}, bf16[2,112,512]{2,1,0:T(8,128)(2,1)S(1)}, u32[]{:S(2)}, u32[]{:S(2)}) %collective-permute-start.17) | collective-permute-done | bytes 229408 | tf_op jit(solution)/shard_map/ppermute | solution.py:469
  73.1 1.9 %collective-permute-start.18 = (bf16[1,112,512]{2,1,0:T(8,128)(2,1)S(1)}, bf16[1,112,512]{2,1,0:T(8,128)(2,1)S(1)}, u32[]{:S(2)}, u32[]{:S(2)}) collective-permute-start(bf16[1,112,512]{2,1,0:T(8,128)(2,1)S(1)} %get-tuple-element.199), channel_id=1, source_target_pairs={{0,16},{2,18},{4,20},{6,22},{8,24},{10,26},{12,28},{14,30},{16,0},... | collective-permute-start | bytes 344072 | tf_op jit(solution)/shard_map/ppermute | solution.py:469
  75.1 5.0 %collective-permute-done.18.refs_1_.refs_3_ = bf16[1,112,512]{2,1,0:T(8,128)(2,1)S(1)} collective-permute-done((bf16[1,112,512]{2,1,0:T(8,128)(2,1)S(1)}, bf16[1,112,512]{2,1,0:T(8,128)(2,1)S(1)}, u32[]{:S(2)}, u32[]{:S(2)}) %collective-permute-start.18) | collective-permute-done | bytes 114720 | tf_op jit(solution)/shard_map/ppermute | solution.py:469
  81.6 3.5 %collective-permute-done.20.refs_2_ = bf16[112,512]{1,0:T(8,128)(2,1)S(1)} collective-permute-done((bf16[112,512]{1,0:T(8,128)(2,1)S(1)}, bf16[112,512]{1,0:T(8,128)(2,1)S(1)}, u32[]{:S(2)}, u32[]{:S(2)}) %collective-permute-start.20) | collective-permute-done | bytes 114720 | tf_op jit(solution)/shard_map/ppermute | solution.py:469
  85.0 1.5 %shard_map.182 = (f32[2,96,512]{2,1,0:T(8,128)}, f32[2,32,512]{2,1,0:T(8,128)}, f32[2,64,512]{2,1,0:T(8,128)}, f32[2,32,512]{2,1,0:T(8,128)}) custom-call(s32[2]{0:T(128)S(1)} %pad_add_fusion.refs_0_, bf16[112,512]{1,0:T(8,128)(2,1)S(1)} %bitcast.14, bf16[112,512]{1,0:T(8,128)(2,1)S(1)} %collective-permute-done.20.refs_2_, bf16[224,512]{1,0:T(8,128)(2,1)S(1)} %bitcast.16, ...), custom_call_target="tpu_custom_call" | custom-call | tf_op jit(solution)/shard_map/pallas_call | solution.py:124
  (41 shorter events, 19.3 us)
Async XLA Ops:
  1.7 5.6 %collective-permute-start = (bf16[32,512]{1,0:T(8,128)(2,1)S(1)}, bf16[32,512]{1,0:T(8,128)(2,1)S(1)}, u32[]{:S(2)}, u32[]{:S(2)}) collective-permute-start(bf16[32,512]{1,0:T(8,128)(2,1)S(1)} %shard_map.164), channel_id=1, source_target_pairs={{0,1},{1,0},{2,3},{3,2},{4,5},{5,4},{6,7},{7,6},{8,9},{9,8},{10,11... | collective-permute-start | bytes 98312 | tf_op jit(solution)/shard_map/ppermute | solution.py:458
  4.7 2.6 %copy-start = (s32[1,32]{1,0:T(1,128)S(1)}, s32[1,32]{1,0:T(1,128)}, u32[]{:S(2)}) copy-start(s32[1,32]{1,0:T(1,128)} %refs_4_.3) | copy-start | bytes 388
  10.9 4.0 %collective-permute-start.1 = (bf16[32,512]{1,0:T(8,128)(2,1)S(1)}, bf16[32,512]{1,0:T(8,128)(2,1)S(1)}, u32[]{:S(2)}, u32[]{:S(2)}) collective-permute-start(bf16[32,512]{1,0:T(8,128)(2,1)S(1)} %get-tuple-element.122), channel_id=1, source_target_pairs={{0,1},{1,0},{2,3},{3,2},{4,5},{5,4},{6,7},{7,6},{8,9},{9,8},{10,11... | collective-permute-start | bytes 98312 | tf_op jit(solution)/shard_map/ppermute | solution.py:458
  21.6 2.7 %collective-permute-start.5 = (bf16[8,128,512]{2,1,0:T(8,128)(2,1)S(1)}, bf16[8,128,512]{2,1,0:T(8,128)(2,1)S(1)}, u32[]{:S(2)}, u32[]{:S(2)}) collective-permute-start(bf16[8,128,512]{2,1,0:T(8,128)(2,1)S(1)} %get-tuple-element.165), channel_id=1, source_target_pairs={{0,2},{2,0},{4,6},{6,4},{8,10},{10,8},{12,14},{14,12},{16,18},{18,... | collective-permute-start | bytes 3145736 | tf_op jit(solution)/shard_map/ppermute | solution.py:469
  22.9 4.6 %collective-permute-start.3 = (bf16[8,96,512]{2,1,0:T(8,128)(2,1)S(1)}, bf16[8,96,512]{2,1,0:T(8,128)(2,1)S(1)}, u32[]{:S(2)}, u32[]{:S(2)}) collective-permute-start(bf16[8,96,512]{2,1,0:T(8,128)(2,1)S(1)} %get-tuple-element.150), channel_id=1, source_target_pairs={{0,2},{2,0},{4,6},{6,4},{8,10},{10,8},{12,14},{14,12},{16,18},{18,... | collective-permute-start | bytes 2359304 | tf_op jit(solution)/shard_map/ppermute | solution.py:469
  24.6 14.0 %collective-permute-start.6 = (bf16[4,128,512]{2,1,0:T(8,128)(2,1)S(1)}, bf16[4,128,512]{2,1,0:T(8,128)(2,1)S(1)}, u32[]{:S(2)}, u32[]{:S(2)}) collective-permute-start(bf16[4,128,512]{2,1,0:T(8,128)(2,1)S(1)} %get-tuple-element.166), channel_id=1, source_target_pairs={{0,4},{2,6},{4,0},{6,2},{8,12},{10,14},{12,8},{14,10},{16,20},{18,... | collective-permute-start | bytes 1572872 | tf_op jit(solution)/shard_map/ppermute | solution.py:469
  26.2 6.0 %collective-permute-start.2 = (bf16[160,512]{1,0:T(8,128)(2,1)S(1)}, bf16[160,512]{1,0:T(8,128)(2,1)S(1)}, u32[]{:S(2)}, u32[]{:S(2)}) collective-permute-start(bf16[160,512]{1,0:T(8,128)(2,1)S(1)} %get-tuple-element.132.refs_7_), channel_id=1, source_target_pairs={{0,1},{1,0},{2,3},{3,2},{4,5},{5,4},{6,7},{7,6},{8,9},{9,8},{10,11... | collective-permute-start | bytes 491528 | tf_op jit(solution)/shard_map/ppermute | solution.py:458
  27.7 10.7 %collective-permute-start.4 = (bf16[4,96,512]{2,1,0:T(8,128)(2,1)S(1)}, bf16[4,96,512]{2,1,0:T(8,128)(2,1)S(1)}, u32[]{:S(2)}, u32[]{:S(2)}) collective-permute-start(bf16[4,96,512]{2,1,0:T(8,128)(2,1)S(1)} %get-tuple-element.151.refs_23_), channel_id=1, source_target_pairs={{0,8},{2,10},{4,12},{6,14},{8,0},{10,2},{12,4},{14,6},{16,24},{18,... | collective-permute-start | bytes 1179656 | tf_op jit(solution)/shard_map/ppermute | solution.py:469
  37.2 2.8 %collective-permute-start.8 = (bf16[16,64,512]{2,1,0:T(8,128)(2,1)S(1)}, bf16[16,64,512]{2,1,0:T(8,128)(2,1)S(1)}, u32[]{:S(2)}, u32[]{:S(2)}) collective-permute-start(bf16[16,64,512]{2,1,0:T(8,128)(2,1)S(1)} %get-tuple-element.176), channel_id=1, source_target_pairs={{0,2},{2,0},{4,6},{6,4},{8,10},{10,8},{12,14},{14,12},{16,18},{18,... | collective-permute-start | bytes 3145736 | tf_op jit(solution)/shard_map/ppermute | solution.py:469
  39.9 2.4 %collective-permute-start.7 = (bf16[16,48,512]{2,1,0:T(8,128)(2,1)S(1)}, bf16[16,48,512]{2,1,0:T(8,128)(2,1)S(1)}, u32[]{:S(2)}, u32[]{:S(2)}) collective-permute-start(bf16[16,48,512]{2,1,0:T(8,128)(2,1)S(1)} %get-tuple-element.168), channel_id=1, source_target_pairs={{0,2},{2,0},{4,6},{6,4},{8,10},{10,8},{12,14},{14,12},{16,18},{18,... | collective-permute-start | bytes 2359304 | tf_op jit(solution)/shard_map/ppermute | solution.py:469
  40.3 15.9 %collective-permute-start.10 = (bf16[8,64,512]{2,1,0:T(8,128)(2,1)S(1)}, bf16[8,64,512]{2,1,0:T(8,128)(2,1)S(1)}, u32[]{:S(2)}, u32[]{:S(2)}) collective-permute-start(bf16[8,64,512]{2,1,0:T(8,128)(2,1)S(1)} %get-tuple-element.178.refs_5_), channel_id=1, source_target_pairs={{0,4},{2,6},{4,0},{6,2},{8,12},{10,14},{12,8},{14,10},{16,20},{18,... | collective-permute-start | bytes 1572872 | tf_op jit(solution)/shard_map/ppermute | solution.py:469
  42.5 13.7 %collective-permute-start.9 = (bf16[9,48,512]{2,1,0:T(8,128)(2,1)S(1)}, bf16[9,48,512]{2,1,0:T(8,128)(2,1)S(1)}, u32[]{:S(2)}, u32[]{:S(2)}) collective-permute-start(bf16[9,48,512]{2,1,0:T(8,128)(2,1)S(1)} %get-tuple-element.179), channel_id=1, source_target_pairs={{0,1},{1,0},{2,3},{3,2},{4,5},{5,4},{6,7},{7,6},{8,9},{9,8},{10,11... | collective-permute-start | bytes 1327112 | tf_op jit(solution)/shard_map/ppermute | solution.py:469
  43.9 12.3 %collective-permute-start.11 = (bf16[2,128,512]{2,1,0:T(8,128)(2,1)S(1)}, bf16[2,128,512]{2,1,0:T(8,128)(2,1)S(1)}, u32[]{:S(2)}, u32[]{:S(2)}) collective-permute-start(bf16[2,128,512]{2,1,0:T(8,128)(2,1)S(1)} %get-tuple-element.182), channel_id=1, source_target_pairs={{0,8},{2,10},{4,12},{6,14},{8,0},{10,2},{12,4},{14,6},{16,24},{18,... | collective-permute-start | bytes 786440 | tf_op jit(solution)/shard_map/ppermute | solution.py:469
  45.5 10.7 %collective-permute-start.12 = (bf16[2,96,512]{2,1,0:T(8,128)(2,1)S(1)}, bf16[2,96,512]{2,1,0:T(8,128)(2,1)S(1)}, u32[]{:S(2)}, u32[]{:S(2)}) collective-permute-start(bf16[2,96,512]{2,1,0:T(8,128)(2,1)S(1)} %get-tuple-element.184), channel_id=1, source_target_pairs={{0,16},{2,18},{4,20},{6,22},{8,24},{10,26},{12,28},{14,30},{16,0},... | collective-permute-start | bytes 589832 | tf_op jit(solution)/shard_map/ppermute | solution.py:469
  56.4 10.4 %collective-permute-start.13 = (bf16[4,64,512]{2,1,0:T(8,128)(2,1)S(1)}, bf16[4,64,512]{2,1,0:T(8,128)(2,1)S(1)}, u32[]{:S(2)}, u32[]{:S(2)}) collective-permute-start(bf16[4,64,512]{2,1,0:T(8,128)(2,1)S(1)} %get-tuple-element.186.refs_6_), channel_id=1, source_target_pairs={{0,1},{1,0},{2,3},{3,2},{4,5},{5,4},{6,7},{7,6},{8,9},{9,8},{10,11... | collective-permute-start | bytes 786440 | tf_op jit(solution)/shard_map/ppermute | solution.py:469
  57.2 9.6 %collective-permute-start.14 = (bf16[4,48,512]{2,1,0:T(8,128)(2,1)S(1)}, bf16[4,48,512]{2,1,0:T(8,128)(2,1)S(1)}, u32[]{:S(2)}, u32[]{:S(2)}) collective-permute-start(bf16[4,48,512]{2,1,0:T(8,128)(2,1)S(1)} %get-tuple-element.190), channel_id=1, source_target_pairs={{0,4},{2,6},{4,0},{6,2},{8,12},{10,14},{12,8},{14,10},{16,20},{18,... | collective-permute-start | bytes 589832 | tf_op jit(solution)/shard_map/ppermute | solution.py:469
  58.7 8.1 %collective-permute-start.15 = (bf16[1,128,512]{2,1,0:T(8,128)(2,1)S(1)}, bf16[1,128,512]{2,1,0:T(8,128)(2,1)S(1)}, u32[]{:S(2)}, u32[]{:S(2)}) collective-permute-start(bf16[1,128,512]{2,1,0:T(8,128)(2,1)S(1)} %get-tuple-element.192), channel_id=1, source_target_pairs={{0,16},{2,18},{4,20},{6,22},{8,24},{10,26},{12,28},{14,30},{16,0},... | collective-permute-start | bytes 393224 | tf_op jit(solution)/shard_map/ppermute | solution.py:469
  61.2 4.6 %collective-permute-start.16 = (bf16[1,96,512]{2,1,0:T(8,128)(2,1)S(1)}, bf16[1,96,512]{2,1,0:T(8,128)(2,1)S(1)}, u32[]{:S(2)}, u32[]{:S(2)}) collective-permute-start(bf16[1,96,512]{2,1,0:T(8,128)(2,1)S(1)} %get-tuple-element.194), channel_id=1, source_target_pairs={{0,4},{2,6},{4,0},{6,2},{8,12},{10,14},{12,8},{14,10},{16,20},{18,... | collective-permute-start | bytes 294920 | tf_op jit(solution)/shard_map/ppermute | solution.py:469
  67.0 6.1 %collective-permute-start.17 = (bf16[2,112,512]{2,1,0:T(8,128)(2,1)S(1)}, bf16[2,112,512]{2,1,0:T(8,128)(2,1)S(1)}, u32[]{:S(2)}, u32[]{:S(2)}) collective-permute-start(bf16[2,112,512]{2,1,0:T(8,128)(2,1)S(1)} %get-tuple-element.196), channel_id=1, source_target_pairs={{0,8},{2,10},{4,12},{6,14},{8,0},{10,2},{12,4},{14,6},{16,24},{18,... | collective-permute-start | bytes 688136 | tf_op jit(solution)/shard_map/ppermute | solution.py:469
  67.8 7.3 %collective-permute-start.19 = (bf16[224,512]{1,0:T(8,128)(2,1)S(1)}, bf16[224,512]{1,0:T(8,128)(2,1)S(1)}, u32[]{:S(2)}, u32[]{:S(2)}) collective-permute-start(bf16[224,512]{1,0:T(8,128)(2,1)S(1)} %bitcast.15), channel_id=1, source_target_pairs={{0,1},{1,0},{2,3},{3,2},{4,5},{5,4},{6,7},{7,6},{8,9},{9,8},{10,11... | collective-permute-start | bytes 688136 | tf_op jit(solution)/shard_map/ppermute | solution.py:469
  73.1 7.0 %collective-permute-start.18 = (bf16[1,112,512]{2,1,0:T(8,128)(2,1)S(1)}, bf16[1,112,512]{2,1,0:T(8,128)(2,1)S(1)}, u32[]{:S(2)}, u32[]{:S(2)}) collective-permute-start(bf16[1,112,512]{2,1,0:T(8,128)(2,1)S(1)} %get-tuple-element.199), channel_id=1, source_target_pairs={{0,16},{2,18},{4,20},{6,22},{8,24},{10,26},{12,28},{14,30},{16,0},... | collective-permute-start | bytes 344072 | tf_op jit(solution)/shard_map/ppermute | solution.py:469
  80.1 4.9 %collective-permute-start.20 = (bf16[112,512]{1,0:T(8,128)(2,1)S(1)}, bf16[112,512]{1,0:T(8,128)(2,1)S(1)}, u32[]{:S(2)}, u32[]{:S(2)}) collective-permute-start(bf16[112,512]{1,0:T(8,128)(2,1)S(1)} %bitcast.13), channel_id=1, source_target_pairs={{0,1},{1,0},{2,3},{3,2},{4,5},{5,4},{6,7},{7,6},{8,9},{9,8},{10,11... | collective-permute-start | bytes 344072 | tf_op jit(solution)/shard_map/ppermute | solution.py:469

commit v6 on v5

--- a/solution.py
+++ b/solution.py
@@ -131,7 +131,7 @@
         out_shape=tuple((pltpu.HBM if r else VMEM)(s.shape, s.dtype) for s, r in zip(shapes, is_far)),
         scratch_shapes=buffers + sems + list(scratch),
         compiler_params=pltpu.CompilerParams(vmem_limit_bytes=limit),
-        cost_estimate=pl.CostEstimate(flops=0, bytes_accessed=0, transcendentals=0),
+        cost_estimate=pl.CostEstimate(flops=100000000, bytes_accessed=0, transcendentals=0),
     )(*smem, *arrays, *[p.array for p in fetch], *after)
 
 
@@ -583,6 +583,7 @@
         both = (a + other1_ref[row1 : row1 + end, :].astype(F32)) * factor
         first[1] = both[:cut]
         second[1] = both[cut:end]
+        flush(first, second)
         row0 += rows
         row1 += end
 

time: 86.8 us -> 86.8 us (level)
  no operation moved by 1% of the time
where the time goes in v6:
time: 86.8 us; the launch traced here: 86.5 us
  waiting for transfers between devices  29.9 us (34%)
  Pallas kernels  28.1 us (32%)
  starting transfers between devices  27.6 us (32%)
    pallas_call x20, Pallas kernels, call(): pl.pallas_call(run, in_specs=[pl.BlockSpec(memory_space=pltpu.SMEM)] * le...  28.1 us
    ppermute x18, waiting for transfers between devices, flip(): lax.ppermute(values, axis, [(i, i ^ bit) for i in range(lax.axis_size(axi...  26.3 us
    ppermute x18, starting transfers between devices, flip(): lax.ppermute(values, axis, [(i, i ^ bit) for i in range(lax.axis_size(axi...  21.8 us
    ppermute x3, starting transfers between devices, trade(): return lax.ppermute(rows, 'mesh', [(0, 1), (1, 0)])  5.77 us
    ppermute x3, waiting for transfers between devices, trade(): return lax.ppermute(rows, 'mesh', [(0, 1), (1, 0)])  3.55 us
  transfers between devices with their start and end apart: 21, of which 12 were waited for; matrix products, arithmetic and copies ran while one was open for 0% of the time, Pallas kernels for 17%

profile of v6, /device:TPU:0, one launch (start us, length us, event | category | flops | bytes accessed | tf_op | source)
XLA Modules:
  0.0 86.5 jit_solution(8186818223452226841)
XLA Ops:
  1.7 3.0 %collective-permute-start = (bf16[32,512]{1,0:T(8,128)(2,1)S(1)}, bf16[32,512]{1,0:T(8,128)(2,1)S(1)}, u32[]{:S(2)}, u32[]{:S(2)}) collective-permute-start(bf16[32,512]{1,0:T(8,128)(2,1)S(1)} %shard_map.164), channel_id=1, source_target_pairs={{0,1},{1,0},{2,3},{3,2},{4,5},{5,4},{6,7},{7,6},{8,9},{9,8},{10,11... | collective-permute-start | bytes 98312 | tf_op jit(solution)/shard_map/ppermute | solution.py:458
  4.7 2.5 %shard_map.163 = (bf16[512,160]{1,0:T(8,128)(2,1)S(1)}, bf16[512,64]{1,0:T(8,128)(2,1)S(1)}, f32[512,1]{1,0:T(8,128)S(1)}, f32[64,1]{1,0:T(8,128)S(1)}, f32[512,...) custom-call(s32[8,64]{1,0:T(8,128)} %bitcast.27, ...), custom_call_target="tpu_custom_call" | custom-call | flops 100000000 | tf_op jit(solution)/shard_map/pallas_call | solution.py:124
  7.3 3.6 %shard_map.165 = (bf16[512,512]{1,0:T(8,128)(2,1)S(1)}, bf16[512,512]{1,0:T(8,128)(2,1)S(1)}, bf16[512,512]{1,0:T(8,128)(2,1)S(1)}, f32[512,1]{1,0:T(8,128)S(1)}...) custom-call(f32[512,512]{1,0:T(8,128)S(1)} %get-tuple-element.106.re, ...), custom_call_target="tpu_custom_call" | custom-call | flops 100000000 | tf_op jit(solution)/shard_map/pallas_call | solution.py:124
  12.3 1.7 %shard_map.166 = (f32[512,512]{1,0:T(8,128)S(1)}, bf16[512,512]{1,0:T(8,128)(2,1)S(1)}, bf16[1024,512]{1,0:T(8,128)(2,1)S(1)}, bf16[512,512]{1,0:T(8,128)(2,1)S(...) custom-call(bf16[64,512]{1,0:T(8,128)(2,1)S(1)} %get-tuple-element.117.refs_0_.refs_2_.refs_1_, ...), custom_call_target="tpu_custom_call" | custom-call | flops 100000000 | tf_op jit(solution)/shard_map/pallas_call | solution.py:124
  14.8 4.9 %shard_map.167 = (bf16[512,512]{1,0:T(8,128)(2,1)S(1)}, bf16[64,512]{1,0:T(8,128)(2,1)S(1)}, bf16[64,512]{1,0:T(8,128)(2,1)S(1)}, bf16[64,512]{1,0:T(8,128)(2,1)...) custom-call(f32[512,512]{1,0:T(8,128)S(1)} %get-tuple-element.121.re, ...), custom_call_target="tpu_custom_call" | custom-call | flops 100000000 | tf_op jit(solution)/shard_map/pallas_call | solution.py:124
  19.8 1.8 %shard_map.171 = (bf16[8,128,512]{2,1,0:T(8,128)(2,1)S(1)}, bf16[8,128,512]{2,1,0:T(8,128)(2,1)S(1)}) custom-call(s32[2]{0:T(128)S(1)} %pad_add_fusion.refs_0_, bf16[512,512]{1,0:T(8,128)(2,1)S(1)} %get-tuple-element.118.refs_2_.refs_1_, bf16[64,512]{1,0:T(8,128)(2,1)S(1)} %get-tuple-element.117.refs_0_.refs_2_.refs_1_, ...), custom_call_target="tpu_custom_call" | custom-call | flops 100000000 | tf_op jit(solution)/shard_map/pallas_call | solution.py:124
  24.6 1.6 %collective-permute-start.6 = (bf16[4,128,512]{2,1,0:T(8,128)(2,1)S(1)}, bf16[4,128,512]{2,1,0:T(8,128)(2,1)S(1)}, u32[]{:S(2)}, u32[]{:S(2)}) collective-permute-start(bf16[4,128,512]{2,1,0:T(8,128)(2,1)S(1)} %get-tuple-element.166), channel_id=1, source_target_pairs={{0,4},{2,6},{4,0},{6,2},{8,12},{10,14},{12,8},{14,10},{16,20},{18,... | collective-permute-start | bytes 1572872 | tf_op jit(solution)/shard_map/ppermute | solution.py:469
  27.7 1.6 %collective-permute-start.4 = (bf16[4,96,512]{2,1,0:T(8,128)(2,1)S(1)}, bf16[4,96,512]{2,1,0:T(8,128)(2,1)S(1)}, u32[]{:S(2)}, u32[]{:S(2)}) collective-permute-start(bf16[4,96,512]{2,1,0:T(8,128)(2,1)S(1)} %get-tuple-element.151.refs_23_), channel_id=1, source_target_pairs={{0,8},{2,10},{4,12},{6,14},{8,0},{10,2},{12,4},{14,6},{16,24},{18,... | collective-permute-start | bytes 1179656 | tf_op jit(solution)/shard_map/ppermute | solution.py:469
  29.3 2.8 %collective-permute-done.2.refs_3_ = bf16[160,512]{1,0:T(8,128)(2,1)S(1)} collective-permute-done((bf16[160,512]{1,0:T(8,128)(2,1)S(1)}, bf16[160,512]{1,0:T(8,128)(2,1)S(1)}, u32[]{:S(2)}, u32[]{:S(2)}) %collective-permute-start.2) | collective-permute-done | bytes 163872 | tf_op jit(solution)/shard_map/ppermute | solution.py:458
  32.1 3.2 %shard_map.170 = (bf16[64,512]{1,0:T(8,128)(2,1)S(1)}, bf16[64,512]{1,0:T(8,128)(2,1)S(1)}, f32[64,512]{1,0:T(8,128)S(1)}, f32[64,512]{1,0:T(8,128)S(1)}, f32[64...) custom-call(f32[64,512]{1,0:T(8,128)S(1)} %get-tuple-element.129.ref, ...), custom_call_target="tpu_custom_call" | custom-call | flops 100000000 | tf_op jit(solution)/shard_map/pallas_call | solution.py:124
  35.3 1.8 %shard_map.174 = (bf16[16,64,512]{2,1,0:T(8,128)(2,1)S(1)}, bf16[16,64,512]{2,1,0:T(8,128)(2,1)S(1)}) custom-call(s32[2]{0:T(128)S(1)} %pad_add_fusion.refs_0_, bf16[512,512]{1,0:T(8,128)(2,1)S(1)} %get-tuple-element.170.refs_1_, bf16[64,512]{1,0:T(8,128)(2,1)S(1)} %get-tuple-element.156.refs_1_.refs_2_, bf16[32,512]{1,0:T(8,128)(2,1)S(1)} %collective-permute-done.refs_3_, ...), custom_call_target="tpu_custom_call" | custom-call | flops 100000000 | tf_op jit(solution)/shard_map/pallas_call | solution.py:124
  40.2 1.6 %collective-permute-start.10 = (bf16[8,64,512]{2,1,0:T(8,128)(2,1)S(1)}, bf16[8,64,512]{2,1,0:T(8,128)(2,1)S(1)}, u32[]{:S(2)}, u32[]{:S(2)}) collective-permute-start(bf16[8,64,512]{2,1,0:T(8,128)(2,1)S(1)} %get-tuple-element.178.refs_5_), channel_id=1, source_target_pairs={{0,4},{2,6},{4,0},{6,2},{8,12},{10,14},{12,8},{14,10},{16,20},{18,... | collective-permute-start | bytes 1572872 | tf_op jit(solution)/shard_map/ppermute | solution.py:469
  43.9 1.6 %collective-permute-start.11 = (bf16[2,128,512]{2,1,0:T(8,128)(2,1)S(1)}, bf16[2,128,512]{2,1,0:T(8,128)(2,1)S(1)}, u32[]{:S(2)}, u32[]{:S(2)}) collective-permute-start(bf16[2,128,512]{2,1,0:T(8,128)(2,1)S(1)} %get-tuple-element.182), channel_id=1, source_target_pairs={{0,8},{2,10},{4,12},{6,14},{8,0},{10,2},{12,4},{14,6},{16,24},{18,... | collective-permute-start | bytes 786440 | tf_op jit(solution)/shard_map/ppermute | solution.py:469
  45.5 2.6 %collective-permute-start.12 = (bf16[2,96,512]{2,1,0:T(8,128)(2,1)S(1)}, bf16[2,96,512]{2,1,0:T(8,128)(2,1)S(1)}, u32[]{:S(2)}, u32[]{:S(2)}) collective-permute-start(bf16[2,96,512]{2,1,0:T(8,128)(2,1)S(1)} %get-tuple-element.184), channel_id=1, source_target_pairs={{0,16},{2,18},{4,20},{6,22},{8,24},{10,26},{12,28},{14,30},{16,0},... | collective-permute-start | bytes 589832 | tf_op jit(solution)/shard_map/ppermute | solution.py:469
  48.0 8.1 %collective-permute-done.11.refs_3_ = bf16[2,128,512]{2,1,0:T(8,128)(2,1)S(1)} collective-permute-done((bf16[2,128,512]{2,1,0:T(8,128)(2,1)S(1)}, bf16[2,128,512]{2,1,0:T(8,128)(2,1)S(1)}, u32[]{:S(2)}, u32[]{:S(2)}) %collective-permute-start.11) | collective-permute-done | bytes 262176 | tf_op jit(solution)/shard_map/ppermute | solution.py:469
  57.2 1.5 %collective-permute-start.14 = (bf16[4,48,512]{2,1,0:T(8,128)(2,1)S(1)}, bf16[4,48,512]{2,1,0:T(8,128)(2,1)S(1)}, u32[]{:S(2)}, u32[]{:S(2)}) collective-permute-start(bf16[4,48,512]{2,1,0:T(8,128)(2,1)S(1)} %get-tuple-element.190), channel_id=1, source_target_pairs={{0,4},{2,6},{4,0},{6,2},{8,12},{10,14},{12,8},{14,10},{16,20},{18,... | collective-permute-start | bytes 589832 | tf_op jit(solution)/shard_map/ppermute | solution.py:469
  58.6 2.5 %collective-permute-start.15 = (bf16[1,128,512]{2,1,0:T(8,128)(2,1)S(1)}, bf16[1,128,512]{2,1,0:T(8,128)(2,1)S(1)}, u32[]{:S(2)}, u32[]{:S(2)}) collective-permute-start(bf16[1,128,512]{2,1,0:T(8,128)(2,1)S(1)} %get-tuple-element.192), channel_id=1, source_target_pairs={{0,16},{2,18},{4,20},{6,22},{8,24},{10,26},{12,28},{14,30},{16,0},... | collective-permute-start | bytes 393224 | tf_op jit(solution)/shard_map/ppermute | solution.py:469
  61.6 2.0 %shard_map.178.refs_8_ = f32[64,512]{1,0:T(8,128)} custom-call(f32[64,512]{1,0:T(8,128)S(1)} %get-tuple-element.152.refs_0_, f32[64,512]{1,0:T(8,128)S(1)} %get-tuple-element.153.refs_1_, f32[64,512]{1,0:T(8,128)S(1)} %get-tuple-element.154.refs_2_, bf16[9,48,512]{2,1,0:T(8,128)(2,1)S(1)} %collective-permute-done.9.refs_7_.refs_3_, s32[1,32]{1,0:T(1,128)S(1)} %copy-done, ...), custom_call_target="tpu_custom_call" | custom-call | flops 100000000 | tf_op jit(solution)/shard_map/pallas_call | solution.py:124
  63.7 2.0 %collective-permute-done.16.refs_7_ = bf16[1,96,512]{2,1,0:T(8,128)(2,1)S(1)} collective-permute-done((bf16[1,96,512]{2,1,0:T(8,128)(2,1)S(1)}, bf16[1,96,512]{2,1,0:T(8,128)(2,1)S(1)}, u32[]{:S(2)}, u32[]{:S(2)}) %collective-permute-start.16) | collective-permute-done | bytes 98336 | tf_op jit(solution)/shard_map/ppermute | solution.py:469
  69.1 4.0 %collective-permute-done.17.refs_1_.refs_3_ = bf16[2,112,512]{2,1,0:T(8,128)(2,1)S(1)} collective-permute-done((bf16[2,112,512]{2,1,0:T(8,128)(2,1)S(1)}, bf16[2,112,512]{2,1,0:T(8,128)(2,1)S(1)}, u32[]{:S(2)}, u32[]{:S(2)}) %collective-permute-start.17) | collective-permute-done | bytes 229408 | tf_op jit(solution)/shard_map/ppermute | solution.py:469
  73.1 1.9 %collective-permute-start.18 = (bf16[1,112,512]{2,1,0:T(8,128)(2,1)S(1)}, bf16[1,112,512]{2,1,0:T(8,128)(2,1)S(1)}, u32[]{:S(2)}, u32[]{:S(2)}) collective-permute-start(bf16[1,112,512]{2,1,0:T(8,128)(2,1)S(1)} %get-tuple-element.199), channel_id=1, source_target_pairs={{0,16},{2,18},{4,20},{6,22},{8,24},{10,26},{12,28},{14,30},{16,0},... | collective-permute-start | bytes 344072 | tf_op jit(solution)/shard_map/ppermute | solution.py:469
  75.0 5.0 %collective-permute-done.18.refs_1_.refs_3_ = bf16[1,112,512]{2,1,0:T(8,128)(2,1)S(1)} collective-permute-done((bf16[1,112,512]{2,1,0:T(8,128)(2,1)S(1)}, bf16[1,112,512]{2,1,0:T(8,128)(2,1)S(1)}, u32[]{:S(2)}, u32[]{:S(2)}) %collective-permute-start.18) | collective-permute-done | bytes 114720 | tf_op jit(solution)/shard_map/ppermute | solution.py:469
  81.5 3.5 %collective-permute-done.20.refs_2_ = bf16[112,512]{1,0:T(8,128)(2,1)S(1)} collective-permute-done((bf16[112,512]{1,0:T(8,128)(2,1)S(1)}, bf16[112,512]{1,0:T(8,128)(2,1)S(1)}, u32[]{:S(2)}, u32[]{:S(2)}) %collective-permute-start.20) | collective-permute-done | bytes 114720 | tf_op jit(solution)/shard_map/ppermute | solution.py:469
  85.0 1.5 %shard_map.182 = (f32[2,96,512]{2,1,0:T(8,128)}, f32[2,32,512]{2,1,0:T(8,128)}, f32[2,64,512]{2,1,0:T(8,128)}, f32[2,32,512]{2,1,0:T(8,128)}) custom-call(s32[2]{0:T(128)S(1)} %pad_add_fusion.refs_0_, bf16[112,512]{1,0:T(8,128)(2,1)S(1)} %bitcast.14, bf16[112,512]{1,0:T(8,128)(2,1)S(1)} %collective-permute-done.20.refs_2_, bf16[224,512]{1,0:T(8,128)(2,1)S(1)} %bitcast.16, ...), custom_call_target="tpu_custom_call" | custom-call | flops 100000000 | tf_op jit(solution)/shard_map/pallas_call | solution.py:124
  (41 shorter events, 19.2 us)
Async XLA Ops:
  1.7 5.6 %collective-permute-start = (bf16[32,512]{1,0:T(8,128)(2,1)S(1)}, bf16[32,512]{1,0:T(8,128)(2,1)S(1)}, u32[]{:S(2)}, u32[]{:S(2)}) collective-permute-start(bf16[32,512]{1,0:T(8,128)(2,1)S(1)} %shard_map.164), channel_id=1, source_target_pairs={{0,1},{1,0},{2,3},{3,2},{4,5},{5,4},{6,7},{7,6},{8,9},{9,8},{10,11... | collective-permute-start | bytes 98312 | tf_op jit(solution)/shard_map/ppermute | solution.py:458
  4.7 2.6 %copy-start = (s32[1,32]{1,0:T(1,128)S(1)}, s32[1,32]{1,0:T(1,128)}, u32[]{:S(2)}) copy-start(s32[1,32]{1,0:T(1,128)} %refs_4_.3) | copy-start | bytes 388
  10.9 4.0 %collective-permute-start.1 = (bf16[32,512]{1,0:T(8,128)(2,1)S(1)}, bf16[32,512]{1,0:T(8,128)(2,1)S(1)}, u32[]{:S(2)}, u32[]{:S(2)}) collective-permute-start(bf16[32,512]{1,0:T(8,128)(2,1)S(1)} %get-tuple-element.122), channel_id=1, source_target_pairs={{0,1},{1,0},{2,3},{3,2},{4,5},{5,4},{6,7},{7,6},{8,9},{9,8},{10,11... | collective-permute-start | bytes 98312 | tf_op jit(solution)/shard_map/ppermute | solution.py:458
  21.6 2.7 %collective-permute-start.5 = (bf16[8,128,512]{2,1,0:T(8,128)(2,1)S(1)}, bf16[8,128,512]{2,1,0:T(8,128)(2,1)S(1)}, u32[]{:S(2)}, u32[]{:S(2)}) collective-permute-start(bf16[8,128,512]{2,1,0:T(8,128)(2,1)S(1)} %get-tuple-element.165), channel_id=1, source_target_pairs={{0,2},{2,0},{4,6},{6,4},{8,10},{10,8},{12,14},{14,12},{16,18},{18,... | collective-permute-start | bytes 3145736 | tf_op jit(solution)/shard_map/ppermute | solution.py:469
  22.9 4.6 %collective-permute-start.3 = (bf16[8,96,512]{2,1,0:T(8,128)(2,1)S(1)}, bf16[8,96,512]{2,1,0:T(8,128)(2,1)S(1)}, u32[]{:S(2)}, u32[]{:S(2)}) collective-permute-start(bf16[8,96,512]{2,1,0:T(8,128)(2,1)S(1)} %get-tuple-element.150), channel_id=1, source_target_pairs={{0,2},{2,0},{4,6},{6,4},{8,10},{10,8},{12,14},{14,12},{16,18},{18,... | collective-permute-start | bytes 2359304 | tf_op jit(solution)/shard_map/ppermute | solution.py:469
  24.6 14.0 %collective-permute-start.6 = (bf16[4,128,512]{2,1,0:T(8,128)(2,1)S(1)}, bf16[4,128,512]{2,1,0:T(8,128)(2,1)S(1)}, u32[]{:S(2)}, u32[]{:S(2)}) collective-permute-start(bf16[4,128,512]{2,1,0:T(8,128)(2,1)S(1)} %get-tuple-element.166), channel_id=1, source_target_pairs={{0,4},{2,6},{4,0},{6,2},{8,12},{10,14},{12,8},{14,10},{16,20},{18,... | collective-permute-start | bytes 1572872 | tf_op jit(solution)/shard_map/ppermute | solution.py:469
  26.1 6.0 %collective-permute-start.2 = (bf16[160,512]{1,0:T(8,128)(2,1)S(1)}, bf16[160,512]{1,0:T(8,128)(2,1)S(1)}, u32[]{:S(2)}, u32[]{:S(2)}) collective-permute-start(bf16[160,512]{1,0:T(8,128)(2,1)S(1)} %get-tuple-element.132.refs_7_), channel_id=1, source_target_pairs={{0,1},{1,0},{2,3},{3,2},{4,5},{5,4},{6,7},{7,6},{8,9},{9,8},{10,11... | collective-permute-start | bytes 491528 | tf_op jit(solution)/shard_map/ppermute | solution.py:458
  27.7 10.7 %collective-permute-start.4 = (bf16[4,96,512]{2,1,0:T(8,128)(2,1)S(1)}, bf16[4,96,512]{2,1,0:T(8,128)(2,1)S(1)}, u32[]{:S(2)}, u32[]{:S(2)}) collective-permute-start(bf16[4,96,512]{2,1,0:T(8,128)(2,1)S(1)} %get-tuple-element.151.refs_23_), channel_id=1, source_target_pairs={{0,8},{2,10},{4,12},{6,14},{8,0},{10,2},{12,4},{14,6},{16,24},{18,... | collective-permute-start | bytes 1179656 | tf_op jit(solution)/shard_map/ppermute | solution.py:469
  37.1 2.8 %collective-permute-start.8 = (bf16[16,64,512]{2,1,0:T(8,128)(2,1)S(1)}, bf16[16,64,512]{2,1,0:T(8,128)(2,1)S(1)}, u32[]{:S(2)}, u32[]{:S(2)}) collective-permute-start(bf16[16,64,512]{2,1,0:T(8,128)(2,1)S(1)} %get-tuple-element.176), channel_id=1, source_target_pairs={{0,2},{2,0},{4,6},{6,4},{8,10},{10,8},{12,14},{14,12},{16,18},{18,... | collective-permute-start | bytes 3145736 | tf_op jit(solution)/shard_map/ppermute | solution.py:469
  39.8 2.4 %collective-permute-start.7 = (bf16[16,48,512]{2,1,0:T(8,128)(2,1)S(1)}, bf16[16,48,512]{2,1,0:T(8,128)(2,1)S(1)}, u32[]{:S(2)}, u32[]{:S(2)}) collective-permute-start(bf16[16,48,512]{2,1,0:T(8,128)(2,1)S(1)} %get-tuple-element.168), channel_id=1, source_target_pairs={{0,2},{2,0},{4,6},{6,4},{8,10},{10,8},{12,14},{14,12},{16,18},{18,... | collective-permute-start | bytes 2359304 | tf_op jit(solution)/shard_map/ppermute | solution.py:469
  40.2 15.9 %collective-permute-start.10 = (bf16[8,64,512]{2,1,0:T(8,128)(2,1)S(1)}, bf16[8,64,512]{2,1,0:T(8,128)(2,1)S(1)}, u32[]{:S(2)}, u32[]{:S(2)}) collective-permute-start(bf16[8,64,512]{2,1,0:T(8,128)(2,1)S(1)} %get-tuple-element.178.refs_5_), channel_id=1, source_target_pairs={{0,4},{2,6},{4,0},{6,2},{8,12},{10,14},{12,8},{14,10},{16,20},{18,... | collective-permute-start | bytes 1572872 | tf_op jit(solution)/shard_map/ppermute | solution.py:469
  42.5 13.7 %collective-permute-start.9 = (bf16[9,48,512]{2,1,0:T(8,128)(2,1)S(1)}, bf16[9,48,512]{2,1,0:T(8,128)(2,1)S(1)}, u32[]{:S(2)}, u32[]{:S(2)}) collective-permute-start(bf16[9,48,512]{2,1,0:T(8,128)(2,1)S(1)} %get-tuple-element.179), channel_id=1, source_target_pairs={{0,1},{1,0},{2,3},{3,2},{4,5},{5,4},{6,7},{7,6},{8,9},{9,8},{10,11... | collective-permute-start | bytes 1327112 | tf_op jit(solution)/shard_map/ppermute | solution.py:469
  43.9 12.3 %collective-permute-start.11 = (bf16[2,128,512]{2,1,0:T(8,128)(2,1)S(1)}, bf16[2,128,512]{2,1,0:T(8,128)(2,1)S(1)}, u32[]{:S(2)}, u32[]{:S(2)}) collective-permute-start(bf16[2,128,512]{2,1,0:T(8,128)(2,1)S(1)} %get-tuple-element.182), channel_id=1, source_target_pairs={{0,8},{2,10},{4,12},{6,14},{8,0},{10,2},{12,4},{14,6},{16,24},{18,... | collective-permute-start | bytes 786440 | tf_op jit(solution)/shard_map/ppermute | solution.py:469
  45.5 10.7 %collective-permute-start.12 = (bf16[2,96,512]{2,1,0:T(8,128)(2,1)S(1)}, bf16[2,96,512]{2,1,0:T(8,128)(2,1)S(1)}, u32[]{:S(2)}, u32[]{:S(2)}) collective-permute-start(bf16[2,96,512]{2,1,0:T(8,128)(2,1)S(1)} %get-tuple-element.184), channel_id=1, source_target_pairs={{0,16},{2,18},{4,20},{6,22},{8,24},{10,26},{12,28},{14,30},{16,0},... | collective-permute-start | bytes 589832 | tf_op jit(solution)/shard_map/ppermute | solution.py:469
  56.4 10.4 %collective-permute-start.13 = (bf16[4,64,512]{2,1,0:T(8,128)(2,1)S(1)}, bf16[4,64,512]{2,1,0:T(8,128)(2,1)S(1)}, u32[]{:S(2)}, u32[]{:S(2)}) collective-permute-start(bf16[4,64,512]{2,1,0:T(8,128)(2,1)S(1)} %get-tuple-element.186.refs_6_), channel_id=1, source_target_pairs={{0,1},{1,0},{2,3},{3,2},{4,5},{5,4},{6,7},{7,6},{8,9},{9,8},{10,11... | collective-permute-start | bytes 786440 | tf_op jit(solution)/shard_map/ppermute | solution.py:469
  57.2 9.6 %collective-permute-start.14 = (bf16[4,48,512]{2,1,0:T(8,128)(2,1)S(1)}, bf16[4,48,512]{2,1,0:T(8,128)(2,1)S(1)}, u32[]{:S(2)}, u32[]{:S(2)}) collective-permute-start(bf16[4,48,512]{2,1,0:T(8,128)(2,1)S(1)} %get-tuple-element.190), channel_id=1, source_target_pairs={{0,4},{2,6},{4,0},{6,2},{8,12},{10,14},{12,8},{14,10},{16,20},{18,... | collective-permute-start | bytes 589832 | tf_op jit(solution)/shard_map/ppermute | solution.py:469
  58.6 8.1 %collective-permute-start.15 = (bf16[1,128,512]{2,1,0:T(8,128)(2,1)S(1)}, bf16[1,128,512]{2,1,0:T(8,128)(2,1)S(1)}, u32[]{:S(2)}, u32[]{:S(2)}) collective-permute-start(bf16[1,128,512]{2,1,0:T(8,128)(2,1)S(1)} %get-tuple-element.192), channel_id=1, source_target_pairs={{0,16},{2,18},{4,20},{6,22},{8,24},{10,26},{12,28},{14,30},{16,0},... | collective-permute-start | bytes 393224 | tf_op jit(solution)/shard_map/ppermute | solution.py:469
  61.1 4.6 %collective-permute-start.16 = (bf16[1,96,512]{2,1,0:T(8,128)(2,1)S(1)}, bf16[1,96,512]{2,1,0:T(8,128)(2,1)S(1)}, u32[]{:S(2)}, u32[]{:S(2)}) collective-permute-start(bf16[1,96,512]{2,1,0:T(8,128)(2,1)S(1)} %get-tuple-element.194), channel_id=1, source_target_pairs={{0,4},{2,6},{4,0},{6,2},{8,12},{10,14},{12,8},{14,10},{16,20},{18,... | collective-permute-start | bytes 294920 | tf_op jit(solution)/shard_map/ppermute | solution.py:469
  66.9 6.1 %collective-permute-start.17 = (bf16[2,112,512]{2,1,0:T(8,128)(2,1)S(1)}, bf16[2,112,512]{2,1,0:T(8,128)(2,1)S(1)}, u32[]{:S(2)}, u32[]{:S(2)}) collective-permute-start(bf16[2,112,512]{2,1,0:T(8,128)(2,1)S(1)} %get-tuple-element.196), channel_id=1, source_target_pairs={{0,8},{2,10},{4,12},{6,14},{8,0},{10,2},{12,4},{14,6},{16,24},{18,... | collective-permute-start | bytes 688136 | tf_op jit(solution)/shard_map/ppermute | solution.py:469
  67.7 7.3 %collective-permute-start.19 = (bf16[224,512]{1,0:T(8,128)(2,1)S(1)}, bf16[224,512]{1,0:T(8,128)(2,1)S(1)}, u32[]{:S(2)}, u32[]{:S(2)}) collective-permute-start(bf16[224,512]{1,0:T(8,128)(2,1)S(1)} %bitcast.15), channel_id=1, source_target_pairs={{0,1},{1,0},{2,3},{3,2},{4,5},{5,4},{6,7},{7,6},{8,9},{9,8},{10,11... | collective-permute-start | bytes 688136 | tf_op jit(solution)/shard_map/ppermute | solution.py:469
  73.1 7.0 %collective-permute-start.18 = (bf16[1,112,512]{2,1,0:T(8,128)(2,1)S(1)}, bf16[1,112,512]{2,1,0:T(8,128)(2,1)S(1)}, u32[]{:S(2)}, u32[]{:S(2)}) collective-permute-start(bf16[1,112,512]{2,1,0:T(8,128)(2,1)S(1)} %get-tuple-element.199), channel_id=1, source_target_pairs={{0,16},{2,18},{4,20},{6,22},{8,24},{10,26},{12,28},{14,30},{16,0},... | collective-permute-start | bytes 344072 | tf_op jit(solution)/shard_map/ppermute | solution.py:469
  80.1 4.9 %collective-permute-start.20 = (bf16[112,512]{1,0:T(8,128)(2,1)S(1)}, bf16[112,512]{1,0:T(8,128)(2,1)S(1)}, u32[]{:S(2)}, u32[]{:S(2)}) collective-permute-start(bf16[112,512]{1,0:T(8,128)(2,1)S(1)} %bitcast.13), channel_id=1, source_target_pairs={{0,1},{1,0},{2,3},{3,2},{4,5},{5,4},{6,7},{7,6},{8,9},{9,8},{10,11... | collective-permute-start | bytes 344072 | tf_op jit(solution)/shard_map/ppermute | solution.py:469
